TPU v7x, 256 devices: a whole 4x4x8 slice. The times are simulated.
256 devices in a mesh: dp: 64 (over z, y, core), rep: 4 (over x).
Axes of the slice: x: 4, y: 4, z: 8, core: 2. Of those that a mesh axis runs over, the one named last changes fastest.
Arguments:
- waveform: bfloat16 [4, 3072, 320], P('rep', 'dp'), may hold values from -6 to 6
- lengths: int32 [4, 3072], P('rep', 'dp'), may hold values from 214 to 320
- target: int32 [4, 3072], P('rep', 'dp'), may hold values from 0 to 3071, as said below
- conv0_weight: bfloat16 [10, 512], replicated, may hold values from -2 to 2
- norm_gain: float32 [512], replicated, may hold values from 0.5 to 1.5
- norm_bias: float32 [512], replicated, may hold values from -0.5 to 0.5
- conv1_weight: bfloat16 [3, 512, 512], replicated, may hold values from -0.15625 to 0.15625
- feature_grad: bfloat16 [4, 3072, 31, 512], P('rep', 'dp'), may hold values from -6 to 6
Outputs:
- features: bfloat16 [4, 3072, 31, 512], P('rep', 'dp')
- grad_conv0: float32 [10, 512], replicated
- grad_gain: float32 [512], replicated
- grad_bias: float32 [512], replicated
- grad_conv1: float32 [3, 512, 512], replicated
Inputs may be any that keep to these rules, and one draw needn't show every extreme that they name: In each group target is a permutation of the 3072 slots; the spans of one device go to slots of devices along dp such that every pair of devices exchanges either 0 or exactly 2 spans.
All inputs are finite; a program needn't handle non-finite values.
Results may differ from a plain program's by a relative error of at most 0.0064.
Values may be sent and summed in bfloat16 or wider, within the bound.
No kernel may reach another device: no remote copies, remote signals or barrier semaphores. Data moves between devices by JAX's collectives and lax.ppermute only.
A program may use at most 128 MiB of HBM per device.

v0:
```python
import jax
import jax.numpy as jnp
from jax import lax
from jax.sharding import PartitionSpec as P


def product(form, left, right):
    return jnp.einsum(form, left, right, preferred_element_type=jnp.float32)


def gelu_and_slope(values):
    cumul = 0.5 * (1.0 + lax.erf(values * 0.7071067811865476))
    density = jnp.exp(-0.5 * values * values) * 0.3989422804014327
    return (values * cumul, cumul + values * density)


def encode(
    panels, panel_len, conv0_weight, norm_gain, norm_bias, conv1_weight, feature_grad, scale
):
    panel_num, sample_num = panels.shape
    chans = conv0_weight.shape[1]
    frames_zero = (sample_num - 10) // 5 + 1
    frames_one = (frames_zero - 3) // 2 + 1
    pieces = panels.reshape(panel_num, frames_zero + 1, 5)
    patches = jnp.concatenate([pieces[:, :-1], pieces[:, 1:]], axis=2)
    first_pre = product("ptk,kc->ptc", patches, conv0_weight)
    valid_zero = (panel_len - 10) // 5 + 1
    mask_zero = (jnp.arange(frames_zero)[None, :] < valid_zero[:, None]).astype(jnp.float32)[
        :, :, None
    ]
    inverse = (1.0 / valid_zero.astype(jnp.float32))[:, None, None]
    center = jnp.sum(first_pre * mask_zero, axis=1, keepdims=True) * inverse
    centred = (first_pre - center) * mask_zero
    variance = jnp.sum(centred * centred, axis=1, keepdims=True) * inverse
    inv_std = lax.rsqrt(variance + 1e-05)
    normed = centred * inv_std
    act_zero, slope_zero = gelu_and_slope(normed * norm_gain + norm_bias)
    hidden = (act_zero * mask_zero).astype(jnp.bfloat16)
    taps = [hidden[:, k : k + 2 * frames_one - 1 : 2] for k in range(3)]
    second_pre = product("ptc,cd->ptd", taps[0], conv1_weight[0])
    second_pre = second_pre + product("ptc,cd->ptd", taps[1], conv1_weight[1])
    second_pre = second_pre + product("ptc,cd->ptd", taps[2], conv1_weight[2])
    valid_one = (valid_zero - 3) // 2 + 1
    mask_one = (jnp.arange(frames_one)[None, :] < valid_one[:, None]).astype(jnp.float32)[
        :, :, None
    ]
    act_one, slope_one = gelu_and_slope(second_pre)
    features = (act_one * mask_one).astype(jnp.bfloat16)
    grad_one = (feature_grad.astype(jnp.float32) * scale * mask_one * slope_one).astype(
        jnp.bfloat16
    )
    weight_one = jnp.stack([product("ptc,ptd->cd", taps[k], grad_one) for k in range(3)])
    backs = [product("ptd,cd->ptc", grad_one, conv1_weight[k]) for k in range(3)]
    even_part = jnp.pad(backs[0], ((0, 0), (0, 1), (0, 0))) + jnp.pad(
        backs[2], ((0, 0), (1, 0), (0, 0))
    )
    odd_part = jnp.pad(backs[1], ((0, 0), (0, 1), (0, 0)))
    dhidden = jnp.stack([even_part, odd_part], axis=2).reshape(
        panel_num, 2 * frames_one + 2, chans
    )[:, :frames_zero]
    dpre = dhidden * mask_zero * slope_zero
    grad_b = jnp.sum(dpre, axis=(0, 1))
    grad_g = jnp.sum(dpre * normed, axis=(0, 1))
    dnorm = dpre * norm_gain
    mean_d = jnp.sum(dnorm, axis=1, keepdims=True) * inverse
    mean_dn = jnp.sum(dnorm * normed, axis=1, keepdims=True) * inverse
    dinput = (inv_std * (dnorm - mean_d - normed * mean_dn) * mask_zero).astype(jnp.bfloat16)
    weight_zero = product("ptk,ptc->kc", patches, dinput)
    rows = jnp.concatenate(
        [weight_zero, grad_g[None], grad_b[None], weight_one.reshape(3 * chans, chans)], axis=0
    )
    return (features, rows)


def body(waveform, lengths, target, conv0_weight, norm_gain, norm_bias, conv1_weight, feature_grad):
    devices = lax.axis_size("dp")
    panel_num = waveform.shape[1]
    sample_num = waveform.shape[2]
    chans = conv0_weight.shape[1]
    capacity = max(2, (panel_num + devices - 1) // devices)
    targets = target[0]
    dest_dev = targets // panel_num
    dest_slot = targets % panel_num
    order_idx = jnp.arange(panel_num)
    before = (dest_dev[:, None] == dest_dev[None, :]) & (order_idx[None, :] < order_idx[:, None])
    ranking = jnp.sum(before.astype(jnp.int32), axis=1)
    bucket = dest_dev * capacity + ranking
    select = jnp.arange(devices * capacity)[:, None] == bucket[None, :]
    send_wave = jnp.dot(
        select.astype(jnp.bfloat16), waveform[0], preferred_element_type=jnp.float32
    )
    send_wave = send_wave.astype(jnp.bfloat16).reshape(devices, capacity, sample_num)
    details = jnp.stack([dest_slot + 1, lengths[0]], axis=1)
    send_meta = jnp.dot(select.astype(jnp.int32), details).reshape(devices, capacity, 2)
    recv_wave, recv_meta = (
        lax.all_to_all(send_wave, "dp", split_axis=0, concat_axis=0, tiled=True),
        lax.all_to_all(send_meta, "dp", split_axis=0, concat_axis=0, tiled=True),
    )
    arrived = recv_wave.reshape(devices * capacity, sample_num)
    arrived_meta = recv_meta.reshape(devices * capacity, 2)
    placing = order_idx[:, None] == (arrived_meta[:, 0] - 1)[None, :]
    panels = jnp.dot(
        placing.astype(jnp.bfloat16), arrived, preferred_element_type=jnp.float32
    ).astype(jnp.bfloat16)
    panel_len = jnp.dot(placing.astype(jnp.int32), arrived_meta[:, 1])
    frames_one = ((sample_num - 10) // 5 + 1 - 3) // 2 + 1
    scale = 1.0 / float(lax.axis_size("rep") * devices * panel_num * frames_one) ** 0.5
    features, rows = encode(
        panels, panel_len, conv0_weight, norm_gain, norm_bias, conv1_weight, feature_grad[0], scale
    )
    total = lax.psum(rows, ("dp", "rep"))
    return (features[None], total[:10], total[10], total[11], total[12:].reshape(3, chans, chans))


def solution(mesh):
    placed = (
        P("rep", "dp", None),
        P("rep", "dp"),
        P("rep", "dp"),
        P(),
        P(),
        P(),
        P(),
        P("rep", "dp", None, None),
    )
    return jax.shard_map(
        body,
        mesh=mesh,
        in_specs=placed,
        out_specs=(P("rep", "dp", None, None), P(), P(), P(), P()),
        check_vma=False,
    )
```

profile of v0, /device:TPU:1, one launch (start us, length us, event | category | flops | bytes accessed | tf_op | source)
XLA Modules:
  0.0 415.9 jit_solution(8603431224123315835)
XLA Ops:
  10.0 0.8 fusion.40
  11.7 13.2 %all-to-all-start = ((s32[64,2,2]{1,2,0:T(2,128)}), s32[64,2,2]{1,2,0:T(2,128)S(1)}, u32[]{:S(2)}, u32[]{:S(2)}) async-start(s32[64,2,2]{1,2,0:T(2,128)} %copy.46), calls=%async_computation | async-start | bytes 131072 | tf_op jit(solution)/shard_map/all_to_all | solution.py:97
  25.9 9.0 %all-to-all-done = s32[64,2,2]{1,2,0:T(2,128)S(1)} async-done(((s32[64,2,2]{1,2,0:T(2,128)}), s32[64,2,2]{1,2,0:T(2,128)S(1)}, u32[]{:S(2)}, u32[]{:S(2)}) %all-to-all-start) | async-done | bytes 1056 | tf_op jit(solution)/shard_map/all_to_all | solution.py:97
  35.0 4.4 %all-to-all-start.1 = ((bf16[64,2,320]{2,1,0:T(2,128)(2,1)}), bf16[64,2,320]{2,1,0:T(2,128)(2,1)S(1)}, u32[]{:S(2)}, u32[]{:S(2)}) async-start(bf16[64,2,320]{2,1,0:T(2,128)(2,1)} %reshape.207), calls=%async_computation.1 | async-start | bytes 196608 | tf_op jit(solution)/shard_map/all_to_all | solution.py:96
  39.9 10.2 %all-to-all-done.1 = bf16[64,2,320]{2,1,0:T(2,128)(2,1)S(1)} async-done(((bf16[64,2,320]{2,1,0:T(2,128)(2,1)}), bf16[64,2,320]{2,1,0:T(2,128)(2,1)S(1)}, u32[]{:S(2)}, u32[]{:S(2)}) %all-to-all-start.1) | async-done | bytes 81952 | tf_op jit(solution)/shard_map/all_to_all | solution.py:96
  51.0 1.8 multiply_reduce_fusion.3
  52.9 1.4 multiply_reduce_fusion.2
  54.5 1.0 copy-done.2
  55.5 2.9 multiply_convert_fusion.1
  58.3 8.6 %slice.56 = bf16[48,31,512]{2,1,0:T(8,128)(2,1)} slice(bf16[48,63,512]{2,1,0:T(8,128)(2,1)S(1)} %multiply_convert_fusion.1), slice={[0:48:1], [2:63:2], [0:512:1]} | slice | bytes 3047424 | tf_op jit(solution)/shard_map/slice | solution.py:39
  66.9 8.4 %slice.54 = bf16[48,31,512]{2,1,0:T(8,128)(2,1)} slice(bf16[48,63,512]{2,1,0:T(8,128)(2,1)S(1)} %multiply_convert_fusion.1), slice={[0:48:1], [1:62:2], [0:512:1]} | slice | bytes 3047424 | tf_op jit(solution)/shard_map/slice | solution.py:39
  75.3 8.4 %slice.52 = bf16[48,31,512]{2,1,0:T(8,128)(2,1)} slice(bf16[48,63,512]{2,1,0:T(8,128)(2,1)S(1)} %multiply_convert_fusion.1), slice={[0:48:1], [0:61:2], [0:512:1]} | slice | bytes 3047424 | tf_op jit(solution)/shard_map/slice | solution.py:39
  83.7 2.9 fusion.17
  86.6 1.3 fusion.15
  88.5 3.9 fusion.12
  92.4 2.2 convolution_bitcast_fusion.1
  94.6 2.2 convolution_bitcast_fusion
  96.8 2.2 convolution_bitcast_fusion.2
  99.0 1.0 fusion.26
  100.0 1.0 fusion.29
  101.4 1.0 add_bitcast_fusion
  102.4 1.3 pad_maximum_fusion
  103.7 7.5 %copy.55 = f32[48,32,2,512]{3,2,1,0:T(2,128)} copy(f32[48,32,2,512]{3,0,1,2:T(8,128)S(1)} %pad_maximum_fusion) | data formatting | bytes 12582912 | tf_op jit(solution)/shard_map/stack | solution.py:58
  111.2 8.6 %reshape.210 = f32[48,64,512]{2,1,0:T(8,128)} reshape(f32[48,32,2,512]{3,2,1,0:T(2,128)} %copy.55) | data formatting | bytes 12582912 | tf_op jit(solution)/shard_map/reshape | solution.py:58
  119.9 9.5 %multiply_reduce_fusion = (f32[512]{0:T(512)S(1)}, f32[48,512]{1,0:T(8,128)S(1)}, f32[48,512]{1,0:T(8,128)S(1)}, f32[512]{0:T(512)S(1)}, f32[48,63,512]{2,1,0:T(8,128)S(1)}) fusion(f32[48,512]{1,0:T(8,128)S(1)} %add_rsqrt_fusion, f32[48,63]{1,0:T(8,128)S(1)} %fusion.45, f32[48,63,512]{2,1,0:T(8,128)} %copy-done.2, f32[48,512]{1,0:T(8,128)S(1)} %broadcast_multiply_fusion.2, ...), kind=kLoop, calls=%fused_computation.8 | loop fusion | flops 34012160 | bytes 18992960 | tf_op jit(solution)/shard_map/reduce_sum | solution.py:63
  129.5 2.0 pad_maximum_fusion.1
  131.5 2.3 fusion.22
  133.8 10.5 %concatenate.7 = f32[1548,512]{1,0:T(8,128)} concatenate(f32[10,512]{1,0:T(8,128)S(1)} %fusion.22, f32[1,512]{1,0:T(1,128)S(1)} %bitcast.95, f32[1,512]{1,0:T(1,128)S(1)} %bitcast.96, f32[1536,512]{1,0:T(8,128)} %bitcast.93), dimensions={0} | concatenate | bytes 6340608 | tf_op jit(solution)/shard_map/concatenate | solution.py:69
  144.3 258.0 %all-reduce.5.cloned.1.call-done = f32[1548,512]{1,0:T(8,128)} async-done(((f32[1548,512]{1,0:T(8,128)}), f32[1548,512]{1,0:T(8,128)}) %all-reduce.5.cloned.1.call-update) | async-done | bytes 3170320 | tf_op jit(solution)/shard_map/psum | solution.py:111
  402.3 1.4 fusion.63
  403.7 1.4 slice.66
  405.1 3.9 slice.69
  (65 shorter events, 7.3 us)
Async XLA Ops:
  7.2 17.7 %copy-start = (bf16[1,48,320]{2,1,0:T(8,128)(2,1)S(1)}, bf16[1,48,320]{2,1,0:T(8,128)(2,1)}, u32[]{:S(2)}) copy-start(bf16[1,48,320]{2,1,0:T(8,128)(2,1)} %param.8) | copy-start | bytes 92164
  11.7 23.3 %all-to-all-start = ((s32[64,2,2]{1,2,0:T(2,128)}), s32[64,2,2]{1,2,0:T(2,128)S(1)}, u32[]{:S(2)}, u32[]{:S(2)}) async-start(s32[64,2,2]{1,2,0:T(2,128)} %copy.46), calls=%async_computation | async-start | bytes 131072 | tf_op jit(solution)/shard_map/all_to_all | solution.py:97
  35.0 15.2 %all-to-all-start.1 = ((bf16[64,2,320]{2,1,0:T(2,128)(2,1)}), bf16[64,2,320]{2,1,0:T(2,128)(2,1)S(1)}, u32[]{:S(2)}, u32[]{:S(2)}) async-start(bf16[64,2,320]{2,1,0:T(2,128)(2,1)} %reshape.207), calls=%async_computation.1 | async-start | bytes 196608 | tf_op jit(solution)/shard_map/all_to_all | solution.py:96
  39.4 362.9 %all-reduce.5.cloned.1.call-start = ((), (), s32[]{:S(2)}) async-start(), calls=%async_computation.2 | async-start | bytes 6356992 | tf_op jit(solution)/shard_map/psum | solution.py:111
  51.0 1.8 copy-start.10
  52.8 2.7 copy-start.2
  52.9 2.6 copy-start.12
  52.9 2.6 copy-start.13
  83.7 2.9 copy-start.4
  83.7 2.9 copy-start.5
  86.6 1.4 copy-start.6
  86.6 1.9 copy-start.14
  94.6 2.2 copy-start.3
  111.2 20.3 %slice-start = ((s8[6291456]{0:T(1024)(128)(4,1)}), s8[2097152]{0:T(1024)(128)(4,1)S(1)}, s32[]{:S(2)}) async-start(s8[6291456]{0:T(1024)(128)(4,1)} %bitcast.91), calls=%async_computation.3 | async-start | bytes 4194304
  119.9 9.6 %copy-start.7 = (f32[1,512,512]{2,1,0:T(8,128)S(1)}, f32[1,512,512]{2,1,0:T(8,128)}, u32[]{:S(2)}) copy-start(f32[1,512,512]{2,1,0:T(8,128)} %convolution_bitcast_fusion.1) | copy-start | bytes 3145732
  119.9 9.6 %copy-start.8 = (f32[1,512,512]{2,1,0:T(8,128)S(1)}, f32[1,512,512]{2,1,0:T(8,128)}, u32[]{:S(2)}) copy-start(f32[1,512,512]{2,1,0:T(8,128)} %convolution_bitcast_fusion) | copy-start | bytes 3145732
  119.9 9.6 %copy-start.9 = (f32[1,512,512]{2,1,0:T(8,128)S(1)}, f32[1,512,512]{2,1,0:T(8,128)}, u32[]{:S(2)}) copy-start(f32[1,512,512]{2,1,0:T(8,128)} %convolution_bitcast_fusion.2) | copy-start | bytes 3145732
  119.9 11.6 %slice-start.1 = ((s8[6291456]{0:T(1024)(128)(4,1)}), s8[4194304]{0:T(1024)(128)(4,1)S(1)}, s32[]{:S(2)}) async-start(s8[6291456]{0:T(1024)(128)(4,1)} %bitcast.91), calls=%async_computation.4 | async-start | bytes 8388608
  129.5 2.0 copy-start.11
  403.7 5.3 %copy-start.1 = (bf16[1,48,320]{2,1,0:T(8,128)(2,1)S(1)}, bf16[1,48,320]{2,1,0:T(8,128)(2,1)}, u32[]{:S(2)}) copy-start(bf16[1,48,320]{2,1,0:T(8,128)(2,1)} %param.8) | copy-start | bytes 92164
Sparse Core Ops, SparseCore 0:
  144.4 257.8 all-reduce.4
where the time goes:
time: 419 us; the launch traced here: 416 us
  waiting for transfers between devices  277 us (66%)
  local copies, waits for them, and re-layouts  63.1 us (15%)
  matrix products  23.2 us (6%)
  other arithmetic  20.3 us (5%)
  starting transfers between devices  17.6 us (4%)
  between operations  14.3 us (3%)
    psum x1, waiting for transfers between devices, body(): total = lax.psum(rows, ('dp', 'rep'))  258 us
    slice x3, local copies, waits for them, and re-layouts, encode(): taps = [hidden[:, k:k + 2 * frames_one - 1:2] for k in range(3)]  25.3 us
    dot_general x10, matrix products, product(): return jnp.einsum(form, left, right, preferred_element_type=jnp.float32)  20.8 us
    all_to_all x1, starting transfers between devices, body(): lax.all_to_all(send_meta, 'dp', split_axis=0, concat_axis=0, tiled=True)  13.2 us
    concatenate x1, local copies, waits for them, and re-layouts, encode(): jnp.concatenate([weight_zero, grad_g[None], grad_b[None], weight_one.resh...  10.5 us
    all_to_all x1, waiting for transfers between devices, body(): lax.all_to_all(send_wave, 'dp', split_axis=0, concat_axis=0, tiled=True)  10.2 us
    reduce_sum x1, other arithmetic, encode(): grad_g = jnp.sum(dpre * normed, axis=(0, 1))  9.51 us
    all_to_all x1, waiting for transfers between devices, body(): lax.all_to_all(send_meta, 'dp', split_axis=0, concat_axis=0, tiled=True)  9.02 us
  transfers between devices with their start and end apart: 3, of which 3 were waited for; matrix products, arithmetic and copies ran while one was open for 0% of the time, Pallas kernels for 0%

commit v1 on v0

v1 whole, which is shorter than its diff:
```python
import functools

import jax
import jax.numpy as jnp
import numpy as np
from jax import lax
from jax.experimental import pallas as pl
from jax.experimental.pallas import tpu as pltpu
from jax.sharding import PartitionSpec as P

BF, F32 = jnp.bfloat16, jnp.float32
VM = pl.BlockSpec(memory_space=pltpu.VMEM)
SM = pl.BlockSpec(memory_space=pltpu.SMEM)
BOTH = ("dp", "rep")
SAMPLES = 320


def call(kernel, outs, ins, scal=None, scratch=(), limit=48):
    specs = [VM] * len(ins)
    if scal is not None:
        specs = [SM] + specs
        ins = [scal] + list(ins)
    shapes = [jax.ShapeDtypeStruct(s, d) for s, d in outs]
    return pl.pallas_call(
        kernel,
        out_shape=shapes,
        in_specs=specs,
        out_specs=[VM] * len(outs),
        scratch_shapes=[pltpu.VMEM(s, d) for s, d in scratch],
        compiler_params=pltpu.CompilerParams(vmem_limit_bytes=limit << 20),
    )(*ins)


def perms():
    every = [(z, y, c, x) for z in range(8) for y in range(4) for c in range(2) for x in range(4)]

    def lin(z, y, c, x):
        return ((z * 4 + y) * 2 + c) * 4 + x

    def build(move):
        return [(lin(*p), lin(*move(*p))) for p in every]

    def along(first, k):
        def move(z, y, c, x):
            if (c == 0) == first:
                return (z, y, c, (x + k) % 4)
            return (z, (y + k) % 4, c, x)

        return build(move)

    core = build(lambda z, y, c, x: (z, y, 1 - c, x))
    one = [along(True, k) for k in range(1, 4)]
    two = [along(False, k) for k in range(1, 4)]
    pair = build(lambda z, y, c, x: (z ^ 1, y, c, x))
    quad = [build(lambda z, y, c, x, k=k: ((z + 2 * k) % 8, y, c, x)) for k in range(1, 4)]
    return core, one, two, pair, quad


def send(value, perm):
    return lax.ppermute(value, BOTH, perm)


def split(value):
    high = value.astype(BF)
    return high, (value - high.astype(F32)).astype(BF)


def k_scatter_one(pos, own, got, m1, m2, m3, keep):
    a1, core = pos[0], pos[2]
    for k, out in ((0, None), (1, m1), (2, m2), (3, m3)):
        j = (a1 + k) & 3
        mine = pl.ds(pl.multiple_of(core * 768 + j * 192, 192), 192)
        theirs = pl.ds(pl.multiple_of(j * 192, 192), 192)
        total = own[mine, :] + got[theirs, :].astype(F32)
        if out is None:
            keep[...] = total
        else:
            out[...] = total.astype(BF)


def k_scatter_two(pos, keep, r1, r2, r3, small_a, small_b, m1, m2, m3, keep2, small):
    a2 = pos[1]
    for k, out in ((0, None), (1, m1), (2, m2), (3, m3)):
        rows = pl.ds(pl.multiple_of(((a2 + k) & 3) * 48, 16), 48)
        total = keep[rows, :] + r1[rows, :].astype(F32) + r2[rows, :].astype(F32) + r3[rows, :].astype(F32)
        if out is None:
            keep2[...] = total
        else:
            out[pl.ds(0, 48), :] = total.astype(BF)
    high, low = split(small_a[...] + small_b[...])
    small[pl.ds(0, 16), :] = high
    small[pl.ds(16, 16), :] = low
    for out in (m1, m2, m3):
        out[pl.ds(48, 16), :] = high
        out[pl.ds(64, 16), :] = low


def lift(ref, at):
    return ref[pl.ds(at, 16), :].astype(F32) + ref[pl.ds(at + 16, 16), :].astype(F32)


def put(out, at, value):
    high, low = split(value)
    out[pl.ds(at, 16), :] = high
    out[pl.ds(at + 16, 16), :] = low


def k_sum_two(keep2, small, r1, r2, r3, out):
    head = pl.ds(0, 48)
    out[head, :] = (
        (keep2[...] + r2[head, :].astype(F32)) + (r1[head, :].astype(F32) + r3[head, :].astype(F32))
    ).astype(BF)
    put(out, 48, (lift(small, 0) + lift(r2, 48)) + (lift(r1, 48) + lift(r3, 48)))


def k_pair(a, b, out):
    head = pl.ds(0, 48)
    out[head, :] = (a[head, :].astype(F32) + b[head, :].astype(F32)).astype(BF)
    put(out, 48, lift(a, 48) + lift(b, 48))


def k_quad(a, r1, r2, r3, out, small):
    head = pl.ds(0, 48)
    out[...] = (
        (a[head, :].astype(F32) + r2[head, :].astype(F32)) + (r1[head, :].astype(F32) + r3[head, :].astype(F32))
    ).astype(BF)
    put(small, 0, (lift(a, 48) + lift(r2, 48)) + (lift(r1, 48) + lift(r3, 48)))


def k_join_two(own, r1, r2, r3, small, out):
    for k, part in enumerate((own, r1, r2, r3)):
        out[pl.ds(48 * k, 48), :] = part[...]
    out[pl.ds(192, 32), :] = small[...]


def k_join_one(own, r1, r2, r3, out):
    for k, part in enumerate((own, r1, r2, r3)):
        out[pl.ds(192 * k, 192), :] = part[pl.ds(0, 192), :]
    put(out, 768, (lift(own, 192) + lift(r2, 192)) + (lift(r1, 192) + lift(r3, 192)))


def k_final(pos, own, got, out, small):
    small[...] = 0.5 * (lift(own, 768) + lift(got, 768))
    core, x, y = pos[2], pos[3], pos[4]

    def place(ref, base, first, second):
        for j1 in range(4):
            for j2 in range(4):
                at = ((first - j1) & 3) * 4 + ((second - j2) & 3)
                out[pl.ds(base + (j1 * 4 + j2) * 48, 48), :] = ref[pl.ds(pl.multiple_of(at * 48, 16), 48), :].astype(F32)

    @pl.when(core == 0)
    def _():
        place(own, 0, x, y)
        place(got, 768, y, x)

    @pl.when(core == 1)
    def _():
        place(got, 0, x, y)
        place(own, 768, y, x)


def where_am_i():
    dp, x = lax.axis_index("dp"), lax.axis_index("rep")
    core, y = dp % 2, (dp // 2) % 4
    first = jnp.where(core == 0, x, y)
    second = jnp.where(core == 0, y, x)
    return jnp.stack([first, second, core, x, y]).astype(jnp.int32)


def reduce_all(pos, own, other, small):
    core, one, two, pair, quad = perms()
    row = 512
    got = send(other, core)
    m1, m2, m3, keep = call(
        k_scatter_one, [((192, row), BF)] * 3 + [((192, row), F32)], [own, got], pos
    )
    small_b = send(small, core)
    r = [send(m, p) for m, p in zip((m1, m2, m3), one)]
    m1, m2, m3, keep2, s = call(
        k_scatter_two,
        [((80, row), BF)] * 3 + [((48, row), F32), ((32, row), BF)],
        [keep, *r, small, small_b],
        pos,
    )
    r = [send(m, p) for m, p in zip((m1, m2, m3), two)]
    (a,) = call(k_sum_two, [((80, row), BF)], [keep2, s, *r])
    b = send(a, pair)
    (a,) = call(k_pair, [((80, row), BF)], [a, b])
    r = [send(a, p) for p in quad]
    a, s = call(k_quad, [((48, row), BF), ((32, row), BF)], [a, *r])
    r = [send(a, p) for p in two]
    (a,) = call(k_join_two, [((224, row), BF)], [a, *r, s])
    r = [send(a, p) for p in one]
    (a,) = call(k_join_one, [((800, row), BF)], [a, *r])
    got = send(a, core)
    return call(k_final, [((1536, row), F32), ((16, row), F32)], [a, got], pos)


WIDE = 384


def k_pack(wave, length, target, out, rows):
    spans = wave.shape[0]
    goal = target[...].astype(F32)
    device = jnp.floor((goal + 0.5) * (1.0 / spans))
    slot = goal - device * spans
    up = lax.broadcasted_iota(jnp.int32, (spans, spans), 0)
    across = lax.broadcasted_iota(jnp.int32, (spans, spans), 1)

    def column(row):
        return jnp.sum(jnp.where(up == across, jnp.broadcast_to(row, (spans, spans)), 0.0), axis=1, keepdims=True)

    same = (column(device) == device) & (up < across)
    rank = jnp.sum(jnp.where(same, 1.0, 0.0), axis=0, keepdims=True)
    bucket = (device * 2.0 + rank).astype(jnp.int32)
    places = out.shape[0]
    pick = lax.broadcasted_iota(jnp.int32, (places, spans), 0) == bucket
    pick = jnp.where(pick, 1.0, 0.0).astype(BF)
    rows[...] = jnp.zeros(rows.shape, F32)
    rows[:, pl.ds(0, SAMPLES)] = wave[...].astype(F32)
    lane = lax.broadcasted_iota(jnp.int32, (spans, 128), 1)
    tail = rows[:, pl.ds(256, 128)]
    tail = jnp.where(lane == SAMPLES - 256, column(slot) + 1.0, tail)
    tail = jnp.where(lane == SAMPLES - 255, column(length[...].astype(F32)) - 214.0, tail)
    rows[:, pl.ds(256, 128)] = tail
    out[...] = jnp.dot(pick, rows[...].astype(BF), preferred_element_type=F32).astype(BF)


def gelu_parts(value):
    cumul = 0.5 * (1.0 + lax.erf(value * 0.7071067811865476))
    density = jnp.exp(-0.5 * value * value) * 0.3989422804014327
    return cumul, density


BLOCK = 8
ROWS = 32 * BLOCK


def tall(rows):
    return jnp.concatenate([rows] * 4, axis=0)


def dot_t(left, right):
    return lax.dot_general(left, right, (((0,), (0,)), ((), ())), preferred_element_type=F32)


def dot_nt(left, right):
    return lax.dot_general(left, right, (((1,), (1,)), ((), ())), preferred_element_type=F32)


def k_forward(
    scale, pos, arrived, fold, weo, gain, bias, weight, fgrad,
    feats, g, gs, se, so, ne, no, istd, valid, x, full, other,
    panels, window, am, pre, he, ho, hs, pre1,
):
    spans = panels.shape[0]
    arr = arrived[...]
    lane = lax.broadcasted_iota(jnp.int32, (128, 128), 1).astype(F32)
    meta = arr[:, 256:384].astype(F32)
    slot = meta[:, SAMPLES - 256 : SAMPLES - 255]
    place = jnp.where(slot - 1.0 == lane, 1.0, 0.0).astype(BF)
    moved = dot_t(place, arr)[0:spans]
    panels[...] = jnp.broadcast_to(moved[:, None, :], panels.shape)
    length = moved[:, SAMPLES + 1 : SAMPLES + 2] + 214.0
    count = jnp.broadcast_to(jnp.floor((length - 9.5) * 0.2) + 1.0, (spans, 128))
    valid[...] = jnp.broadcast_to(count[:, None, :], valid.shape)
    step = lax.broadcasted_iota(jnp.int32, (32, WIDE), 0) * 10
    sample = lax.broadcasted_iota(jnp.int32, (32, WIDE), 1)
    window[:, pl.ds(0, WIDE)] = jnp.where((sample >= step) & (sample < step + 10), 1.0, 0.0)
    window[:, pl.ds(WIDE, WIDE)] = jnp.where((sample >= step + 5) & (sample < step + 15), 1.0, 0.0)
    frame = lax.broadcasted_iota(jnp.int32, (32, 128), 0).astype(F32)

    def block(b, carry):
        base = b * BLOCK

        def patch(q, carry):
            p = base + q
            count = tall(valid[p])
            keep_e, keep_o = 2.0 * frame < count, 2.0 * frame + 1.0 < count
            rows = pl.ds(pl.multiple_of(q * 32, 32), 32)
            for t in range(6):
                part = tall(panels[p, :, pl.ds((t % 3) * 128, 128)])
                part = jnp.where(keep_e if t < 3 else keep_o, part * window[:, pl.ds(t * 128, 128)], 0.0)
                am[rows, pl.ds(t * 128, 128)] = part.astype(BF)
            return carry

        lax.fori_loop(0, BLOCK, patch, 0)
        every = pl.ds(pl.multiple_of(b * ROWS, ROWS), ROWS)
        xs = jnp.dot(am[...], fold[...], preferred_element_type=F32).astype(BF)
        x[every, :] = xs
        pre[...] = jnp.dot(xs, weo[...], preferred_element_type=F32)

        def norm(q, carry):
            p = base + q
            count = valid[p]
            inverse = 1.0 / count[0:1]
            wide = tall(count)
            keep_e, keep_o = 2.0 * frame < wide, 2.0 * frame + 1.0 < wide
            rows = pl.ds(pl.multiple_of(q * 32, 32), 32)
            at = pl.ds(pl.multiple_of(p * 32, 32), 32)
            for t in range(4):
                cols = pl.ds(t * 128, 128)
                e = pre[rows, cols]
                o = pre[rows, pl.ds(512 + t * 128, 128)]
                center = jnp.sum(e + o, axis=0, keepdims=True) * inverse
                e = jnp.where(keep_e, e - center, 0.0)
                o = jnp.where(keep_o, o - center, 0.0)
                variance = jnp.sum(e * e + o * o, axis=0, keepdims=True) * inverse
                rs = lax.rsqrt(variance + 1e-05)
                istd[p, :, cols] = jnp.broadcast_to(rs, (8, 128))
                scale_row, bias_row = gain[:, cols], bias[:, cols]
                for value, keep, n_ref, s_ref, h_ref in ((e, keep_e, ne, se, he), (o, keep_o, no, so, ho)):
                    value = value * rs
                    n_ref[at, cols] = value.astype(BF)
                    value = value * scale_row + bias_row
                    cumul, density = gelu_parts(value)
                    hidden = jnp.where(keep, value * cumul, 0.0)
                    s_ref[at, cols] = jnp.where(keep, cumul + value * density, 0.0).astype(BF)
                    h_ref[at, cols] = hidden.astype(BF)
                    if h_ref is he:
                        hs[rows, cols] = pltpu.roll(hidden, 31, 0).astype(BF)
            return carry

        lax.fori_loop(0, BLOCK, norm, 0)
        pre1[...] = (
            jnp.dot(he[every, :], weight[0], preferred_element_type=F32)
            + jnp.dot(ho[every, :], weight[1], preferred_element_type=F32)
            + jnp.dot(hs[...], weight[2], preferred_element_type=F32)
        )

        def second(q, carry):
            p = base + q
            count = tall(jnp.floor((valid[p] - 2.5) * 0.5) + 1.0)
            keep = frame < count
            rows = pl.ds(pl.multiple_of(q * 32, 32), 32)
            at = pl.ds(pl.multiple_of(p * 32, 32), 32)
            for t in range(4):
                cols = pl.ds(t * 128, 128)
                value = pre1[rows, cols]
                cumul, density = gelu_parts(value)
                act = jnp.where(keep, value * cumul, 0.0)
                feats[p, :, cols] = act[0:31].astype(BF)
                up = fgrad[p, :, cols].astype(F32) * scale
                up = jnp.concatenate([up, jnp.zeros((1, 128), F32)], axis=0)
                grad = jnp.where(keep, up * (cumul + value * density), 0.0)
                g[at, cols] = grad.astype(BF)
                gs[at, cols] = pltpu.roll(grad, 1, 0).astype(BF)
            return carry

        lax.fori_loop(0, BLOCK, second, 0)
        return carry

    lax.fori_loop(0, spans // BLOCK, block, 0)
    full[pl.ds(0, 512), :] = dot_t(he[...], g[...])
    full[pl.ds(512, 512), :] = dot_t(ho[...], g[...])
    full[pl.ds(1024, 512), :] = dot_t(he[...], gs[...])
    away = pl.ds(pl.multiple_of((1 - pos[2]) * 768, 768), 768)
    other[...] = full[away, :].astype(BF)


def k_backward(
    g, gs, se, so, ne, no, istd, valid, x, gain, weight, small,
    de, do, dxe, dxo, sums,
):
    spans = istd.shape[0]
    sums[...] = jnp.zeros(sums.shape, F32)

    def block(b, carry):
        base = b * BLOCK
        every = pl.ds(pl.multiple_of(b * ROWS, ROWS), ROWS)
        de[...] = dot_nt(g[every, :], weight[0]) + dot_nt(gs[every, :], weight[2])
        do[...] = dot_nt(g[every, :], weight[1])

        def back(q, carry):
            p = base + q
            inverse = 1.0 / valid[p, pl.ds(0, 1), :]
            rows = pl.ds(pl.multiple_of(q * 32, 32), 32)
            at = pl.ds(pl.multiple_of(p * 32, 32), 32)
            for t in range(4):
                cols = pl.ds(t * 128, 128)
                pe = de[rows, cols] * se[at, cols].astype(F32)
                po = do[rows, cols] * so[at, cols].astype(F32)
                e, o = ne[at, cols].astype(F32), no[at, cols].astype(F32)
                plain = jnp.sum(pe + po, axis=0, keepdims=True)
                mixed = jnp.sum(pe * e + po * o, axis=0, keepdims=True)
                sums[pl.ds(0, 1), cols] += mixed
                sums[pl.ds(1, 1), cols] += plain
                lead = istd[p, pl.ds(0, 1), cols] * gain[:, cols]
                plain, mixed = plain * inverse, mixed * inverse
                dxe[at, cols] = ((pe - plain - e * mixed) * lead).astype(BF)
                dxo[at, cols] = ((po - plain - o * mixed) * lead).astype(BF)
            return carry

        lax.fori_loop(0, BLOCK, back, 0)
        return carry

    lax.fori_loop(0, spans // BLOCK, block, 0)
    small[...] = dot_t(x[...], dxe[...])[0:16] + dot_t(x[...], dxo[...])[16:32]
    small[pl.ds(10, 1), :] = sums[pl.ds(0, 1), :]
    small[pl.ds(11, 1), :] = sums[pl.ds(1, 1), :]


def folding():
    table = np.zeros((2 * WIDE, 128), np.float32)
    for s in range(SAMPLES):
        table[s, s % 10] = 1.0
        if s >= 5:
            table[WIDE + s, 16 + (s - 5) % 10] = 1.0
    return jnp.asarray(table, BF)


def encode(pos, arrived, conv0_weight, norm_gain, norm_bias, conv1_weight, feature_grad, scale):
    spans = feature_grad.shape[0]
    rows = spans * 32
    zero = jnp.zeros
    weo = jnp.concatenate(
        [
            jnp.concatenate([conv0_weight, zero((6, 512), BF), zero((16, 512), BF)], axis=0),
            jnp.concatenate([zero((16, 512), BF), conv0_weight, zero((6, 512), BF)], axis=0),
        ],
        axis=1,
    )
    weo = jnp.concatenate([weo, zero((96, 1024), BF)], axis=0)
    gain, bias = norm_gain[None], norm_bias[None]
    wide = ((rows, 512), BF)
    feats, g, gs, se, so, ne, no, istd, valid, x, full, other = call(
        functools.partial(k_forward, scale),
        [
            (feature_grad.shape, BF), wide, wide, wide, wide, wide, wide,
            ((spans, 8, 512), F32), ((spans, 8, 128), F32), ((rows, 128), BF), ((1536, 512), F32), ((768, 512), BF),
        ],
        [arrived, folding(), weo, gain, bias, conv1_weight, feature_grad],
        pos,
        scratch=[
            ((spans, 8, WIDE), F32), ((32, 2 * WIDE), F32), ((ROWS, 2 * WIDE), BF), ((ROWS, 1024), F32),
            ((rows, 512), BF), ((rows, 512), BF), ((ROWS, 512), BF), ((ROWS, 512), F32),
        ],
    )
    (small,) = call(
        k_backward,
        [((16, 512), F32)],
        [g, gs, se, so, ne, no, istd, valid, x, gain, conv1_weight],
        scratch=[((ROWS, 512), F32), ((ROWS, 512), F32), ((rows, 512), BF), ((rows, 512), BF), ((8, 512), F32)],
    )
    return feats, full, other, small


def body(waveform, lengths, target, conv0_weight, norm_gain, norm_bias, conv1_weight, feature_grad):
    spans = waveform.shape[1]
    devices = lax.axis_size("dp")
    frames = feature_grad.shape[2]
    pos = where_am_i()
    (packed,) = call(
        k_pack, [((2 * devices, WIDE), BF)], [waveform[0], lengths, target], scratch=[((spans, WIDE), F32)]
    )
    arrived = lax.all_to_all(packed.reshape(devices, 2, WIDE), "dp", split_axis=0, concat_axis=0, tiled=True)
    arrived = arrived.reshape(2 * devices, WIDE)
    scale = 1.0 / float(lax.axis_size("rep") * devices * spans * frames) ** 0.5
    feats, full, other, small = encode(
        pos, arrived, conv0_weight, norm_gain, norm_bias, conv1_weight, feature_grad[0], scale
    )
    full, small = reduce_all(pos, full, other, small)
    return (feats[None], small[:10], small[10], small[11], full.reshape(conv1_weight.shape))


def solution(mesh):
    placed = (
        P("rep", "dp", None),
        P("rep", "dp"),
        P("rep", "dp"),
        P(),
        P(),
        P(),
        P(),
        P("rep", "dp", None, None),
    )
    return jax.shard_map(
        body,
        mesh=mesh,
        in_specs=placed,
        out_specs=(P("rep", "dp", None, None), P(), P(), P(), P()),
        check_vma=False,
    )
```

time: 419 us -> 129 us (0.31)
  waiting for transfers between devices: 277 us -> 32.9 us
  local copies, waits for them, and re-layouts: 63.1 us -> 11.6 us
  Pallas kernels: 0 us -> 38.4 us
  starting transfers between devices: 17.6 us -> 44.5 us
  matrix products: 23.2 us -> 0 us
  other arithmetic: 20.3 us -> 0.02 us
  between operations: 14.3 us -> 0.83 us
    psum x1 -> x0, waiting for transfers between devices: 258 us -> none  [body(): total = lax.psum(rows, ('dp', 'rep'))]
    pallas_call x0 -> x11, Pallas kernels: none -> 38.4 us  [call(): pl.pallas_call(kernel, out_shape=shapes, in_specs=specs, out_specs=[VM] *...]
    ppermute x0 -> x19, starting transfers between devices: none -> 31.3 us  [send(): return lax.ppermute(value, BOTH, perm)]
    slice x7 -> x1, local copies, waits for them, and re-layouts: 32 us -> 1.38 us  [body(): small[11]]
    ppermute x0 -> x19, waiting for transfers between devices: none -> 26 us  [send(): return lax.ppermute(value, BOTH, perm)]
    dot_general x14 -> x0, matrix products: 22.2 us -> none  [the longest x10 20.8 us: product(): return jnp.einsum(form, left, right, preferred_element_type=jnp.float32)]
    all_to_all x2 -> x1, waiting for transfers between devices: 19.3 us -> 6.89 us  [body(): lax.all_to_all(packed.reshape(devices, 2, WIDE), 'dp', split_axis=0, conc...]
    reduce_sum x3 -> x0, other arithmetic: 11.1 us -> none  [the longest x1 9.51 us: encode(): grad_g = jnp.sum(dpre * normed, axis=(0, 1))]
  transfers between devices with their start and end apart: 3 -> 20, of which waited for: 3 -> 15; matrix products, arithmetic and copies ran while one was open for 0% -> 4% of each run, Pallas kernels for 0% -> 8%
where the time goes in v1:
time: 129 us; the launch traced here: 128 us
  starting transfers between devices  44.5 us (34%)
  Pallas kernels  38.4 us (30%)
  waiting for transfers between devices  32.9 us (26%)
  local copies, waits for them, and re-layouts  11.6 us (9%)
    pallas_call x11, Pallas kernels, call(): pl.pallas_call(kernel, out_shape=shapes, in_specs=specs, out_specs=[VM] *...  38.4 us
    ppermute x19, starting transfers between devices, send(): return lax.ppermute(value, BOTH, perm)  31.3 us
    ppermute x19, waiting for transfers between devices, send(): return lax.ppermute(value, BOTH, perm)  26 us
    all_to_all x1, starting transfers between devices, body(): lax.all_to_all(packed.reshape(devices, 2, WIDE), 'dp', split_axis=0, conc...  13.2 us
    unnamed x22, local copies, waits for them, and re-layouts  9.44 us
    all_to_all x1, waiting for transfers between devices, body(): lax.all_to_all(packed.reshape(devices, 2, WIDE), 'dp', split_axis=0, conc...  6.89 us
  transfers between devices with their start and end apart: 20, of which 15 were waited for; matrix products, arithmetic and copies ran while one was open for 4% of the time, Pallas kernels for 8%

profile of v1, /device:TPU:1, one launch (start us, length us, event | category | flops | bytes accessed | tf_op | source)
XLA Modules:
  0.0 128.3 jit_solution(12429417008912510059)
XLA Ops:
  0.6 0.8 copy-done.4
  3.0 0.7 reshape.19
  3.6 13.2 %all-to-all-start = ((bf16[64,2,384]{2,1,0:T(2,128)(2,1)}), bf16[64,2,384]{2,1,0:T(2,128)(2,1)S(1)}, u32[]{:S(2)}, u32[]{:S(2)}) async-start(bf16[64,2,384]{2,1,0:T(2,128)(2,1)} %reshape.19), calls=%async_computation | async-start | bytes 196608 | tf_op jit(solution)/shard_map/all_to_all | solution.py:457
  16.9 3.5 %copy.17 = bf16[1,48,31,512]{3,2,1,0:T(8,128)(2,1)} copy(bf16[1,48,31,512]{3,1,2,0:T(8,128)(2,1)} %param.16) | data formatting | bytes 3047424 | tf_op args[7]
  20.5 6.9 %all-to-all-done = bf16[64,2,384]{2,1,0:T(2,128)(2,1)S(1)} async-done(((bf16[64,2,384]{2,1,0:T(2,128)(2,1)}), bf16[64,2,384]{2,1,0:T(2,128)(2,1)S(1)}, u32[]{:S(2)}, u32[]{:S(2)}) %all-to-all-start) | async-done | bytes 98336 | tf_op jit(solution)/shard_map/all_to_all | solution.py:457
  27.4 23.6 %shard_map.129 = (bf16[48,31,512]{2,1,0:T(8,128)(2,1)S(1)}, bf16[1536,512]{1,0:T(8,128)(2,1)S(1)}, bf16[1536,512]{1,0:T(8,128)(2,1)}, bf16[1536,512]{1,0:T(8,128...) custom-call(s32[5]{0:T(128)S(1)} %stack.23.pos, ...), custom_call_target="tpu_custom_call" | custom-call | tf_op jit(solution)/shard_map/pallas_call | solution.py:24
  51.4 1.9 %collective-permute-done.got = bf16[768,512]{1,0:T(8,128)(2,1)S(1)} collective-permute-done((bf16[768,512]{1,0:T(8,128)(2,1)S(1)}, bf16[768,512]{1,0:T(8,128)(2,1)S(1)}, u32[]{:S(2)}, u32[]{:S(2)}) %collective-permute-start) | collective-permute-done | bytes 786464 | tf_op jit(solution)/shard_map/ppermute | solution.py:60
  53.3 1.9 %copy-done = f32[1536,512]{1,0:T(8,128)S(1)} copy-done((f32[1536,512]{1,0:T(8,128)S(1)}, f32[1536,512]{1,0:T(8,128)}, u32[]{:S(2)}) %copy-start) | copy-done | bytes 3145752
  55.2 0.7 shard_map.130
  56.2 1.4 %collective-permute-start.2 = (bf16[192,512]{1,0:T(8,128)(2,1)S(1)}, bf16[192,512]{1,0:T(8,128)(2,1)S(1)}, u32[]{:S(2)}, u32[]{:S(2)}) collective-permute-start(bf16[192,512]{1,0:T(8,128)(2,1)S(1)} %get-tuple-element.35), channel_id=1, source_target_pairs={{0,2},{1,3},{2,0},{3,1},{4,20},{5,21},{6,22},{7,23},{8,10},{9,11},... | collective-permute-start | bytes 589832 | tf_op jit(solution)/shard_map/ppermute | solution.py:60
  57.6 1.6 %collective-permute-start.3 = (bf16[192,512]{1,0:T(8,128)(2,1)S(1)}, bf16[192,512]{1,0:T(8,128)(2,1)S(1)}, u32[]{:S(2)}, u32[]{:S(2)}) collective-permute-start(bf16[192,512]{1,0:T(8,128)(2,1)S(1)} %get-tuple-element.36), channel_id=1, source_target_pairs={{0,3},{1,0},{2,1},{3,2},{4,28},{5,29},{6,30},{7,31},{8,11},{9,8},{... | collective-permute-start | bytes 589832 | tf_op jit(solution)/shard_map/ppermute | solution.py:60
  59.2 10.6 %shard_map.131.small_a = f32[16,512]{1,0:T(8,128)S(1)} custom-call(bf16[1536,512]{1,0:T(8,128)(2,1)S(1)} %get-tuple-element.37.g, bf16[1536,512]{1,0:T(8,128)(2,1)S(1)} %copy-done.1, bf16[1536,512]{1,0:T(8,128)(2,1)S(1)} %copy-done.2, bf16[1536,512]{1,0:T(8,128)(2,1)} %get-tuple-element.40.so, bf16[1536,512]{1,0:T(8,128)(2,1)} %get-tuple-element.41.ne, ...), custom_call_target="tpu_custom_call" | custom-call | tf_op jit(solution)/shard_map/pallas_call | solution.py:24
  69.8 2.9 %collective-permute-start.4 = (f32[16,512]{1,0:T(8,128)S(1)}, f32[16,512]{1,0:T(8,128)S(1)}, u32[]{:S(2)}, u32[]{:S(2)}) collective-permute-start(f32[16,512]{1,0:T(8,128)S(1)} %shard_map.131.small_a), channel_id=1, source_target_pairs={{0,4},{1,5},{2,6},{3,7},{4,0},{5,1},{6,2},{7,3},{8,12},{9,13},{10,... | collective-permute-start | bytes 98312 | tf_op jit(solution)/shard_map/ppermute | solution.py:60
  72.7 0.9 collective-permute-done.4.small_b
  74.6 0.9 collective-permute-start.6
  75.5 1.6 %collective-permute-start.7 = (bf16[80,512]{1,0:T(8,128)(2,1)S(1)}, bf16[80,512]{1,0:T(8,128)(2,1)S(1)}, u32[]{:S(2)}, u32[]{:S(2)}) collective-permute-start(bf16[80,512]{1,0:T(8,128)(2,1)S(1)} %get-tuple-element.50), channel_id=1, source_target_pairs={{0,24},{1,25},{2,26},{3,27},{4,7},{5,4},{6,5},{7,6},{8,0},{9,1},{1... | collective-permute-start | bytes 245768 | tf_op jit(solution)/shard_map/ppermute | solution.py:60
  77.1 2.9 %collective-permute-done.5.r1 = bf16[80,512]{1,0:T(8,128)(2,1)S(1)} collective-permute-done((bf16[80,512]{1,0:T(8,128)(2,1)S(1)}, bf16[80,512]{1,0:T(8,128)(2,1)S(1)}, u32[]{:S(2)}, u32[]{:S(2)}) %collective-permute-start.5) | collective-permute-done | bytes 81952 | tf_op jit(solution)/shard_map/ppermute | solution.py:60
  81.2 2.9 %collective-permute-done.8.b = bf16[80,512]{1,0:T(8,128)(2,1)S(1)} collective-permute-done((bf16[80,512]{1,0:T(8,128)(2,1)S(1)}, bf16[80,512]{1,0:T(8,128)(2,1)S(1)}, u32[]{:S(2)}, u32[]{:S(2)}) %collective-permute-start.8) | collective-permute-done | bytes 81952 | tf_op jit(solution)/shard_map/ppermute | solution.py:60
  84.7 3.4 %collective-permute-start.10 = (bf16[80,512]{1,0:T(8,128)(2,1)S(1)}, bf16[80,512]{1,0:T(8,128)(2,1)S(1)}, u32[]{:S(2)}, u32[]{:S(2)}) collective-permute-start(bf16[80,512]{1,0:T(8,128)(2,1)S(1)} %shard_map.134.a), channel_id=1, source_target_pairs={{0,128},{1,129},{2,130},{3,131},{4,132},{5,133},{6,134},{7,135},{8... | collective-permute-start | bytes 245768 | tf_op jit(solution)/shard_map/ppermute | solution.py:60
  88.1 2.1 %collective-permute-done.11.r3 = bf16[80,512]{1,0:T(8,128)(2,1)S(1)} collective-permute-done((bf16[80,512]{1,0:T(8,128)(2,1)S(1)}, bf16[80,512]{1,0:T(8,128)(2,1)S(1)}, u32[]{:S(2)}, u32[]{:S(2)}) %collective-permute-start.11) | collective-permute-done | bytes 81952 | tf_op jit(solution)/shard_map/ppermute | solution.py:60
  90.3 2.6 %collective-permute-done.10.r2 = bf16[80,512]{1,0:T(8,128)(2,1)S(1)} collective-permute-done((bf16[80,512]{1,0:T(8,128)(2,1)S(1)}, bf16[80,512]{1,0:T(8,128)(2,1)S(1)}, u32[]{:S(2)}, u32[]{:S(2)}) %collective-permute-start.10) | collective-permute-done | bytes 81952 | tf_op jit(solution)/shard_map/ppermute | solution.py:60
  92.9 0.9 collective-permute-done.9.r1
  93.9 4.8 %collective-permute-start.14 = (bf16[48,512]{1,0:T(8,128)(2,1)S(1)}, bf16[48,512]{1,0:T(8,128)(2,1)S(1)}, u32[]{:S(2)}, u32[]{:S(2)}) collective-permute-start(bf16[48,512]{1,0:T(8,128)(2,1)S(1)} %get-tuple-element.51.own), channel_id=1, source_target_pairs={{0,24},{1,25},{2,26},{3,27},{4,7},{5,4},{6,5},{7,6},{8,0},{9,1},{1... | collective-permute-start | bytes 147464 | tf_op jit(solution)/shard_map/ppermute | solution.py:60
  99.9 3.4 %collective-permute-done.13.r2 = bf16[48,512]{1,0:T(8,128)(2,1)S(1)} collective-permute-done((bf16[48,512]{1,0:T(8,128)(2,1)S(1)}, bf16[48,512]{1,0:T(8,128)(2,1)S(1)}, u32[]{:S(2)}, u32[]{:S(2)}) %collective-permute-start.13) | collective-permute-done | bytes 49184 | tf_op jit(solution)/shard_map/ppermute | solution.py:60
  103.7 2.3 %collective-permute-start.16 = (bf16[224,512]{1,0:T(8,128)(2,1)S(1)}, bf16[224,512]{1,0:T(8,128)(2,1)S(1)}, u32[]{:S(2)}, u32[]{:S(2)}) collective-permute-start(bf16[224,512]{1,0:T(8,128)(2,1)S(1)} %shard_map.136.own), channel_id=1, source_target_pairs={{0,2},{1,3},{2,0},{3,1},{4,20},{5,21},{6,22},{7,23},{8,10},{9,11},... | collective-permute-start | bytes 688136 | tf_op jit(solution)/shard_map/ppermute | solution.py:60
  106.4 2.5 %collective-permute-done.17.r3 = bf16[224,512]{1,0:T(8,128)(2,1)S(1)} collective-permute-done((bf16[224,512]{1,0:T(8,128)(2,1)S(1)}, bf16[224,512]{1,0:T(8,128)(2,1)S(1)}, u32[]{:S(2)}, u32[]{:S(2)}) %collective-permute-start.17) | collective-permute-done | bytes 229408 | tf_op jit(solution)/shard_map/ppermute | solution.py:60
  108.9 2.3 %collective-permute-done.16.r2 = bf16[224,512]{1,0:T(8,128)(2,1)S(1)} collective-permute-done((bf16[224,512]{1,0:T(8,128)(2,1)S(1)}, bf16[224,512]{1,0:T(8,128)(2,1)S(1)}, u32[]{:S(2)}, u32[]{:S(2)}) %collective-permute-start.16) | collective-permute-done | bytes 229408 | tf_op jit(solution)/shard_map/ppermute | solution.py:60
  111.2 2.4 %collective-permute-done.15.r1 = bf16[224,512]{1,0:T(8,128)(2,1)S(1)} collective-permute-done((bf16[224,512]{1,0:T(8,128)(2,1)S(1)}, bf16[224,512]{1,0:T(8,128)(2,1)S(1)}, u32[]{:S(2)}, u32[]{:S(2)}) %collective-permute-start.15) | collective-permute-done | bytes 229408 | tf_op jit(solution)/shard_map/ppermute | solution.py:60
  113.6 8.8 %collective-permute-start.18 = (bf16[800,512]{1,0:T(8,128)(2,1)S(1)}, bf16[800,512]{1,0:T(8,128)(2,1)S(1)}, u32[]{:S(2)}, u32[]{:S(2)}) collective-permute-start(bf16[800,512]{1,0:T(8,128)(2,1)S(1)} %shard_map.137.own), channel_id=1, source_target_pairs={{0,4},{1,5},{2,6},{3,7},{4,0},{5,1},{6,2},{7,3},{8,12},{9,13},{10,... | collective-permute-start | bytes 2457608 | tf_op jit(solution)/shard_map/ppermute | solution.py:60
  122.5 2.0 %copy.15 = bf16[1,48,31,512]{3,1,2,0:T(8,128)(2,1)} copy(bf16[1,48,31,512]{3,2,1,0:T(8,128)(2,1)S(1)} %bitcast.16) | data formatting | bytes 3047424
  124.5 2.4 %shard_map.138 = (f32[1536,512]{1,0:T(8,128)}, f32[16,512]{1,0:T(8,128)}) custom-call(s32[5]{0:T(128)S(1)} %stack.23.pos, bf16[800,512]{1,0:T(8,128)(2,1)S(1)} %shard_map.137.own, bf16[800,512]{1,0:T(8,128)(2,1)S(1)} %collective-permute-done.18.got), custom_call_target="tpu_custom_call" | custom-call | tf_op jit(solution)/shard_map/pallas_call | solution.py:24
  126.9 1.4 %fusion.11 = (f32[1,512]{1,0:T(1,128)}, f32[1,512]{1,0:T(1,128)}) fusion(f32[16,512]{1,0:T(8,128)} %get-tuple-element.53), kind=kLoop, calls=%fused_computation.13 | loop fusion | bytes 8192 | tf_op jit(solution)/shard_map/slice | solution.py:464
  (48 shorter events, 7.4 us)
Async XLA Ops:
  0.6 0.8 copy-start.4
  1.4 0.7 copy-start.7
  2.1 0.7 copy-start.8
  3.6 23.7 %all-to-all-start = ((bf16[64,2,384]{2,1,0:T(2,128)(2,1)}), bf16[64,2,384]{2,1,0:T(2,128)(2,1)S(1)}, u32[]{:S(2)}, u32[]{:S(2)}) async-start(bf16[64,2,384]{2,1,0:T(2,128)(2,1)} %reshape.19), calls=%async_computation | async-start | bytes 196608 | tf_op jit(solution)/shard_map/all_to_all | solution.py:457
  16.8 3.6 %copy-start.9 = (bf16[10,512]{1,0:T(8,128)(2,1)S(1)}, bf16[10,512]{1,0:T(8,128)(2,1)}, u32[]{:S(2)}) copy-start(bf16[10,512]{1,0:T(8,128)(2,1)} %param.12) | copy-start | bytes 30724
  16.9 10.5 %copy-start.3 = (bf16[768,128]{1,0:T(8,128)(2,1)S(1)}, bf16[768,128]{1,0:T(8,128)(2,1)}, u32[]{:S(2)}) copy-start(bf16[768,128]{1,0:T(8,128)(2,1)} %constant.50.clone.fold) | copy-start | bytes 589828
  16.9 10.5 %copy-start.5 = (f32[512]{0:T(512)S(1)}, f32[512]{0:T(512)}, u32[]{:S(2)}) copy-start(f32[512]{0:T(512)} %param.13) | copy-start | bytes 6148
  16.9 10.5 %copy-start.6 = (f32[512]{0:T(512)S(1)}, f32[512]{0:T(512)}, u32[]{:S(2)}) copy-start(f32[512]{0:T(512)} %param.14) | copy-start | bytes 6148
  51.0 2.3 %collective-permute-start = (bf16[768,512]{1,0:T(8,128)(2,1)S(1)}, bf16[768,512]{1,0:T(8,128)(2,1)S(1)}, u32[]{:S(2)}, u32[]{:S(2)}) collective-permute-start(bf16[768,512]{1,0:T(8,128)(2,1)S(1)} %get-tuple-element.32), channel_id=1, source_target_pairs={{0,4},{1,5},{2,6},{3,7},{4,0},{5,1},{6,2},{7,3},{8,12},{9,13},{10,... | collective-permute-start | bytes 2359304 | tf_op jit(solution)/shard_map/ppermute | solution.py:60
  53.3 1.9 %copy-start = (f32[1536,512]{1,0:T(8,128)S(1)}, f32[1536,512]{1,0:T(8,128)}, u32[]{:S(2)}) copy-start(f32[1536,512]{1,0:T(8,128)} %get-tuple-element.31.own) | copy-start | bytes 9437188
  55.2 4.0 %copy-start.1 = (bf16[1536,512]{1,0:T(8,128)(2,1)S(1)}, bf16[1536,512]{1,0:T(8,128)(2,1)}, u32[]{:S(2)}) copy-start(bf16[1536,512]{1,0:T(8,128)(2,1)} %get-tuple-element.38.gs) | copy-start | bytes 4718596
  55.2 4.0 %copy-start.2 = (bf16[1536,512]{1,0:T(8,128)(2,1)S(1)}, bf16[1536,512]{1,0:T(8,128)(2,1)}, u32[]{:S(2)}) copy-start(bf16[1536,512]{1,0:T(8,128)(2,1)} %get-tuple-element.39.se) | copy-start | bytes 4718596
  55.9 17.7 %collective-permute-start.1 = (bf16[192,512]{1,0:T(8,128)(2,1)S(1)}, bf16[192,512]{1,0:T(8,128)(2,1)S(1)}, u32[]{:S(2)}, u32[]{:S(2)}) collective-permute-start(bf16[192,512]{1,0:T(8,128)(2,1)S(1)} %get-tuple-element.34), channel_id=1, source_target_pairs={{0,1},{1,2},{2,3},{3,0},{4,12},{5,13},{6,14},{7,15},{8,9},{9,10},{... | collective-permute-start | bytes 589832 | tf_op jit(solution)/shard_map/ppermute | solution.py:60
  56.2 17.4 %collective-permute-start.2 = (bf16[192,512]{1,0:T(8,128)(2,1)S(1)}, bf16[192,512]{1,0:T(8,128)(2,1)S(1)}, u32[]{:S(2)}, u32[]{:S(2)}) collective-permute-start(bf16[192,512]{1,0:T(8,128)(2,1)S(1)} %get-tuple-element.35), channel_id=1, source_target_pairs={{0,2},{1,3},{2,0},{3,1},{4,20},{5,21},{6,22},{7,23},{8,10},{9,11},... | collective-permute-start | bytes 589832 | tf_op jit(solution)/shard_map/ppermute | solution.py:60
  57.6 16.0 %collective-permute-start.3 = (bf16[192,512]{1,0:T(8,128)(2,1)S(1)}, bf16[192,512]{1,0:T(8,128)(2,1)S(1)}, u32[]{:S(2)}, u32[]{:S(2)}) collective-permute-start(bf16[192,512]{1,0:T(8,128)(2,1)S(1)} %get-tuple-element.36), channel_id=1, source_target_pairs={{0,3},{1,0},{2,1},{3,2},{4,28},{5,29},{6,30},{7,31},{8,11},{9,8},{... | collective-permute-start | bytes 589832 | tf_op jit(solution)/shard_map/ppermute | solution.py:60
  69.8 3.8 %collective-permute-start.4 = (f32[16,512]{1,0:T(8,128)S(1)}, f32[16,512]{1,0:T(8,128)S(1)}, u32[]{:S(2)}, u32[]{:S(2)}) collective-permute-start(f32[16,512]{1,0:T(8,128)S(1)} %shard_map.131.small_a), channel_id=1, source_target_pairs={{0,4},{1,5},{2,6},{3,7},{4,0},{5,1},{6,2},{7,3},{8,12},{9,13},{10,... | collective-permute-start | bytes 98312 | tf_op jit(solution)/shard_map/ppermute | solution.py:60
  74.2 5.8 %collective-permute-start.5 = (bf16[80,512]{1,0:T(8,128)(2,1)S(1)}, bf16[80,512]{1,0:T(8,128)(2,1)S(1)}, u32[]{:S(2)}, u32[]{:S(2)}) collective-permute-start(bf16[80,512]{1,0:T(8,128)(2,1)S(1)} %get-tuple-element.48), channel_id=1, source_target_pairs={{0,8},{1,9},{2,10},{3,11},{4,5},{5,6},{6,7},{7,4},{8,16},{9,17},{1... | collective-permute-start | bytes 245768 | tf_op jit(solution)/shard_map/ppermute | solution.py:60
  74.6 5.4 %collective-permute-start.6 = (bf16[80,512]{1,0:T(8,128)(2,1)S(1)}, bf16[80,512]{1,0:T(8,128)(2,1)S(1)}, u32[]{:S(2)}, u32[]{:S(2)}) collective-permute-start(bf16[80,512]{1,0:T(8,128)(2,1)S(1)} %get-tuple-element.49), channel_id=1, source_target_pairs={{0,16},{1,17},{2,18},{3,19},{4,6},{5,7},{6,4},{7,5},{8,24},{9,25},... | collective-permute-start | bytes 245768 | tf_op jit(solution)/shard_map/ppermute | solution.py:60
  75.5 5.1 %collective-permute-start.7 = (bf16[80,512]{1,0:T(8,128)(2,1)S(1)}, bf16[80,512]{1,0:T(8,128)(2,1)S(1)}, u32[]{:S(2)}, u32[]{:S(2)}) collective-permute-start(bf16[80,512]{1,0:T(8,128)(2,1)S(1)} %get-tuple-element.50), channel_id=1, source_target_pairs={{0,24},{1,25},{2,26},{3,27},{4,7},{5,4},{6,5},{7,6},{8,0},{9,1},{1... | collective-permute-start | bytes 245768 | tf_op jit(solution)/shard_map/ppermute | solution.py:60
  80.6 3.6 %collective-permute-start.8 = (bf16[80,512]{1,0:T(8,128)(2,1)S(1)}, bf16[80,512]{1,0:T(8,128)(2,1)S(1)}, u32[]{:S(2)}, u32[]{:S(2)}) collective-permute-start(bf16[80,512]{1,0:T(8,128)(2,1)S(1)} %shard_map.133.a), channel_id=1, source_target_pairs={{0,32},{1,33},{2,34},{3,35},{4,36},{5,37},{6,38},{7,39},{8,40},{9,... | collective-permute-start | bytes 245768 | tf_op jit(solution)/shard_map/ppermute | solution.py:60
  84.2 6.1 %collective-permute-start.11 = (bf16[80,512]{1,0:T(8,128)(2,1)S(1)}, bf16[80,512]{1,0:T(8,128)(2,1)S(1)}, u32[]{:S(2)}, u32[]{:S(2)}) collective-permute-start(bf16[80,512]{1,0:T(8,128)(2,1)S(1)} %shard_map.134.a), channel_id=1, source_target_pairs={{0,192},{1,193},{2,194},{3,195},{4,196},{5,197},{6,198},{7,199},{8... | collective-permute-start | bytes 245768 | tf_op jit(solution)/shard_map/ppermute | solution.py:60
  84.7 8.2 %collective-permute-start.10 = (bf16[80,512]{1,0:T(8,128)(2,1)S(1)}, bf16[80,512]{1,0:T(8,128)(2,1)S(1)}, u32[]{:S(2)}, u32[]{:S(2)}) collective-permute-start(bf16[80,512]{1,0:T(8,128)(2,1)S(1)} %shard_map.134.a), channel_id=1, source_target_pairs={{0,128},{1,129},{2,130},{3,131},{4,132},{5,133},{6,134},{7,135},{8... | collective-permute-start | bytes 245768 | tf_op jit(solution)/shard_map/ppermute | solution.py:60
  88.1 5.7 %collective-permute-start.9 = (bf16[80,512]{1,0:T(8,128)(2,1)S(1)}, bf16[80,512]{1,0:T(8,128)(2,1)S(1)}, u32[]{:S(2)}, u32[]{:S(2)}) collective-permute-start(bf16[80,512]{1,0:T(8,128)(2,1)S(1)} %shard_map.134.a), channel_id=1, source_target_pairs={{0,64},{1,65},{2,66},{3,67},{4,68},{5,69},{6,70},{7,71},{8,72},{9,... | collective-permute-start | bytes 245768 | tf_op jit(solution)/shard_map/ppermute | solution.py:60
  93.9 6.0 %collective-permute-start.14 = (bf16[48,512]{1,0:T(8,128)(2,1)S(1)}, bf16[48,512]{1,0:T(8,128)(2,1)S(1)}, u32[]{:S(2)}, u32[]{:S(2)}) collective-permute-start(bf16[48,512]{1,0:T(8,128)(2,1)S(1)} %get-tuple-element.51.own), channel_id=1, source_target_pairs={{0,24},{1,25},{2,26},{3,27},{4,7},{5,4},{6,5},{7,6},{8,0},{9,1},{1... | collective-permute-start | bytes 147464 | tf_op jit(solution)/shard_map/ppermute | solution.py:60
  98.7 4.5 %collective-permute-start.13 = (bf16[48,512]{1,0:T(8,128)(2,1)S(1)}, bf16[48,512]{1,0:T(8,128)(2,1)S(1)}, u32[]{:S(2)}, u32[]{:S(2)}) collective-permute-start(bf16[48,512]{1,0:T(8,128)(2,1)S(1)} %get-tuple-element.51.own), channel_id=1, source_target_pairs={{0,16},{1,17},{2,18},{3,19},{4,6},{5,7},{6,4},{7,5},{8,24},{9,25},... | collective-permute-start | bytes 147464 | tf_op jit(solution)/shard_map/ppermute | solution.py:60
  98.7 4.7 %collective-permute-start.12 = (bf16[48,512]{1,0:T(8,128)(2,1)S(1)}, bf16[48,512]{1,0:T(8,128)(2,1)S(1)}, u32[]{:S(2)}, u32[]{:S(2)}) collective-permute-start(bf16[48,512]{1,0:T(8,128)(2,1)S(1)} %get-tuple-element.51.own), channel_id=1, source_target_pairs={{0,8},{1,9},{2,10},{3,11},{4,5},{5,6},{6,7},{7,4},{8,16},{9,17},{1... | collective-permute-start | bytes 147464 | tf_op jit(solution)/shard_map/ppermute | solution.py:60
  103.4 5.5 %collective-permute-start.17 = (bf16[224,512]{1,0:T(8,128)(2,1)S(1)}, bf16[224,512]{1,0:T(8,128)(2,1)S(1)}, u32[]{:S(2)}, u32[]{:S(2)}) collective-permute-start(bf16[224,512]{1,0:T(8,128)(2,1)S(1)} %shard_map.136.own), channel_id=1, source_target_pairs={{0,3},{1,0},{2,1},{3,2},{4,28},{5,29},{6,30},{7,31},{8,11},{9,8},{... | collective-permute-start | bytes 688136 | tf_op jit(solution)/shard_map/ppermute | solution.py:60
  103.7 7.5 %collective-permute-start.16 = (bf16[224,512]{1,0:T(8,128)(2,1)S(1)}, bf16[224,512]{1,0:T(8,128)(2,1)S(1)}, u32[]{:S(2)}, u32[]{:S(2)}) collective-permute-start(bf16[224,512]{1,0:T(8,128)(2,1)S(1)} %shard_map.136.own), channel_id=1, source_target_pairs={{0,2},{1,3},{2,0},{3,1},{4,20},{5,21},{6,22},{7,23},{8,10},{9,11},... | collective-permute-start | bytes 688136 | tf_op jit(solution)/shard_map/ppermute | solution.py:60
  106.0 7.6 %collective-permute-start.15 = (bf16[224,512]{1,0:T(8,128)(2,1)S(1)}, bf16[224,512]{1,0:T(8,128)(2,1)S(1)}, u32[]{:S(2)}, u32[]{:S(2)}) collective-permute-start(bf16[224,512]{1,0:T(8,128)(2,1)S(1)} %shard_map.136.own), channel_id=1, source_target_pairs={{0,1},{1,2},{2,3},{3,0},{4,12},{5,13},{6,14},{7,15},{8,9},{9,10},{... | collective-permute-start | bytes 688136 | tf_op jit(solution)/shard_map/ppermute | solution.py:60
  113.6 10.8 %collective-permute-start.18 = (bf16[800,512]{1,0:T(8,128)(2,1)S(1)}, bf16[800,512]{1,0:T(8,128)(2,1)S(1)}, u32[]{:S(2)}, u32[]{:S(2)}) collective-permute-start(bf16[800,512]{1,0:T(8,128)(2,1)S(1)} %shard_map.137.own), channel_id=1, source_target_pairs={{0,4},{1,5},{2,6},{3,7},{4,0},{5,1},{6,2},{7,3},{8,12},{9,13},{10,... | collective-permute-start | bytes 2457608 | tf_op jit(solution)/shard_map/ppermute | solution.py:60

commit v2 on v1

--- a/solution.py
+++ b/solution.py
@@ -11,22 +11,25 @@
 BF, F32 = jnp.bfloat16, jnp.float32
 VM = pl.BlockSpec(memory_space=pltpu.VMEM)
 SM = pl.BlockSpec(memory_space=pltpu.SMEM)
+ANY = pl.BlockSpec(memory_space=pl.ANY)
+HBM = pl.BlockSpec(memory_space=pltpu.HBM)
 BOTH = ("dp", "rep")
 SAMPLES = 320
 
 
-def call(kernel, outs, ins, scal=None, scratch=(), limit=48):
-    specs = [VM] * len(ins)
+def call(kernel, outs, ins, scal=None, scratch=(), after=(), late=ANY, limit=20):
+    specs = [VM] * len(ins) + [late] * len(after)
+    ins = [*ins, *after]
     if scal is not None:
         specs = [SM] + specs
-        ins = [scal] + list(ins)
+        ins = [scal, *ins]
     shapes = [jax.ShapeDtypeStruct(s, d) for s, d in outs]
     return pl.pallas_call(
         kernel,
         out_shape=shapes,
         in_specs=specs,
         out_specs=[VM] * len(outs),
-        scratch_shapes=[pltpu.VMEM(s, d) for s, d in scratch],
+        scratch_shapes=[pltpu.VMEM(*s) if isinstance(s, tuple) else s for s in scratch],
         compiler_params=pltpu.CompilerParams(vmem_limit_bytes=limit << 20),
     )(*ins)
 
@@ -51,21 +54,15 @@
     core = build(lambda z, y, c, x: (z, y, 1 - c, x))
     one = [along(True, k) for k in range(1, 4)]
     two = [along(False, k) for k in range(1, 4)]
-    pair = build(lambda z, y, c, x: (z ^ 1, y, c, x))
-    quad = [build(lambda z, y, c, x, k=k: ((z + 2 * k) % 8, y, c, x)) for k in range(1, 4)]
-    return core, one, two, pair, quad
+    steps = [build(lambda z, y, c, x, flip=flip: (z ^ flip, y, c, x)) for flip in (1, 3, 7)]
+    return core, one, two, steps
 
 
 def send(value, perm):
     return lax.ppermute(value, BOTH, perm)
 
 
-def split(value):
-    high = value.astype(BF)
-    return high, (value - high.astype(F32)).astype(BF)
-
-
-def k_scatter_one(pos, own, got, m1, m2, m3, keep):
+def k_scatter_one(pos, own, got, before, m1, m2, m3, keep):
     a1, core = pos[0], pos[2]
     for k, out in ((0, None), (1, m1), (2, m2), (3, m3)):
         j = (a1 + k) & 3
@@ -78,7 +75,7 @@
             out[...] = total.astype(BF)
 
 
-def k_scatter_two(pos, keep, r1, r2, r3, small_a, small_b, m1, m2, m3, keep2, small):
+def k_scatter_two(pos, keep, r1, r2, r3, before, m1, m2, m3, keep2):
     a2 = pos[1]
     for k, out in ((0, None), (1, m1), (2, m2), (3, m3)):
         rows = pl.ds(pl.multiple_of(((a2 + k) & 3) * 48, 16), 48)
@@ -86,13 +83,7 @@
         if out is None:
             keep2[...] = total
         else:
-            out[pl.ds(0, 48), :] = total.astype(BF)
-    high, low = split(small_a[...] + small_b[...])
-    small[pl.ds(0, 16), :] = high
-    small[pl.ds(16, 16), :] = low
-    for out in (m1, m2, m3):
-        out[pl.ds(48, 16), :] = high
-        out[pl.ds(64, 16), :] = low
+            out[...] = total.astype(BF)
 
 
 def lift(ref, at):
@@ -100,17 +91,16 @@
 
 
 def put(out, at, value):
-    high, low = split(value)
+    high = value.astype(BF)
     out[pl.ds(at, 16), :] = high
-    out[pl.ds(at + 16, 16), :] = low
-
-
-def k_sum_two(keep2, small, r1, r2, r3, out):
-    head = pl.ds(0, 48)
-    out[head, :] = (
-        (keep2[...] + r2[head, :].astype(F32)) + (r1[head, :].astype(F32) + r3[head, :].astype(F32))
+    out[pl.ds(at + 16, 16), :] = (value - high.astype(F32)).astype(BF)
+
+
+def k_sum_two(keep2, r1, r2, r3, small, out):
+    out[pl.ds(0, 48), :] = (
+        (keep2[...] + r2[...].astype(F32)) + (r1[...].astype(F32) + r3[...].astype(F32))
     ).astype(BF)
-    put(out, 48, (lift(small, 0) + lift(r2, 48)) + (lift(r1, 48) + lift(r3, 48)))
+    put(out, 48, small[...])
 
 
 def k_pair(a, b, out):
@@ -119,18 +109,10 @@
     put(out, 48, lift(a, 48) + lift(b, 48))
 
 
-def k_quad(a, r1, r2, r3, out, small):
-    head = pl.ds(0, 48)
-    out[...] = (
-        (a[head, :].astype(F32) + r2[head, :].astype(F32)) + (r1[head, :].astype(F32) + r3[head, :].astype(F32))
-    ).astype(BF)
-    put(small, 0, (lift(a, 48) + lift(r2, 48)) + (lift(r1, 48) + lift(r3, 48)))
-
-
-def k_join_two(own, r1, r2, r3, small, out):
+def k_join_two(own, r1, r2, r3, out):
     for k, part in enumerate((own, r1, r2, r3)):
-        out[pl.ds(48 * k, 48), :] = part[...]
-    out[pl.ds(192, 32), :] = small[...]
+        out[pl.ds(48 * k, 48), :] = part[pl.ds(0, 48), :]
+    put(out, 192, (lift(own, 48) + lift(r2, 48)) + (lift(r1, 48) + lift(r3, 48)))
 
 
 def k_join_one(own, r1, r2, r3, out):
@@ -139,68 +121,96 @@
     put(out, 768, (lift(own, 192) + lift(r2, 192)) + (lift(r1, 192) + lift(r3, 192)))
 
 
-def k_final(pos, own, got, out, small):
-    small[...] = 0.5 * (lift(own, 768) + lift(got, 768))
-    core, x, y = pos[2], pos[3], pos[4]
-
-    def place(ref, base, first, second):
-        for j1 in range(4):
-            for j2 in range(4):
-                at = ((first - j1) & 3) * 4 + ((second - j2) & 3)
-                out[pl.ds(base + (j1 * 4 + j2) * 48, 48), :] = ref[pl.ds(pl.multiple_of(at * 48, 16), 48), :].astype(F32)
-
-    @pl.when(core == 0)
-    def _():
-        place(own, 0, x, y)
-        place(got, 768, y, x)
-
-    @pl.when(core == 1)
-    def _():
-        place(got, 0, x, y)
-        place(own, 768, y, x)
+def order(ref, out, j1, first, second):
+    for j2 in range(4):
+        at = ((first - j1) & 3) * 4 + ((second - j2) & 3)
+        out[pl.ds((j1 * 4 + j2) * 48, 48), :] = ref[pl.ds(pl.multiple_of(at * 48, 16), 48), :].astype(F32)
+
+
+def k_order(pos, own, out):
+    for j1 in range(4):
+        order(own, out, j1, pos[0], pos[1])
+
+
+def k_final(pos, ready, own, got, full, conv0, gain, bias, rest, sems):
+    core = pos[2]
+    mine = pltpu.make_async_copy(ready, full.at[pl.ds(pl.multiple_of(core * 768, 768), 768), :], sems.at[0])
+    mine.start()
+    copies = []
+    for j1 in range(4):
+        order(got, rest, j1, pos[1], pos[0])
+        at = pl.multiple_of((1 - core) * 768 + j1 * 192, 192)
+        copy = pltpu.make_async_copy(rest.at[pl.ds(j1 * 192, 192), :], full.at[pl.ds(at, 192), :], sems.at[1 + j1])
+        copy.start()
+        copies.append(copy)
+    total = lift(own, 768) + lift(got, 768)
+    conv0[...] = total[0:10]
+    gain[...] = total[10:11]
+    bias[...] = total[11:12]
+    mine.wait()
+    for copy in copies:
+        copy.wait()
 
 
 def where_am_i():
     dp, x = lax.axis_index("dp"), lax.axis_index("rep")
-    core, y = dp % 2, (dp // 2) % 4
+    core, y = lax.rem(dp, 2), lax.rem(lax.div(dp, 2), 4)
     first = jnp.where(core == 0, x, y)
     second = jnp.where(core == 0, y, x)
-    return jnp.stack([first, second, core, x, y]).astype(jnp.int32)
-
-
-def reduce_all(pos, own, other, small):
-    core, one, two, pair, quad = perms()
+    return jnp.stack([first, second, core]).astype(jnp.int32)
+
+
+def reduce_all(pos, own, other, backward, feats):
+    core, one, two, steps = perms()
     row = 512
+    third = ((48, row), BF)
     got = send(other, core)
+    small = backward(0, jnp.zeros((16, row), F32), other)
     m1, m2, m3, keep = call(
-        k_scatter_one, [((192, row), BF)] * 3 + [((192, row), F32)], [own, got], pos
-    )
-    small_b = send(small, core)
+        k_scatter_one, [((192, row), BF)] * 3 + [((192, row), F32)], [own, got], pos, after=[small]
+    )
     r = [send(m, p) for m, p in zip((m1, m2, m3), one)]
-    m1, m2, m3, keep2, s = call(
-        k_scatter_two,
-        [((80, row), BF)] * 3 + [((48, row), F32), ((32, row), BF)],
-        [keep, *r, small, small_b],
-        pos,
+    small = backward(1, small, keep)
+    m1, m2, m3, keep2 = call(
+        k_scatter_two, [third] * 3 + [((48, row), F32)], [keep, *r], pos, after=[small]
     )
     r = [send(m, p) for m, p in zip((m1, m2, m3), two)]
-    (a,) = call(k_sum_two, [((80, row), BF)], [keep2, s, *r])
-    b = send(a, pair)
-    (a,) = call(k_pair, [((80, row), BF)], [a, b])
-    r = [send(a, p) for p in quad]
-    a, s = call(k_quad, [((48, row), BF), ((32, row), BF)], [a, *r])
+    small = backward(2, small, keep2)
+    (a,) = call(k_sum_two, [((80, row), BF)], [keep2, *r, small])
+    for step in steps:
+        b = send(a, step)
+        (a,) = call(k_pair, [((80, row), BF)], [a, b])
     r = [send(a, p) for p in two]
-    (a,) = call(k_join_two, [((224, row), BF)], [a, *r, s])
+    (a,) = call(k_join_two, [((224, row), BF)], [a, *r])
+    feats = jnp.transpose(feats, (1, 0, 2))
     r = [send(a, p) for p in one]
+    a, feats, *r = lax.optimization_barrier((a, feats, *r))
     (a,) = call(k_join_one, [((800, row), BF)], [a, *r])
     got = send(a, core)
-    return call(k_final, [((1536, row), F32), ((16, row), F32)], [a, got], pos)
+    (ready,) = call(k_order, [((768, row), F32)], [a], pos)
+    full, conv0, gain, bias = pl.pallas_call(
+        k_final,
+        out_shape=[jax.ShapeDtypeStruct((n, row), F32) for n in (1536, 10, 1, 1)],
+        in_specs=[SM, VM, VM, VM],
+        out_specs=[ANY, VM, VM, VM],
+        scratch_shapes=[pltpu.VMEM((768, row), F32), pltpu.SemaphoreType.DMA((5,))],
+        compiler_params=pltpu.CompilerParams(vmem_limit_bytes=20 << 20),
+    )(pos, ready, a, got)
+    return full, conv0, gain[0], bias[0], jnp.transpose(feats, (1, 0, 2))
 
 
 WIDE = 384
 
 
-def k_pack(wave, length, target, out, rows):
+def k_pack(wave_in, length_in, target_in, out, rows, wave, length, target, sems):
+    copies = [
+        pltpu.make_async_copy(source, place, sems.at[n])
+        for n, (source, place) in enumerate(((wave_in, wave), (length_in, length), (target_in, target)))
+    ]
+    for copy in copies:
+        copy.start()
+    for copy in copies:
+        copy.wait()
     spans = wave.shape[0]
     goal = target[...].astype(F32)
     device = jnp.floor((goal + 0.5) * (1.0 / spans))
@@ -285,7 +295,7 @@
                 am[rows, pl.ds(t * 128, 128)] = part.astype(BF)
             return carry
 
-        lax.fori_loop(0, BLOCK, patch, 0)
+        lax.fori_loop(0, BLOCK, patch, 0, unroll=2)
         every = pl.ds(pl.multiple_of(b * ROWS, ROWS), ROWS)
         xs = jnp.dot(am[...], fold[...], preferred_element_type=F32).astype(BF)
         x[every, :] = xs
@@ -322,7 +332,7 @@
                         hs[rows, cols] = pltpu.roll(hidden, 31, 0).astype(BF)
             return carry
 
-        lax.fori_loop(0, BLOCK, norm, 0)
+        lax.fori_loop(0, BLOCK, norm, 0, unroll=2)
         pre1[...] = (
             jnp.dot(he[every, :], weight[0], preferred_element_type=F32)
             + jnp.dot(ho[every, :], weight[1], preferred_element_type=F32)
@@ -348,7 +358,7 @@
                 gs[at, cols] = pltpu.roll(grad, 1, 0).astype(BF)
             return carry
 
-        lax.fori_loop(0, BLOCK, second, 0)
+        lax.fori_loop(0, BLOCK, second, 0, unroll=2)
         return carry
 
     lax.fori_loop(0, spans // BLOCK, block, 0)
@@ -360,15 +370,15 @@
 
 
 def k_backward(
-    g, gs, se, so, ne, no, istd, valid, x, gain, weight, small,
+    step, g, gs, se, so, ne, no, istd, valid, x, gain, weight, start, before, small,
     de, do, dxe, dxo, sums,
 ):
-    spans = istd.shape[0]
+    blocks = dxe.shape[0] // ROWS
     sums[...] = jnp.zeros(sums.shape, F32)
 
     def block(b, carry):
-        base = b * BLOCK
-        every = pl.ds(pl.multiple_of(b * ROWS, ROWS), ROWS)
+        base = (step * blocks + b) * BLOCK
+        every = pl.ds(pl.multiple_of((step * blocks + b) * ROWS, ROWS), ROWS)
         de[...] = dot_nt(g[every, :], weight[0]) + dot_nt(gs[every, :], weight[2])
         do[...] = dot_nt(g[every, :], weight[1])
 
@@ -377,6 +387,7 @@
             inverse = 1.0 / valid[p, pl.ds(0, 1), :]
             rows = pl.ds(pl.multiple_of(q * 32, 32), 32)
             at = pl.ds(pl.multiple_of(p * 32, 32), 32)
+            here = pl.ds(pl.multiple_of((b * BLOCK + q) * 32, 32), 32)
             for t in range(4):
                 cols = pl.ds(t * 128, 128)
                 pe = de[rows, cols] * se[at, cols].astype(F32)
@@ -388,17 +399,17 @@
                 sums[pl.ds(1, 1), cols] += plain
                 lead = istd[p, pl.ds(0, 1), cols] * gain[:, cols]
                 plain, mixed = plain * inverse, mixed * inverse
-                dxe[at, cols] = ((pe - plain - e * mixed) * lead).astype(BF)
-                dxo[at, cols] = ((po - plain - o * mixed) * lead).astype(BF)
+                dxe[here, cols] = ((pe - plain - e * mixed) * lead).astype(BF)
+                dxo[here, cols] = ((po - plain - o * mixed) * lead).astype(BF)
             return carry
 
-        lax.fori_loop(0, BLOCK, back, 0)
+        lax.fori_loop(0, BLOCK, back, 0, unroll=2)
         return carry
 
-    lax.fori_loop(0, spans // BLOCK, block, 0)
-    small[...] = dot_t(x[...], dxe[...])[0:16] + dot_t(x[...], dxo[...])[16:32]
-    small[pl.ds(10, 1), :] = sums[pl.ds(0, 1), :]
-    small[pl.ds(11, 1), :] = sums[pl.ds(1, 1), :]
+    lax.fori_loop(0, blocks, block, 0)
+    part = x[pl.ds(step * blocks * ROWS, blocks * ROWS), :]
+    small[...] = start[...] + dot_t(part, dxe[...])[0:16] + dot_t(part, dxo[...])[16:32]
+    small[pl.ds(10, 2), :] += sums[pl.ds(0, 2), :]
 
 
 def folding():
@@ -437,13 +448,18 @@
             ((rows, 512), BF), ((rows, 512), BF), ((ROWS, 512), BF), ((ROWS, 512), F32),
         ],
     )
-    (small,) = call(
-        k_backward,
-        [((16, 512), F32)],
-        [g, gs, se, so, ne, no, istd, valid, x, gain, conv1_weight],
-        scratch=[((ROWS, 512), F32), ((ROWS, 512), F32), ((rows, 512), BF), ((rows, 512), BF), ((8, 512), F32)],
-    )
-    return feats, full, other, small
+
+    def backward(step, small, before):
+        part = (rows // 3, 512)
+        return call(
+            functools.partial(k_backward, step),
+            [((16, 512), F32)],
+            [g, gs, se, so, ne, no, istd, valid, x, gain, conv1_weight, small],
+            scratch=[((ROWS, 512), F32), ((ROWS, 512), F32), (part, BF), (part, BF), ((8, 512), F32)],
+            after=[before],
+        )[0]
+
+    return feats, full, other, backward
 
 
 def body(waveform, lengths, target, conv0_weight, norm_gain, norm_bias, conv1_weight, feature_grad):
@@ -452,16 +468,24 @@
     frames = feature_grad.shape[2]
     pos = where_am_i()
     (packed,) = call(
-        k_pack, [((2 * devices, WIDE), BF)], [waveform[0], lengths, target], scratch=[((spans, WIDE), F32)]
+        k_pack,
+        [((2 * devices, WIDE), BF)],
+        [],
+        scratch=[
+            ((spans, WIDE), F32), (waveform.shape[1:], BF), (lengths.shape, jnp.int32), (target.shape, jnp.int32),
+            pltpu.SemaphoreType.DMA((3,)),
+        ],
+        after=[waveform[0], lengths, target],
+        late=HBM,
     )
     arrived = lax.all_to_all(packed.reshape(devices, 2, WIDE), "dp", split_axis=0, concat_axis=0, tiled=True)
     arrived = arrived.reshape(2 * devices, WIDE)
     scale = 1.0 / float(lax.axis_size("rep") * devices * spans * frames) ** 0.5
-    feats, full, other, small = encode(
+    feats, full, other, backward = encode(
         pos, arrived, conv0_weight, norm_gain, norm_bias, conv1_weight, feature_grad[0], scale
     )
-    full, small = reduce_all(pos, full, other, small)
-    return (feats[None], small[:10], small[10], small[11], full.reshape(conv1_weight.shape))
+    full, conv0, gain, bias, feats = reduce_all(pos, full, other, backward, feats)
+    return (feats[None], conv0, gain, bias, full.reshape(conv1_weight.shape))
 
 
 def solution(mesh):

time: 129 us -> 114 us (0.88)
  Pallas kernels: 38.4 us -> 32.9 us
  starting transfers between devices: 44.5 us -> 39.2 us
  local copies, waits for them, and re-layouts: 11.6 us -> 8.98 us
  waiting for transfers between devices: 32.9 us -> 31.3 us
    pallas_call x11 -> x14, Pallas kernels: 38.4 us -> 30.1 us  [call(): pl.pallas_call(kernel, out_shape=shapes, in_specs=specs, out_specs=[VM] *...]
    ppermute x19 -> x17, starting transfers between devices: 31.3 us -> 25.8 us  [send(): return lax.ppermute(value, BOTH, perm)]
    pallas_call x0 -> x1, Pallas kernels: none -> 2.86 us  [reduce_all(): pl.pallas_call(k_final, out_shape=[jax.ShapeDtypeStruct((n, row), F32) fo...]
    ppermute x19 -> x17, waiting for transfers between devices: 26 us -> 23.3 us  [send(): return lax.ppermute(value, BOTH, perm)]
    unnamed x22 -> x18, local copies, waits for them, and re-layouts: 9.44 us -> 7.36 us
    slice x1 -> x0, local copies, waits for them, and re-layouts: 1.38 us -> none  [body(): small[11]]
  transfers between devices with their start and end apart: 20 -> 18, of which waited for: 15 -> 12; matrix products, arithmetic and copies ran while one was open for 4% -> 4% of each run, Pallas kernels for 8% -> 7%
where the time goes in v2:
time: 114 us
  starting transfers between devices  39.2 us (34%)
  Pallas kernels  32.9 us (29%)
  waiting for transfers between devices  31.3 us (27%)
  local copies, waits for them, and re-layouts  8.98 us (8%)
    pallas_call x14, Pallas kernels, call(): pl.pallas_call(kernel, out_shape=shapes, in_specs=specs, out_specs=[VM] *...  30.1 us
    ppermute x17, starting transfers between devices, send(): return lax.ppermute(value, BOTH, perm)  25.8 us
    ppermute x17, waiting for transfers between devices, send(): return lax.ppermute(value, BOTH, perm)  23.3 us
    all_to_all x1, starting transfers between devices, body(): lax.all_to_all(packed.reshape(devices, 2, WIDE), 'dp', split_axis=0, conc...  13.3 us
    all_to_all x1, waiting for transfers between devices, body(): lax.all_to_all(packed.reshape(devices, 2, WIDE), 'dp', split_axis=0, conc...  7.96 us
    unnamed x18, local copies, waits for them, and re-layouts  7.36 us
    pallas_call x1, Pallas kernels, reduce_all(): pl.pallas_call(k_final, out_shape=[jax.ShapeDtypeStruct((n, row), F32) fo...  2.86 us
  transfers between devices with their start and end apart: 18, of which 12 were waited for; matrix products, arithmetic and copies ran while one was open for 4% of the time, Pallas kernels for 7%

profile of v2, /device:TPU:1, one launch (start us, length us, event | category | flops | bytes accessed | tf_op | source)
XLA Modules:
  0.0 113.5 jit_solution(16989529434982222290)
XLA Ops:
  0.6 0.8 copy-done.2
  3.0 0.7 reshape.19
  3.7 13.3 %all-to-all-start = ((bf16[64,2,384]{2,1,0:T(2,128)(2,1)}), bf16[64,2,384]{2,1,0:T(2,128)(2,1)}, u32[]{:S(2)}, u32[]{:S(2)}) async-start(bf16[64,2,384]{2,1,0:T(2,128)(2,1)} %reshape.19), calls=%async_computation | async-start | bytes 196608 | tf_op jit(solution)/shard_map/all_to_all | solution.py:481
  17.1 2.3 %copy.17 = bf16[1,48,31,512]{3,2,1,0:T(8,128)(2,1)S(1)} copy(bf16[1,48,31,512]{3,1,2,0:T(8,128)(2,1)} %param.16) | data formatting | bytes 3047424 | tf_op args[7]
  19.6 8.0 %all-to-all-done = bf16[64,2,384]{2,1,0:T(2,128)(2,1)} async-done(((bf16[64,2,384]{2,1,0:T(2,128)(2,1)}), bf16[64,2,384]{2,1,0:T(2,128)(2,1)}, u32[]{:S(2)}, u32[]{:S(2)}) %all-to-all-start) | async-done | bytes 98336 | tf_op jit(solution)/shard_map/all_to_all | solution.py:481
  27.5 0.9 reshape.20.arrived
  28.5 0.9 copy-done.1
  29.4 19.8 %shard_map.129 = (bf16[48,31,512]{2,1,0:T(8,128)(2,1)S(1)}, bf16[1536,512]{1,0:T(8,128)(2,1)S(1)}, bf16[1536,512]{1,0:T(8,128)(2,1)S(1)}, bf16[1536,512]{1,0:T(8...) custom-call(s32[3]{0:T(128)S(1)} %pad_add_fusion.pos, ...), custom_call_target="tpu_custom_call" | custom-call | tf_op jit(solution)/shard_map/pallas_call | solution.py:27
  49.7 2.6 %shard_map.130.before.start = f32[16,512]{1,0:T(8,128)S(1)} custom-call(bf16[1536,512]{1,0:T(8,128)(2,1)S(1)} %get-tuple-element.36.g, bf16[1536,512]{1,0:T(8,128)(2,1)S(1)} %get-tuple-element.37.gs, bf16[1536,512]{1,0:T(8,128)(2,1)S(1)} %get-tuple-element.38.se, bf16[1536,512]{1,0:T(8,128)(2,1)S(1)} %get-tuple-element.39.so, ...), custom_call_target="tpu_custom_call" | custom-call | tf_op jit(solution)/shard_map/pallas_call | solution.py:27
  53.3 1.5 %collective-permute-start.2 = (bf16[192,512]{1,0:T(8,128)(2,1)S(1)}, bf16[192,512]{1,0:T(8,128)(2,1)S(1)}, u32[]{:S(2)}, u32[]{:S(2)}) collective-permute-start(bf16[192,512]{1,0:T(8,128)(2,1)S(1)} %get-tuple-element.47), channel_id=1, source_target_pairs={{0,2},{1,3},{2,0},{3,1},{4,20},{5,21},{6,22},{7,23},{8,10},{9,11},... | collective-permute-start | bytes 589832 | tf_op jit(solution)/shard_map/ppermute | solution.py:62
  54.7 1.5 %collective-permute-start.3 = (bf16[192,512]{1,0:T(8,128)(2,1)S(1)}, bf16[192,512]{1,0:T(8,128)(2,1)S(1)}, u32[]{:S(2)}, u32[]{:S(2)}) collective-permute-start(bf16[192,512]{1,0:T(8,128)(2,1)S(1)} %get-tuple-element.48), channel_id=1, source_target_pairs={{0,3},{1,0},{2,1},{3,2},{4,28},{5,29},{6,30},{7,31},{8,11},{9,8},{... | collective-permute-start | bytes 589832 | tf_op jit(solution)/shard_map/ppermute | solution.py:62
  56.3 2.6 %shard_map.132.before.start = f32[16,512]{1,0:T(8,128)S(1)} custom-call(bf16[1536,512]{1,0:T(8,128)(2,1)S(1)} %get-tuple-element.36.g, bf16[1536,512]{1,0:T(8,128)(2,1)S(1)} %get-tuple-element.37.gs, bf16[1536,512]{1,0:T(8,128)(2,1)S(1)} %get-tuple-element.38.se, bf16[1536,512]{1,0:T(8,128)(2,1)S(1)} %get-tuple-element.39.so, ...), custom_call_target="tpu_custom_call" | custom-call | tf_op jit(solution)/shard_map/pallas_call | solution.py:27
  58.9 2.3 %collective-permute-done.1.r1 = bf16[192,512]{1,0:T(8,128)(2,1)S(1)} collective-permute-done((bf16[192,512]{1,0:T(8,128)(2,1)S(1)}, bf16[192,512]{1,0:T(8,128)(2,1)S(1)}, u32[]{:S(2)}, u32[]{:S(2)}) %collective-permute-start.1) | collective-permute-done | bytes 196640 | tf_op jit(solution)/shard_map/ppermute | solution.py:62
  62.5 1.3 %collective-permute-start.4 = (bf16[48,512]{1,0:T(8,128)(2,1)S(1)}, bf16[48,512]{1,0:T(8,128)(2,1)S(1)}, u32[]{:S(2)}, u32[]{:S(2)}) collective-permute-start(bf16[48,512]{1,0:T(8,128)(2,1)S(1)} %get-tuple-element.50), channel_id=1, source_target_pairs={{0,8},{1,9},{2,10},{3,11},{4,5},{5,6},{6,7},{7,4},{8,16},{9,17},{1... | collective-permute-start | bytes 147464 | tf_op jit(solution)/shard_map/ppermute | solution.py:62
  63.8 2.5 %collective-permute-start.5 = (bf16[48,512]{1,0:T(8,128)(2,1)S(1)}, bf16[48,512]{1,0:T(8,128)(2,1)S(1)}, u32[]{:S(2)}, u32[]{:S(2)}) collective-permute-start(bf16[48,512]{1,0:T(8,128)(2,1)S(1)} %get-tuple-element.51), channel_id=1, source_target_pairs={{0,16},{1,17},{2,18},{3,19},{4,6},{5,7},{6,4},{7,5},{8,24},{9,25},... | collective-permute-start | bytes 147464 | tf_op jit(solution)/shard_map/ppermute | solution.py:62
  66.2 1.1 collective-permute-start.6
  67.4 2.6 %shard_map.134.small = f32[16,512]{1,0:T(8,128)S(1)} custom-call(bf16[1536,512]{1,0:T(8,128)(2,1)S(1)} %get-tuple-element.36.g, bf16[1536,512]{1,0:T(8,128)(2,1)S(1)} %get-tuple-element.37.gs, bf16[1536,512]{1,0:T(8,128)(2,1)S(1)} %get-tuple-element.38.se, bf16[1536,512]{1,0:T(8,128)(2,1)S(1)} %get-tuple-element.39.so, ...), custom_call_target="tpu_custom_call" | custom-call | tf_op jit(solution)/shard_map/pallas_call | solution.py:27
  70.5 3.0 %collective-permute-done.7.b = bf16[80,512]{1,0:T(8,128)(2,1)S(1)} collective-permute-done((bf16[80,512]{1,0:T(8,128)(2,1)S(1)}, bf16[80,512]{1,0:T(8,128)(2,1)S(1)}, u32[]{:S(2)}, u32[]{:S(2)}) %collective-permute-start.7) | collective-permute-done | bytes 81952 | tf_op jit(solution)/shard_map/ppermute | solution.py:62
  73.4 0.9 collective-permute-start.8
  74.3 4.4 %collective-permute-done.8.b = bf16[80,512]{1,0:T(8,128)(2,1)S(1)} collective-permute-done((bf16[80,512]{1,0:T(8,128)(2,1)S(1)}, bf16[80,512]{1,0:T(8,128)(2,1)S(1)}, u32[]{:S(2)}, u32[]{:S(2)}) %collective-permute-start.8) | collective-permute-done | bytes 81952 | tf_op jit(solution)/shard_map/ppermute | solution.py:62
  79.1 4.1 %collective-permute-done.9.b = bf16[80,512]{1,0:T(8,128)(2,1)S(1)} collective-permute-done((bf16[80,512]{1,0:T(8,128)(2,1)S(1)}, bf16[80,512]{1,0:T(8,128)(2,1)S(1)}, u32[]{:S(2)}, u32[]{:S(2)}) %collective-permute-start.9) | collective-permute-done | bytes 81952 | tf_op jit(solution)/shard_map/ppermute | solution.py:62
  83.3 1.0 collective-permute-start.10
  84.3 2.0 %collective-permute-start.11 = (bf16[80,512]{1,0:T(8,128)(2,1)S(1)}, bf16[80,512]{1,0:T(8,128)(2,1)S(1)}, u32[]{:S(2)}, u32[]{:S(2)}) collective-permute-start(bf16[80,512]{1,0:T(8,128)(2,1)S(1)} %shard_map.138.own), channel_id=1, source_target_pairs={{0,16},{1,17},{2,18},{3,19},{4,6},{5,7},{6,4},{7,5},{8,24},{9,25},... | collective-permute-start | bytes 245768 | tf_op jit(solution)/shard_map/ppermute | solution.py:62
  87.0 0.9 collective-permute-done.10.r1
  87.9 1.3 %collective-permute-done.11.r2 = bf16[80,512]{1,0:T(8,128)(2,1)S(1)} collective-permute-done((bf16[80,512]{1,0:T(8,128)(2,1)S(1)}, bf16[80,512]{1,0:T(8,128)(2,1)S(1)}, u32[]{:S(2)}, u32[]{:S(2)}) %collective-permute-start.11) | collective-permute-done | bytes 81952 | tf_op jit(solution)/shard_map/ppermute | solution.py:62
  89.7 1.1 collective-permute-start.13
  90.8 2.2 %collective-permute-start.14 = (bf16[224,512]{1,0:T(8,128)(2,1)S(1)}, bf16[224,512]{1,0:T(8,128)(2,1)S(1)}, u32[]{:S(2)}, u32[]{:S(2)}) collective-permute-start(bf16[224,512]{1,0:T(8,128)(2,1)S(1)} %shard_map.139.own), channel_id=1, source_target_pairs={{0,2},{1,3},{2,0},{3,1},{4,20},{5,21},{6,22},{7,23},{8,10},{9,11},... | collective-permute-start | bytes 688136 | tf_op jit(solution)/shard_map/ppermute | solution.py:62
  93.5 3.2 %collective-permute-done.13.r1 = bf16[224,512]{1,0:T(8,128)(2,1)S(1)} collective-permute-done((bf16[224,512]{1,0:T(8,128)(2,1)S(1)}, bf16[224,512]{1,0:T(8,128)(2,1)S(1)}, u32[]{:S(2)}, u32[]{:S(2)}) %collective-permute-start.13) | collective-permute-done | bytes 229408 | tf_op jit(solution)/shard_map/ppermute | solution.py:62
  96.7 2.5 %collective-permute-done.14.r2 = bf16[224,512]{1,0:T(8,128)(2,1)S(1)} collective-permute-done((bf16[224,512]{1,0:T(8,128)(2,1)S(1)}, bf16[224,512]{1,0:T(8,128)(2,1)S(1)}, u32[]{:S(2)}, u32[]{:S(2)}) %collective-permute-start.14) | collective-permute-done | bytes 229408 | tf_op jit(solution)/shard_map/ppermute | solution.py:62
  99.8 8.0 %collective-permute-start.16 = (bf16[800,512]{1,0:T(8,128)(2,1)S(1)}, bf16[800,512]{1,0:T(8,128)(2,1)S(1)}, u32[]{:S(2)}, u32[]{:S(2)}) collective-permute-start(bf16[800,512]{1,0:T(8,128)(2,1)S(1)} %shard_map.140.own), channel_id=1, source_target_pairs={{0,4},{1,5},{2,6},{3,7},{4,0},{5,1},{6,2},{7,3},{8,12},{9,13},{10,... | collective-permute-start | bytes 2457608 | tf_op jit(solution)/shard_map/ppermute | solution.py:62
  108.5 2.0 %copy.15 = bf16[1,48,31,512]{3,1,2,0:T(8,128)(2,1)} copy(bf16[1,48,31,512]{3,2,1,0:T(8,128)(2,1)S(1)} %bitcast.17) | data formatting | bytes 3047424
  110.5 2.9 %shard_map.142 = (f32[1536,512]{1,0:T(8,128)}, f32[10,512]{1,0:T(8,128)}, f32[1,512]{1,0:T(1,128)}, f32[1,512]{1,0:T(1,128)}) custom-call(s32[3]{0:T(128)S(1)} %pad_add_fusion.pos, f32[768,512]{1,0:T(8,128)S(1)} %shard_map.141.ready, bf16[800,512]{1,0:T(8,128)(2,1)S(1)} %shard_map.140.own, bf16[800,512]{1,0:T(8,128)(2,1)S(1)} %collective-permute-done.16.got), custom_call_target="tpu_custom_call" | custom-call | tf_op jit(solution)/shard_map/pallas_call | solution.py:191
  (44 shorter events, 8.4 us)
Async XLA Ops:
  0.6 0.8 copy-start.2
  1.4 0.7 copy-start.5
  2.1 0.7 copy-start.6
  3.7 23.8 %all-to-all-start = ((bf16[64,2,384]{2,1,0:T(2,128)(2,1)}), bf16[64,2,384]{2,1,0:T(2,128)(2,1)}, u32[]{:S(2)}, u32[]{:S(2)}) async-start(bf16[64,2,384]{2,1,0:T(2,128)(2,1)} %reshape.19), calls=%async_computation | async-start | bytes 196608 | tf_op jit(solution)/shard_map/all_to_all | solution.py:481
  17.0 2.5 %copy-start.7 = (bf16[10,512]{1,0:T(8,128)(2,1)S(1)}, bf16[10,512]{1,0:T(8,128)(2,1)}, u32[]{:S(2)}) copy-start(bf16[10,512]{1,0:T(8,128)(2,1)} %param.12) | copy-start | bytes 30724
  17.1 11.4 %copy-start = (bf16[3,512,512]{2,1,0:T(8,128)(2,1)S(1)}, bf16[3,512,512]{2,1,0:T(8,128)(2,1)}, u32[]{:S(2)}) copy-start(bf16[3,512,512]{2,1,0:T(8,128)(2,1)} %weight.7) | copy-start | bytes 4718596
  17.1 11.4 %copy-start.3 = (f32[512]{0:T(512)S(1)}, f32[512]{0:T(512)}, u32[]{:S(2)}) copy-start(f32[512]{0:T(512)} %param.13) | copy-start | bytes 6148
  17.1 11.4 %copy-start.4 = (f32[512]{0:T(512)S(1)}, f32[512]{0:T(512)}, u32[]{:S(2)}) copy-start(f32[512]{0:T(512)} %param.14) | copy-start | bytes 6148
  28.5 0.9 copy-start.1
  49.2 3.1 %collective-permute-start = (bf16[768,512]{1,0:T(8,128)(2,1)S(1)}, bf16[768,512]{1,0:T(8,128)(2,1)S(1)}, u32[]{:S(2)}, u32[]{:S(2)}) collective-permute-start(bf16[768,512]{1,0:T(8,128)(2,1)S(1)} %get-tuple-element.35.before), channel_id=1, source_target_pairs={{0,4},{1,5},{2,6},{3,7},{4,0},{5,1},{6,2},{7,3},{8,12},{9,13},{10,... | collective-permute-start | bytes 2359304 | tf_op jit(solution)/shard_map/ppermute | solution.py:62
  53.0 8.2 %collective-permute-start.1 = (bf16[192,512]{1,0:T(8,128)(2,1)S(1)}, bf16[192,512]{1,0:T(8,128)(2,1)S(1)}, u32[]{:S(2)}, u32[]{:S(2)}) collective-permute-start(bf16[192,512]{1,0:T(8,128)(2,1)S(1)} %get-tuple-element.46), channel_id=1, source_target_pairs={{0,1},{1,2},{2,3},{3,0},{4,12},{5,13},{6,14},{7,15},{8,9},{9,10},{... | collective-permute-start | bytes 589832 | tf_op jit(solution)/shard_map/ppermute | solution.py:62
  53.3 7.9 %collective-permute-start.2 = (bf16[192,512]{1,0:T(8,128)(2,1)S(1)}, bf16[192,512]{1,0:T(8,128)(2,1)S(1)}, u32[]{:S(2)}, u32[]{:S(2)}) collective-permute-start(bf16[192,512]{1,0:T(8,128)(2,1)S(1)} %get-tuple-element.47), channel_id=1, source_target_pairs={{0,2},{1,3},{2,0},{3,1},{4,20},{5,21},{6,22},{7,23},{8,10},{9,11},... | collective-permute-start | bytes 589832 | tf_op jit(solution)/shard_map/ppermute | solution.py:62
  54.7 7.1 %collective-permute-start.3 = (bf16[192,512]{1,0:T(8,128)(2,1)S(1)}, bf16[192,512]{1,0:T(8,128)(2,1)S(1)}, u32[]{:S(2)}, u32[]{:S(2)}) collective-permute-start(bf16[192,512]{1,0:T(8,128)(2,1)S(1)} %get-tuple-element.48), channel_id=1, source_target_pairs={{0,3},{1,0},{2,1},{3,2},{4,28},{5,29},{6,30},{7,31},{8,11},{9,8},{... | collective-permute-start | bytes 589832 | tf_op jit(solution)/shard_map/ppermute | solution.py:62
  62.5 7.5 %collective-permute-start.4 = (bf16[48,512]{1,0:T(8,128)(2,1)S(1)}, bf16[48,512]{1,0:T(8,128)(2,1)S(1)}, u32[]{:S(2)}, u32[]{:S(2)}) collective-permute-start(bf16[48,512]{1,0:T(8,128)(2,1)S(1)} %get-tuple-element.50), channel_id=1, source_target_pairs={{0,8},{1,9},{2,10},{3,11},{4,5},{5,6},{6,7},{7,4},{8,16},{9,17},{1... | collective-permute-start | bytes 147464 | tf_op jit(solution)/shard_map/ppermute | solution.py:62
  63.8 6.2 %collective-permute-start.5 = (bf16[48,512]{1,0:T(8,128)(2,1)S(1)}, bf16[48,512]{1,0:T(8,128)(2,1)S(1)}, u32[]{:S(2)}, u32[]{:S(2)}) collective-permute-start(bf16[48,512]{1,0:T(8,128)(2,1)S(1)} %get-tuple-element.51), channel_id=1, source_target_pairs={{0,16},{1,17},{2,18},{3,19},{4,6},{5,7},{6,4},{7,5},{8,24},{9,25},... | collective-permute-start | bytes 147464 | tf_op jit(solution)/shard_map/ppermute | solution.py:62
  66.2 3.7 %collective-permute-start.6 = (bf16[48,512]{1,0:T(8,128)(2,1)S(1)}, bf16[48,512]{1,0:T(8,128)(2,1)S(1)}, u32[]{:S(2)}, u32[]{:S(2)}) collective-permute-start(bf16[48,512]{1,0:T(8,128)(2,1)S(1)} %get-tuple-element.52), channel_id=1, source_target_pairs={{0,24},{1,25},{2,26},{3,27},{4,7},{5,4},{6,5},{7,6},{8,0},{9,1},{1... | collective-permute-start | bytes 147464 | tf_op jit(solution)/shard_map/ppermute | solution.py:62
  70.0 3.4 %collective-permute-start.7 = (bf16[80,512]{1,0:T(8,128)(2,1)S(1)}, bf16[80,512]{1,0:T(8,128)(2,1)S(1)}, u32[]{:S(2)}, u32[]{:S(2)}) collective-permute-start(bf16[80,512]{1,0:T(8,128)(2,1)S(1)} %shard_map.135.a), channel_id=1, source_target_pairs={{0,32},{1,33},{2,34},{3,35},{4,36},{5,37},{6,38},{7,39},{8,40},{9,... | collective-permute-start | bytes 245768 | tf_op jit(solution)/shard_map/ppermute | solution.py:62
  73.4 5.2 %collective-permute-start.8 = (bf16[80,512]{1,0:T(8,128)(2,1)S(1)}, bf16[80,512]{1,0:T(8,128)(2,1)S(1)}, u32[]{:S(2)}, u32[]{:S(2)}) collective-permute-start(bf16[80,512]{1,0:T(8,128)(2,1)S(1)} %shard_map.136.a), channel_id=1, source_target_pairs={{0,96},{1,97},{2,98},{3,99},{4,100},{5,101},{6,102},{7,103},{8,104... | collective-permute-start | bytes 245768 | tf_op jit(solution)/shard_map/ppermute | solution.py:62
  78.7 4.6 %collective-permute-start.9 = (bf16[80,512]{1,0:T(8,128)(2,1)S(1)}, bf16[80,512]{1,0:T(8,128)(2,1)S(1)}, u32[]{:S(2)}, u32[]{:S(2)}) collective-permute-start(bf16[80,512]{1,0:T(8,128)(2,1)S(1)} %shard_map.137.a), channel_id=1, source_target_pairs={{0,224},{1,225},{2,226},{3,227},{4,228},{5,229},{6,230},{7,231},{8... | collective-permute-start | bytes 245768 | tf_op jit(solution)/shard_map/ppermute | solution.py:62
  83.3 4.6 %collective-permute-start.10 = (bf16[80,512]{1,0:T(8,128)(2,1)S(1)}, bf16[80,512]{1,0:T(8,128)(2,1)S(1)}, u32[]{:S(2)}, u32[]{:S(2)}) collective-permute-start(bf16[80,512]{1,0:T(8,128)(2,1)S(1)} %shard_map.138.own), channel_id=1, source_target_pairs={{0,8},{1,9},{2,10},{3,11},{4,5},{5,6},{6,7},{7,4},{8,16},{9,17},{1... | collective-permute-start | bytes 245768 | tf_op jit(solution)/shard_map/ppermute | solution.py:62
  84.3 4.8 %collective-permute-start.11 = (bf16[80,512]{1,0:T(8,128)(2,1)S(1)}, bf16[80,512]{1,0:T(8,128)(2,1)S(1)}, u32[]{:S(2)}, u32[]{:S(2)}) collective-permute-start(bf16[80,512]{1,0:T(8,128)(2,1)S(1)} %shard_map.138.own), channel_id=1, source_target_pairs={{0,16},{1,17},{2,18},{3,19},{4,6},{5,7},{6,4},{7,5},{8,24},{9,25},... | collective-permute-start | bytes 245768 | tf_op jit(solution)/shard_map/ppermute | solution.py:62
  86.4 3.3 %collective-permute-start.12 = (bf16[80,512]{1,0:T(8,128)(2,1)S(1)}, bf16[80,512]{1,0:T(8,128)(2,1)S(1)}, u32[]{:S(2)}, u32[]{:S(2)}) collective-permute-start(bf16[80,512]{1,0:T(8,128)(2,1)S(1)} %shard_map.138.own), channel_id=1, source_target_pairs={{0,24},{1,25},{2,26},{3,27},{4,7},{5,4},{6,5},{7,6},{8,0},{9,1},{1... | collective-permute-start | bytes 245768 | tf_op jit(solution)/shard_map/ppermute | solution.py:62
  89.7 7.0 %collective-permute-start.13 = (bf16[224,512]{1,0:T(8,128)(2,1)S(1)}, bf16[224,512]{1,0:T(8,128)(2,1)S(1)}, u32[]{:S(2)}, u32[]{:S(2)}) collective-permute-start(bf16[224,512]{1,0:T(8,128)(2,1)S(1)} %shard_map.139.own), channel_id=1, source_target_pairs={{0,1},{1,2},{2,3},{3,0},{4,12},{5,13},{6,14},{7,15},{8,9},{9,10},{... | collective-permute-start | bytes 688136 | tf_op jit(solution)/shard_map/ppermute | solution.py:62
  90.8 8.4 %collective-permute-start.14 = (bf16[224,512]{1,0:T(8,128)(2,1)S(1)}, bf16[224,512]{1,0:T(8,128)(2,1)S(1)}, u32[]{:S(2)}, u32[]{:S(2)}) collective-permute-start(bf16[224,512]{1,0:T(8,128)(2,1)S(1)} %shard_map.139.own), channel_id=1, source_target_pairs={{0,2},{1,3},{2,0},{3,1},{4,20},{5,21},{6,22},{7,23},{8,10},{9,11},... | collective-permute-start | bytes 688136 | tf_op jit(solution)/shard_map/ppermute | solution.py:62
  93.0 6.7 %collective-permute-start.15 = (bf16[224,512]{1,0:T(8,128)(2,1)S(1)}, bf16[224,512]{1,0:T(8,128)(2,1)S(1)}, u32[]{:S(2)}, u32[]{:S(2)}) collective-permute-start(bf16[224,512]{1,0:T(8,128)(2,1)S(1)} %shard_map.139.own), channel_id=1, source_target_pairs={{0,3},{1,0},{2,1},{3,2},{4,28},{5,29},{6,30},{7,31},{8,11},{9,8},{... | collective-permute-start | bytes 688136 | tf_op jit(solution)/shard_map/ppermute | solution.py:62
  99.8 10.6 %collective-permute-start.16 = (bf16[800,512]{1,0:T(8,128)(2,1)S(1)}, bf16[800,512]{1,0:T(8,128)(2,1)S(1)}, u32[]{:S(2)}, u32[]{:S(2)}) collective-permute-start(bf16[800,512]{1,0:T(8,128)(2,1)S(1)} %shard_map.140.own), channel_id=1, source_target_pairs={{0,4},{1,5},{2,6},{3,7},{4,0},{5,1},{6,2},{7,3},{8,12},{9,13},{10,... | collective-permute-start | bytes 2457608 | tf_op jit(solution)/shard_map/ppermute | solution.py:62

commit v3 on v2

--- a/solution.py
+++ b/solution.py
@@ -2,7 +2,6 @@
 
 import jax
 import jax.numpy as jnp
-import numpy as np
 from jax import lax
 from jax.experimental import pallas as pl
 from jax.experimental.pallas import tpu as pltpu
@@ -62,13 +61,12 @@
     return lax.ppermute(value, BOTH, perm)
 
 
-def k_scatter_one(pos, own, got, before, m1, m2, m3, keep):
-    a1, core = pos[0], pos[2]
+def k_scatter_one(pos, own, got, m1, m2, m3, keep):
+    a1 = pos[0]
     for k, out in ((0, None), (1, m1), (2, m2), (3, m3)):
         j = (a1 + k) & 3
-        mine = pl.ds(pl.multiple_of(core * 768 + j * 192, 192), 192)
-        theirs = pl.ds(pl.multiple_of(j * 192, 192), 192)
-        total = own[mine, :] + got[theirs, :].astype(F32)
+        rows = pl.ds(pl.multiple_of(j * 192, 192), 192)
+        total = own[rows, :] + got[rows, :].astype(F32)
         if out is None:
             keep[...] = total
         else:
@@ -127,27 +125,28 @@
         out[pl.ds((j1 * 4 + j2) * 48, 48), :] = ref[pl.ds(pl.multiple_of(at * 48, 16), 48), :].astype(F32)
 
 
-def k_order(pos, own, out):
-    for j1 in range(4):
-        order(own, out, j1, pos[0], pos[1])
-
-
-def k_final(pos, ready, own, got, full, conv0, gain, bias, rest, sems):
-    core = pos[2]
-    mine = pltpu.make_async_copy(ready, full.at[pl.ds(pl.multiple_of(core * 768, 768), 768), :], sems.at[0])
-    mine.start()
+def flush(core, out, rest, sems, ref, first, second):
     copies = []
     for j1 in range(4):
-        order(got, rest, j1, pos[1], pos[0])
-        at = pl.multiple_of((1 - core) * 768 + j1 * 192, 192)
-        copy = pltpu.make_async_copy(rest.at[pl.ds(j1 * 192, 192), :], full.at[pl.ds(at, 192), :], sems.at[1 + j1])
+        order(ref, rest, j1, first, second)
+        at = pl.multiple_of(core * 768 + j1 * 192, 192)
+        copy = pltpu.make_async_copy(rest.at[pl.ds(j1 * 192, 192), :], out.at[pl.ds(at, 192), :], sems.at[j1])
         copy.start()
         copies.append(copy)
+    return copies
+
+
+def k_early(pos, own, full, rest, sems):
+    for copy in flush(pos[2], full, rest, sems, own, pos[0], pos[1]):
+        copy.wait()
+
+
+def k_final(pos, own, got, half, full, conv0, gain, bias, rest, sems):
+    copies = flush(1 - pos[2], full, rest, sems, got, pos[1], pos[0])
     total = lift(own, 768) + lift(got, 768)
     conv0[...] = total[0:10]
     gain[...] = total[10:11]
     bias[...] = total[11:12]
-    mine.wait()
     for copy in copies:
         copy.wait()
 
@@ -160,22 +159,20 @@
     return jnp.stack([first, second, core]).astype(jnp.int32)
 
 
-def reduce_all(pos, own, other, backward, feats):
+def reduce_all(pos, other, mine, backward, feats):
     core, one, two, steps = perms()
     row = 512
     third = ((48, row), BF)
     got = send(other, core)
-    small = backward(0, jnp.zeros((16, row), F32), other)
-    m1, m2, m3, keep = call(
-        k_scatter_one, [((192, row), BF)] * 3 + [((192, row), F32)], [own, got], pos, after=[small]
-    )
+    own = mine(other)
+    m1, m2, m3, keep = call(k_scatter_one, [((192, row), BF)] * 3 + [((192, row), F32)], [own, got], pos)
     r = [send(m, p) for m, p in zip((m1, m2, m3), one)]
-    small = backward(1, small, keep)
+    small = backward(0, 4, jnp.zeros((16, row), F32), keep)
     m1, m2, m3, keep2 = call(
         k_scatter_two, [third] * 3 + [((48, row), F32)], [keep, *r], pos, after=[small]
     )
     r = [send(m, p) for m, p in zip((m1, m2, m3), two)]
-    small = backward(2, small, keep2)
+    small = backward(4, 2, small, keep2)
     (a,) = call(k_sum_two, [((80, row), BF)], [keep2, *r, small])
     for step in steps:
         b = send(a, step)
@@ -187,15 +184,21 @@
     a, feats, *r = lax.optimization_barrier((a, feats, *r))
     (a,) = call(k_join_one, [((800, row), BF)], [a, *r])
     got = send(a, core)
-    (ready,) = call(k_order, [((768, row), F32)], [a], pos)
+    room = [pltpu.VMEM((768, row), F32), pltpu.SemaphoreType.DMA((4,))]
+    grant = pltpu.CompilerParams(vmem_limit_bytes=20 << 20)
+    whole = jax.ShapeDtypeStruct((1536, row), F32)
+    half = pl.pallas_call(
+        k_early, out_shape=whole, in_specs=[SM, VM], out_specs=ANY, scratch_shapes=room, compiler_params=grant
+    )(pos, a)
     full, conv0, gain, bias = pl.pallas_call(
         k_final,
-        out_shape=[jax.ShapeDtypeStruct((n, row), F32) for n in (1536, 10, 1, 1)],
-        in_specs=[SM, VM, VM, VM],
+        out_shape=[whole] + [jax.ShapeDtypeStruct((n, row), F32) for n in (10, 1, 1)],
+        in_specs=[SM, VM, VM, ANY],
         out_specs=[ANY, VM, VM, VM],
-        scratch_shapes=[pltpu.VMEM((768, row), F32), pltpu.SemaphoreType.DMA((5,))],
-        compiler_params=pltpu.CompilerParams(vmem_limit_bytes=20 << 20),
-    )(pos, ready, a, got)
+        scratch_shapes=room,
+        input_output_aliases={3: 0},
+        compiler_params=grant,
+    )(pos, a, got, half)
     return full, conv0, gain[0], bias[0], jnp.transpose(feats, (1, 0, 2))
 
 
@@ -247,6 +250,27 @@
 ROWS = 32 * BLOCK
 
 
+def k_taps(conv0, weo):
+    taps = jnp.concatenate([conv0[...].astype(F32), jnp.zeros((6, 512), F32)], axis=0).astype(BF)
+    weo[...] = jnp.zeros(weo.shape, BF)
+    weo[pl.ds(0, 16), pl.ds(0, 512)] = taps
+    weo[pl.ds(16, 16), pl.ds(512, 512)] = taps
+
+
+def tables(fold, window):
+    sample = lax.broadcasted_iota(jnp.int32, (WIDE, 128), 0).astype(F32)
+    lane = lax.broadcasted_iota(jnp.int32, (WIDE, 128), 1).astype(F32)
+    tens = jnp.floor((sample + 0.5) * 0.1) * 10.0
+    fold[pl.ds(0, WIDE), :] = jnp.where((sample < SAMPLES) & (sample - tens == lane), 1.0, 0.0).astype(BF)
+    tens = jnp.floor((sample - 4.5) * 0.1) * 10.0
+    odd = (sample < SAMPLES) & (sample >= 5.0) & (sample - 5.0 - tens + 16.0 == lane)
+    fold[pl.ds(WIDE, WIDE), :] = jnp.where(odd, 1.0, 0.0).astype(BF)
+    step = lax.broadcasted_iota(jnp.int32, (32, WIDE), 0) * 10
+    at = lax.broadcasted_iota(jnp.int32, (32, WIDE), 1)
+    window[:, pl.ds(0, WIDE)] = jnp.where((at >= step) & (at < step + 10), 1.0, 0.0)
+    window[:, pl.ds(WIDE, WIDE)] = jnp.where((at >= step + 5) & (at < step + 15), 1.0, 0.0)
+
+
 def tall(rows):
     return jnp.concatenate([rows] * 4, axis=0)
 
@@ -260,11 +284,12 @@
 
 
 def k_forward(
-    scale, pos, arrived, fold, weo, gain, bias, weight, fgrad,
-    feats, g, gs, se, so, ne, no, istd, valid, x, full, other,
-    panels, window, am, pre, he, ho, hs, pre1,
+    scale, pos, arrived, weo, gain, bias, weight, fgrad,
+    feats, g, gs, se, so, ne, no, istd, valid, x, he, ho, other,
+    fold, window, panels, am, pre, hs, pre1,
 ):
     spans = panels.shape[0]
+    tables(fold, window)
     arr = arrived[...]
     lane = lax.broadcasted_iota(jnp.int32, (128, 128), 1).astype(F32)
     meta = arr[:, 256:384].astype(F32)
@@ -275,10 +300,6 @@
     length = moved[:, SAMPLES + 1 : SAMPLES + 2] + 214.0
     count = jnp.broadcast_to(jnp.floor((length - 9.5) * 0.2) + 1.0, (spans, 128))
     valid[...] = jnp.broadcast_to(count[:, None, :], valid.shape)
-    step = lax.broadcasted_iota(jnp.int32, (32, WIDE), 0) * 10
-    sample = lax.broadcasted_iota(jnp.int32, (32, WIDE), 1)
-    window[:, pl.ds(0, WIDE)] = jnp.where((sample >= step) & (sample < step + 10), 1.0, 0.0)
-    window[:, pl.ds(WIDE, WIDE)] = jnp.where((sample >= step + 5) & (sample < step + 15), 1.0, 0.0)
     frame = lax.broadcasted_iota(jnp.int32, (32, 128), 0).astype(F32)
 
     def block(b, carry):
@@ -362,23 +383,35 @@
         return carry
 
     lax.fori_loop(0, spans // BLOCK, block, 0)
-    full[pl.ds(0, 512), :] = dot_t(he[...], g[...])
-    full[pl.ds(512, 512), :] = dot_t(ho[...], g[...])
-    full[pl.ds(1024, 512), :] = dot_t(he[...], gs[...])
-    away = pl.ds(pl.multiple_of((1 - pos[2]) * 768, 768), 768)
-    other[...] = full[away, :].astype(BF)
+    half_of(1 - pos[2], he, ho, g, gs, other)
+
+
+def half_of(half, he, ho, g, gs, out):
+    @pl.when(half == 0)
+    def _():
+        out[pl.ds(0, 512), :] = dot_t(he[...], g[...]).astype(out.dtype)
+        out[pl.ds(512, 256), :] = dot_t(ho[:, pl.ds(0, 256)], g[...]).astype(out.dtype)
+
+    @pl.when(half == 1)
+    def _():
+        out[pl.ds(0, 256), :] = dot_t(ho[:, pl.ds(256, 256)], g[...]).astype(out.dtype)
+        out[pl.ds(256, 512), :] = dot_t(he[...], gs[...]).astype(out.dtype)
+
+
+def k_half(pos, he, ho, g, gs, before, out):
+    half_of(pos[2], he, ho, g, gs, out)
 
 
 def k_backward(
-    step, g, gs, se, so, ne, no, istd, valid, x, gain, weight, start, before, small,
+    first, g, gs, se, so, ne, no, istd, valid, x, gain, weight, start, before, small,
     de, do, dxe, dxo, sums,
 ):
     blocks = dxe.shape[0] // ROWS
     sums[...] = jnp.zeros(sums.shape, F32)
 
     def block(b, carry):
-        base = (step * blocks + b) * BLOCK
-        every = pl.ds(pl.multiple_of((step * blocks + b) * ROWS, ROWS), ROWS)
+        base = (first + b) * BLOCK
+        every = pl.ds(pl.multiple_of((first + b) * ROWS, ROWS), ROWS)
         de[...] = dot_nt(g[every, :], weight[0]) + dot_nt(gs[every, :], weight[2])
         do[...] = dot_nt(g[every, :], weight[1])
 
@@ -407,59 +440,45 @@
         return carry
 
     lax.fori_loop(0, blocks, block, 0)
-    part = x[pl.ds(step * blocks * ROWS, blocks * ROWS), :]
+    part = x[pl.ds(first * ROWS, blocks * ROWS), :]
     small[...] = start[...] + dot_t(part, dxe[...])[0:16] + dot_t(part, dxo[...])[16:32]
     small[pl.ds(10, 2), :] += sums[pl.ds(0, 2), :]
-
-
-def folding():
-    table = np.zeros((2 * WIDE, 128), np.float32)
-    for s in range(SAMPLES):
-        table[s, s % 10] = 1.0
-        if s >= 5:
-            table[WIDE + s, 16 + (s - 5) % 10] = 1.0
-    return jnp.asarray(table, BF)
 
 
 def encode(pos, arrived, conv0_weight, norm_gain, norm_bias, conv1_weight, feature_grad, scale):
     spans = feature_grad.shape[0]
     rows = spans * 32
-    zero = jnp.zeros
-    weo = jnp.concatenate(
-        [
-            jnp.concatenate([conv0_weight, zero((6, 512), BF), zero((16, 512), BF)], axis=0),
-            jnp.concatenate([zero((16, 512), BF), conv0_weight, zero((6, 512), BF)], axis=0),
-        ],
-        axis=1,
-    )
-    weo = jnp.concatenate([weo, zero((96, 1024), BF)], axis=0)
+    (weo,) = call(k_taps, [((128, 1024), BF)], [conv0_weight])
     gain, bias = norm_gain[None], norm_bias[None]
     wide = ((rows, 512), BF)
-    feats, g, gs, se, so, ne, no, istd, valid, x, full, other = call(
+    feats, g, gs, se, so, ne, no, istd, valid, x, he, ho, other = call(
         functools.partial(k_forward, scale),
         [
             (feature_grad.shape, BF), wide, wide, wide, wide, wide, wide,
-            ((spans, 8, 512), F32), ((spans, 8, 128), F32), ((rows, 128), BF), ((1536, 512), F32), ((768, 512), BF),
+            ((spans, 8, 512), F32), ((spans, 8, 128), F32), ((rows, 128), BF), wide, wide, ((768, 512), BF),
         ],
-        [arrived, folding(), weo, gain, bias, conv1_weight, feature_grad],
+        [arrived, weo, gain, bias, conv1_weight, feature_grad],
         pos,
         scratch=[
-            ((spans, 8, WIDE), F32), ((32, 2 * WIDE), F32), ((ROWS, 2 * WIDE), BF), ((ROWS, 1024), F32),
-            ((rows, 512), BF), ((rows, 512), BF), ((ROWS, 512), BF), ((ROWS, 512), F32),
+            ((2 * WIDE, 128), BF), ((32, 2 * WIDE), F32), ((spans, 8, WIDE), F32), ((ROWS, 2 * WIDE), BF), ((ROWS, 1024), F32),
+            ((ROWS, 512), BF), ((ROWS, 512), F32),
         ],
     )
 
-    def backward(step, small, before):
-        part = (rows // 3, 512)
+    def mine(before):
+        return call(k_half, [((768, 512), F32)], [he, ho, g, gs], pos, after=[before])[0]
+
+    def backward(first, blocks, small, before):
+        part = (ROWS * blocks, 512)
         return call(
-            functools.partial(k_backward, step),
+            functools.partial(k_backward, first),
             [((16, 512), F32)],
             [g, gs, se, so, ne, no, istd, valid, x, gain, conv1_weight, small],
             scratch=[((ROWS, 512), F32), ((ROWS, 512), F32), (part, BF), (part, BF), ((8, 512), F32)],
             after=[before],
         )[0]
 
-    return feats, full, other, backward
+    return feats, other, mine, backward
 
 
 def body(waveform, lengths, target, conv0_weight, norm_gain, norm_bias, conv1_weight, feature_grad):
@@ -477,14 +496,15 @@
         ],
         after=[waveform[0], lengths, target],
         late=HBM,
+        limit=60,
     )
     arrived = lax.all_to_all(packed.reshape(devices, 2, WIDE), "dp", split_axis=0, concat_axis=0, tiled=True)
     arrived = arrived.reshape(2 * devices, WIDE)
     scale = 1.0 / float(lax.axis_size("rep") * devices * spans * frames) ** 0.5
-    feats, full, other, backward = encode(
+    feats, other, mine, backward = encode(
         pos, arrived, conv0_weight, norm_gain, norm_bias, conv1_weight, feature_grad[0], scale
     )
-    full, conv0, gain, bias, feats = reduce_all(pos, full, other, backward, feats)
+    full, conv0, gain, bias, feats = reduce_all(pos, other, mine, backward, feats)
     return (feats[None], conv0, gain, bias, full.reshape(conv1_weight.shape))
 
 

time: 114 us -> 114 us (level)
  Pallas kernels: 32.9 us -> 35.6 us
  local copies, waits for them, and re-layouts: 8.98 us -> 6.87 us
  waiting for transfers between devices: 31.3 us -> 29.6 us
    unnamed x18 -> x10, local copies, waits for them, and re-layouts: 7.36 us -> 4.36 us
    ppermute x17, waiting for transfers between devices: 23.3 us -> 21.6 us  [send(): return lax.ppermute(value, BOTH, perm)]
    pallas_call x14, Pallas kernels: 30.1 us -> 31.5 us  [call(): pl.pallas_call(kernel, out_shape=shapes, in_specs=specs, out_specs=[VM] *...]
    pallas_call x1 -> x2, Pallas kernels: 2.86 us -> 4.1 us  [the longest x1 2.36 us: reduce_all(): pl.pallas_call(k_final, out_shape=[whole] + [jax.ShapeDtypeStruct((n, row...]
  transfers between devices with their start and end apart: 18 -> 18, of which waited for: 12 -> 11; matrix products, arithmetic and copies ran while one was open for 4% -> 4% of each run, Pallas kernels for 7% -> 10%
where the time goes in v3:
time: 114 us; the launch traced here: 113 us
  starting transfers between devices  39.5 us (35%)
  Pallas kernels  35.6 us (31%)
  waiting for transfers between devices  29.6 us (26%)
  local copies, waits for them, and re-layouts  6.87 us (6%)
    pallas_call x14, Pallas kernels, call(): pl.pallas_call(kernel, out_shape=shapes, in_specs=specs, out_specs=[VM] *...  31.5 us
    ppermute x17, starting transfers between devices, send(): return lax.ppermute(value, BOTH, perm)  26.2 us
    ppermute x17, waiting for transfers between devices, send(): return lax.ppermute(value, BOTH, perm)  21.6 us
    all_to_all x1, starting transfers between devices, body(): lax.all_to_all(packed.reshape(devices, 2, WIDE), 'dp', split_axis=0, conc...  13.3 us
    all_to_all x1, waiting for transfers between devices, body(): lax.all_to_all(packed.reshape(devices, 2, WIDE), 'dp', split_axis=0, conc...  7.96 us
    unnamed x10, local copies, waits for them, and re-layouts  4.36 us
    pallas_call x1, Pallas kernels, reduce_all(): pl.pallas_call(k_final, out_shape=[whole] + [jax.ShapeDtypeStruct((n, row...  2.36 us
  transfers between devices with their start and end apart: 18, of which 11 were waited for; matrix products, arithmetic and copies ran while one was open for 4% of the time, Pallas kernels for 10%

profile of v3, /device:TPU:1, one launch (start us, length us, event | category | flops | bytes accessed | tf_op | source)
XLA Modules:
  0.0 112.7 jit_solution(13703168471553462251)
XLA Ops:
  0.6 1.7 %shard_map.119 = bf16[128,384]{1,0:T(8,128)(2,1)} custom-call(bf16[48,320]{1,0:T(8,128)(2,1)} %bitcast.23, s32[1,48]{1,0:T(1,128)} %length_in.1, s32[1,48]{1,0:T(1,128)} %target_in.1), custom_call_target="tpu_custom_call" | custom-call | tf_op jit(solution)/shard_map/pallas_call | solution.py:26
  2.3 1.6 %reshape.19 = bf16[64,2,384]{2,1,0:T(2,128)(2,1)} reshape(bf16[128,384]{1,0:T(8,128)(2,1)} %shard_map.119) | data formatting | bytes 196608 | tf_op jit(solution)/shard_map/reshape | solution.py:501
  3.9 13.3 %all-to-all-start = ((bf16[64,2,384]{2,1,0:T(2,128)(2,1)}), bf16[64,2,384]{2,1,0:T(2,128)(2,1)}, u32[]{:S(2)}, u32[]{:S(2)}) async-start(bf16[64,2,384]{2,1,0:T(2,128)(2,1)} %reshape.19), calls=%async_computation | async-start | bytes 196608 | tf_op jit(solution)/shard_map/all_to_all | solution.py:501
  17.3 2.3 %copy.17 = bf16[1,48,31,512]{3,2,1,0:T(8,128)(2,1)S(1)} copy(bf16[1,48,31,512]{3,1,2,0:T(8,128)(2,1)} %param.15) | data formatting | bytes 3047424 | tf_op args[7]
  19.8 8.0 %all-to-all-done = bf16[64,2,384]{2,1,0:T(2,128)(2,1)} async-done(((bf16[64,2,384]{2,1,0:T(2,128)(2,1)}), bf16[64,2,384]{2,1,0:T(2,128)(2,1)}, u32[]{:S(2)}, u32[]{:S(2)}) %all-to-all-start) | async-done | bytes 98336 | tf_op jit(solution)/shard_map/all_to_all | solution.py:501
  27.7 0.9 reshape.20.arrived
  28.7 18.7 %shard_map.121 = (bf16[48,31,512]{2,1,0:T(8,128)(2,1)S(1)}, bf16[1536,512]{1,0:T(8,128)(2,1)S(1)}, bf16[1536,512]{1,0:T(8,128)(2,1)S(1)}, bf16[1536,512]{1,0:T(8...) custom-call(s32[3]{0:T(128)S(1)} %pad_add_fusion.pos, ...), custom_call_target="tpu_custom_call" | custom-call | tf_op jit(solution)/shard_map/pallas_call | solution.py:26
  47.9 2.0 %shard_map.122.own = f32[768,512]{1,0:T(8,128)S(1)} custom-call(s32[3]{0:T(128)S(1)} %pad_add_fusion.pos, bf16[1536,512]{1,0:T(8,128)(2,1)S(1)} %get-tuple-element.35.he, bf16[1536,512]{1,0:T(8,128)(2,1)S(1)} %get-tuple-element.36.ho, bf16[1536,512]{1,0:T(8,128)(2,1)S(1)} %get-tuple-element.37.g, bf16[1536,512]{1,0:T(8,128)(2,1)S(1)} %get-tuple-element.38.gs, ...), custom_call_target="tpu_custom_call" | custom-call | tf_op jit(solution)/shard_map/pallas_call | solution.py:26
  49.9 0.7 shard_map.123
  50.9 1.4 %collective-permute-start.2 = (bf16[192,512]{1,0:T(8,128)(2,1)S(1)}, bf16[192,512]{1,0:T(8,128)(2,1)S(1)}, u32[]{:S(2)}, u32[]{:S(2)}) collective-permute-start(bf16[192,512]{1,0:T(8,128)(2,1)S(1)} %get-tuple-element.42), channel_id=1, source_target_pairs={{0,2},{1,3},{2,0},{3,1},{4,20},{5,21},{6,22},{7,23},{8,10},{9,11},... | collective-permute-start | bytes 589832 | tf_op jit(solution)/shard_map/ppermute | solution.py:61
  52.3 1.6 %collective-permute-start.3 = (bf16[192,512]{1,0:T(8,128)(2,1)S(1)}, bf16[192,512]{1,0:T(8,128)(2,1)S(1)}, u32[]{:S(2)}, u32[]{:S(2)}) collective-permute-start(bf16[192,512]{1,0:T(8,128)(2,1)S(1)} %get-tuple-element.43), channel_id=1, source_target_pairs={{0,3},{1,0},{2,1},{3,2},{4,28},{5,29},{6,30},{7,31},{8,11},{9,8},{... | collective-permute-start | bytes 589832 | tf_op jit(solution)/shard_map/ppermute | solution.py:61
  53.8 5.0 %shard_map.124.before.start = f32[16,512]{1,0:T(8,128)S(1)} custom-call(bf16[1536,512]{1,0:T(8,128)(2,1)S(1)} %get-tuple-element.37.g, bf16[1536,512]{1,0:T(8,128)(2,1)S(1)} %get-tuple-element.38.gs, bf16[1536,512]{1,0:T(8,128)(2,1)S(1)} %get-tuple-element.44.se, bf16[1536,512]{1,0:T(8,128)(2,1)S(1)} %get-tuple-element.45.so, ...), custom_call_target="tpu_custom_call" | custom-call | tf_op jit(solution)/shard_map/pallas_call | solution.py:26
  60.0 1.3 %collective-permute-start.4 = (bf16[48,512]{1,0:T(8,128)(2,1)S(1)}, bf16[48,512]{1,0:T(8,128)(2,1)S(1)}, u32[]{:S(2)}, u32[]{:S(2)}) collective-permute-start(bf16[48,512]{1,0:T(8,128)(2,1)S(1)} %get-tuple-element.52), channel_id=1, source_target_pairs={{0,8},{1,9},{2,10},{3,11},{4,5},{5,6},{6,7},{7,4},{8,16},{9,17},{1... | collective-permute-start | bytes 147464 | tf_op jit(solution)/shard_map/ppermute | solution.py:61
  61.3 2.5 %collective-permute-start.5 = (bf16[48,512]{1,0:T(8,128)(2,1)S(1)}, bf16[48,512]{1,0:T(8,128)(2,1)S(1)}, u32[]{:S(2)}, u32[]{:S(2)}) collective-permute-start(bf16[48,512]{1,0:T(8,128)(2,1)S(1)} %get-tuple-element.53), channel_id=1, source_target_pairs={{0,16},{1,17},{2,18},{3,19},{4,6},{5,7},{6,4},{7,5},{8,24},{9,25},... | collective-permute-start | bytes 147464 | tf_op jit(solution)/shard_map/ppermute | solution.py:61
  63.8 1.1 %collective-permute-start.6 = (bf16[48,512]{1,0:T(8,128)(2,1)S(1)}, bf16[48,512]{1,0:T(8,128)(2,1)S(1)}, u32[]{:S(2)}, u32[]{:S(2)}) collective-permute-start(bf16[48,512]{1,0:T(8,128)(2,1)S(1)} %get-tuple-element.54), channel_id=1, source_target_pairs={{0,24},{1,25},{2,26},{3,27},{4,7},{5,4},{6,5},{7,6},{8,0},{9,1},{1... | collective-permute-start | bytes 147464 | tf_op jit(solution)/shard_map/ppermute | solution.py:61
  64.9 2.6 %shard_map.126.small = f32[16,512]{1,0:T(8,128)S(1)} custom-call(bf16[1536,512]{1,0:T(8,128)(2,1)S(1)} %get-tuple-element.37.g, bf16[1536,512]{1,0:T(8,128)(2,1)S(1)} %get-tuple-element.38.gs, bf16[1536,512]{1,0:T(8,128)(2,1)S(1)} %get-tuple-element.44.se, bf16[1536,512]{1,0:T(8,128)(2,1)S(1)} %get-tuple-element.45.so, ...), custom_call_target="tpu_custom_call" | custom-call | tf_op jit(solution)/shard_map/pallas_call | solution.py:26
  68.0 3.0 %collective-permute-done.7.b = bf16[80,512]{1,0:T(8,128)(2,1)S(1)} collective-permute-done((bf16[80,512]{1,0:T(8,128)(2,1)S(1)}, bf16[80,512]{1,0:T(8,128)(2,1)S(1)}, u32[]{:S(2)}, u32[]{:S(2)}) %collective-permute-start.7) | collective-permute-done | bytes 81952 | tf_op jit(solution)/shard_map/ppermute | solution.py:61
  71.0 0.8 collective-permute-start.8
  71.9 4.3 %collective-permute-done.8.b = bf16[80,512]{1,0:T(8,128)(2,1)S(1)} collective-permute-done((bf16[80,512]{1,0:T(8,128)(2,1)S(1)}, bf16[80,512]{1,0:T(8,128)(2,1)S(1)}, u32[]{:S(2)}, u32[]{:S(2)}) %collective-permute-start.8) | collective-permute-done | bytes 81952 | tf_op jit(solution)/shard_map/ppermute | solution.py:61
  76.7 4.5 %collective-permute-done.9.b = bf16[80,512]{1,0:T(8,128)(2,1)S(1)} collective-permute-done((bf16[80,512]{1,0:T(8,128)(2,1)S(1)}, bf16[80,512]{1,0:T(8,128)(2,1)S(1)}, u32[]{:S(2)}, u32[]{:S(2)}) %collective-permute-start.9) | collective-permute-done | bytes 81952 | tf_op jit(solution)/shard_map/ppermute | solution.py:61
  81.2 0.8 collective-permute-start.10
  82.0 2.0 %collective-permute-start.11 = (bf16[80,512]{1,0:T(8,128)(2,1)S(1)}, bf16[80,512]{1,0:T(8,128)(2,1)S(1)}, u32[]{:S(2)}, u32[]{:S(2)}) collective-permute-start(bf16[80,512]{1,0:T(8,128)(2,1)S(1)} %shard_map.130.own), channel_id=1, source_target_pairs={{0,16},{1,17},{2,18},{3,19},{4,6},{5,7},{6,4},{7,5},{8,24},{9,25},... | collective-permute-start | bytes 245768 | tf_op jit(solution)/shard_map/ppermute | solution.py:61
  84.5 1.3 %collective-permute-done.10.r1 = bf16[80,512]{1,0:T(8,128)(2,1)S(1)} collective-permute-done((bf16[80,512]{1,0:T(8,128)(2,1)S(1)}, bf16[80,512]{1,0:T(8,128)(2,1)S(1)}, u32[]{:S(2)}, u32[]{:S(2)}) %collective-permute-start.10) | collective-permute-done | bytes 81952 | tf_op jit(solution)/shard_map/ppermute | solution.py:61
  85.8 1.0 collective-permute-done.11.r2
  87.4 1.1 collective-permute-start.13
  88.4 2.3 %collective-permute-start.14 = (bf16[224,512]{1,0:T(8,128)(2,1)S(1)}, bf16[224,512]{1,0:T(8,128)(2,1)S(1)}, u32[]{:S(2)}, u32[]{:S(2)}) collective-permute-start(bf16[224,512]{1,0:T(8,128)(2,1)S(1)} %shard_map.131.own), channel_id=1, source_target_pairs={{0,2},{1,3},{2,0},{3,1},{4,20},{5,21},{6,22},{7,23},{8,10},{9,11},... | collective-permute-start | bytes 688136 | tf_op jit(solution)/shard_map/ppermute | solution.py:61
  91.3 3.1 %collective-permute-done.13.r1 = bf16[224,512]{1,0:T(8,128)(2,1)S(1)} collective-permute-done((bf16[224,512]{1,0:T(8,128)(2,1)S(1)}, bf16[224,512]{1,0:T(8,128)(2,1)S(1)}, u32[]{:S(2)}, u32[]{:S(2)}) %collective-permute-start.13) | collective-permute-done | bytes 229408 | tf_op jit(solution)/shard_map/ppermute | solution.py:61
  94.4 3.2 %collective-permute-done.14.r2 = bf16[224,512]{1,0:T(8,128)(2,1)S(1)} collective-permute-done((bf16[224,512]{1,0:T(8,128)(2,1)S(1)}, bf16[224,512]{1,0:T(8,128)(2,1)S(1)}, u32[]{:S(2)}, u32[]{:S(2)}) %collective-permute-start.14) | collective-permute-done | bytes 229408 | tf_op jit(solution)/shard_map/ppermute | solution.py:61
  97.8 8.7 %collective-permute-start.16 = (bf16[800,512]{1,0:T(8,128)(2,1)S(1)}, bf16[800,512]{1,0:T(8,128)(2,1)S(1)}, u32[]{:S(2)}, u32[]{:S(2)}) collective-permute-start(bf16[800,512]{1,0:T(8,128)(2,1)S(1)} %shard_map.132.own), channel_id=1, source_target_pairs={{0,4},{1,5},{2,6},{3,7},{4,0},{5,1},{6,2},{7,3},{8,12},{9,13},{10,... | collective-permute-start | bytes 2457608 | tf_op jit(solution)/shard_map/ppermute | solution.py:61
  106.5 1.7 %shard_map.133.half = f32[1536,512]{1,0:T(8,128)} custom-call(s32[3]{0:T(128)S(1)} %pad_add_fusion.pos, bf16[800,512]{1,0:T(8,128)(2,1)S(1)} %shard_map.132.own), custom_call_target="tpu_custom_call" | custom-call | tf_op jit(solution)/shard_map/pallas_call | solution.py:190
  108.2 2.0 %copy.15 = bf16[1,48,31,512]{3,1,2,0:T(8,128)(2,1)} copy(bf16[1,48,31,512]{3,2,1,0:T(8,128)(2,1)S(1)} %bitcast.17) | data formatting | bytes 3047424
  110.2 2.4 %shard_map.134 = (f32[1536,512]{1,0:T(8,128)}, f32[10,512]{1,0:T(8,128)}, f32[1,512]{1,0:T(1,128)}, f32[1,512]{1,0:T(1,128)}) custom-call(s32[3]{0:T(128)S(1)} %pad_add_fusion.pos, bf16[800,512]{1,0:T(8,128)(2,1)S(1)} %shard_map.132.own, bf16[800,512]{1,0:T(8,128)(2,1)S(1)} %collective-permute-done.16.got, ...), custom_call_target="tpu_custom_call", output_to_operand_aliasing={{0}: (3, {})} | custom-call | tf_op jit(solution)/shard_map/pallas_call | solution.py:193
  (34 shorter events, 4.8 us)
Async XLA Ops:
  3.9 23.8 %all-to-all-start = ((bf16[64,2,384]{2,1,0:T(2,128)(2,1)}), bf16[64,2,384]{2,1,0:T(2,128)(2,1)}, u32[]{:S(2)}, u32[]{:S(2)}) async-start(bf16[64,2,384]{2,1,0:T(2,128)(2,1)} %reshape.19), calls=%async_computation | async-start | bytes 196608 | tf_op jit(solution)/shard_map/all_to_all | solution.py:501
  17.2 2.4 %copy-start.2 = (bf16[10,512]{1,0:T(8,128)(2,1)S(1)}, bf16[10,512]{1,0:T(8,128)(2,1)}, u32[]{:S(2)}) copy-start(bf16[10,512]{1,0:T(8,128)(2,1)} %conv0.1) | copy-start | bytes 30724
  17.3 11.4 %copy-start = (bf16[3,512,512]{2,1,0:T(8,128)(2,1)S(1)}, bf16[3,512,512]{2,1,0:T(8,128)(2,1)}, u32[]{:S(2)}) copy-start(bf16[3,512,512]{2,1,0:T(8,128)(2,1)} %weight.5) | copy-start | bytes 4718596
  17.3 11.4 %copy-start.1 = (f32[512]{0:T(512)S(1)}, f32[512]{0:T(512)}, u32[]{:S(2)}) copy-start(f32[512]{0:T(512)} %param.12) | copy-start | bytes 6148
  17.3 11.4 %copy-start.3 = (f32[512]{0:T(512)S(1)}, f32[512]{0:T(512)}, u32[]{:S(2)}) copy-start(f32[512]{0:T(512)} %param.13) | copy-start | bytes 6148
  47.4 2.4 %collective-permute-start = (bf16[768,512]{1,0:T(8,128)(2,1)S(1)}, bf16[768,512]{1,0:T(8,128)(2,1)S(1)}, u32[]{:S(2)}, u32[]{:S(2)}) collective-permute-start(bf16[768,512]{1,0:T(8,128)(2,1)S(1)} %get-tuple-element.39.before), channel_id=1, source_target_pairs={{0,4},{1,5},{2,6},{3,7},{4,0},{5,1},{6,2},{7,3},{8,12},{9,13},{10,... | collective-permute-start | bytes 2359304 | tf_op jit(solution)/shard_map/ppermute | solution.py:61
  50.6 8.3 %collective-permute-start.1 = (bf16[192,512]{1,0:T(8,128)(2,1)S(1)}, bf16[192,512]{1,0:T(8,128)(2,1)S(1)}, u32[]{:S(2)}, u32[]{:S(2)}) collective-permute-start(bf16[192,512]{1,0:T(8,128)(2,1)S(1)} %get-tuple-element.41), channel_id=1, source_target_pairs={{0,1},{1,2},{2,3},{3,0},{4,12},{5,13},{6,14},{7,15},{8,9},{9,10},{... | collective-permute-start | bytes 589832 | tf_op jit(solution)/shard_map/ppermute | solution.py:61
  50.9 8.0 %collective-permute-start.2 = (bf16[192,512]{1,0:T(8,128)(2,1)S(1)}, bf16[192,512]{1,0:T(8,128)(2,1)S(1)}, u32[]{:S(2)}, u32[]{:S(2)}) collective-permute-start(bf16[192,512]{1,0:T(8,128)(2,1)S(1)} %get-tuple-element.42), channel_id=1, source_target_pairs={{0,2},{1,3},{2,0},{3,1},{4,20},{5,21},{6,22},{7,23},{8,10},{9,11},... | collective-permute-start | bytes 589832 | tf_op jit(solution)/shard_map/ppermute | solution.py:61
  52.3 7.1 %collective-permute-start.3 = (bf16[192,512]{1,0:T(8,128)(2,1)S(1)}, bf16[192,512]{1,0:T(8,128)(2,1)S(1)}, u32[]{:S(2)}, u32[]{:S(2)}) collective-permute-start(bf16[192,512]{1,0:T(8,128)(2,1)S(1)} %get-tuple-element.43), channel_id=1, source_target_pairs={{0,3},{1,0},{2,1},{3,2},{4,28},{5,29},{6,30},{7,31},{8,11},{9,8},{... | collective-permute-start | bytes 589832 | tf_op jit(solution)/shard_map/ppermute | solution.py:61
  60.0 7.5 %collective-permute-start.4 = (bf16[48,512]{1,0:T(8,128)(2,1)S(1)}, bf16[48,512]{1,0:T(8,128)(2,1)S(1)}, u32[]{:S(2)}, u32[]{:S(2)}) collective-permute-start(bf16[48,512]{1,0:T(8,128)(2,1)S(1)} %get-tuple-element.52), channel_id=1, source_target_pairs={{0,8},{1,9},{2,10},{3,11},{4,5},{5,6},{6,7},{7,4},{8,16},{9,17},{1... | collective-permute-start | bytes 147464 | tf_op jit(solution)/shard_map/ppermute | solution.py:61
  61.3 6.2 %collective-permute-start.5 = (bf16[48,512]{1,0:T(8,128)(2,1)S(1)}, bf16[48,512]{1,0:T(8,128)(2,1)S(1)}, u32[]{:S(2)}, u32[]{:S(2)}) collective-permute-start(bf16[48,512]{1,0:T(8,128)(2,1)S(1)} %get-tuple-element.53), channel_id=1, source_target_pairs={{0,16},{1,17},{2,18},{3,19},{4,6},{5,7},{6,4},{7,5},{8,24},{9,25},... | collective-permute-start | bytes 147464 | tf_op jit(solution)/shard_map/ppermute | solution.py:61
  63.8 3.8 %collective-permute-start.6 = (bf16[48,512]{1,0:T(8,128)(2,1)S(1)}, bf16[48,512]{1,0:T(8,128)(2,1)S(1)}, u32[]{:S(2)}, u32[]{:S(2)}) collective-permute-start(bf16[48,512]{1,0:T(8,128)(2,1)S(1)} %get-tuple-element.54), channel_id=1, source_target_pairs={{0,24},{1,25},{2,26},{3,27},{4,7},{5,4},{6,5},{7,6},{8,0},{9,1},{1... | collective-permute-start | bytes 147464 | tf_op jit(solution)/shard_map/ppermute | solution.py:61
  67.6 3.4 %collective-permute-start.7 = (bf16[80,512]{1,0:T(8,128)(2,1)S(1)}, bf16[80,512]{1,0:T(8,128)(2,1)S(1)}, u32[]{:S(2)}, u32[]{:S(2)}) collective-permute-start(bf16[80,512]{1,0:T(8,128)(2,1)S(1)} %shard_map.127.a), channel_id=1, source_target_pairs={{0,32},{1,33},{2,34},{3,35},{4,36},{5,37},{6,38},{7,39},{8,40},{9,... | collective-permute-start | bytes 245768 | tf_op jit(solution)/shard_map/ppermute | solution.py:61
  71.0 5.2 %collective-permute-start.8 = (bf16[80,512]{1,0:T(8,128)(2,1)S(1)}, bf16[80,512]{1,0:T(8,128)(2,1)S(1)}, u32[]{:S(2)}, u32[]{:S(2)}) collective-permute-start(bf16[80,512]{1,0:T(8,128)(2,1)S(1)} %shard_map.128.a), channel_id=1, source_target_pairs={{0,96},{1,97},{2,98},{3,99},{4,100},{5,101},{6,102},{7,103},{8,104... | collective-permute-start | bytes 245768 | tf_op jit(solution)/shard_map/ppermute | solution.py:61
  76.2 5.0 %collective-permute-start.9 = (bf16[80,512]{1,0:T(8,128)(2,1)S(1)}, bf16[80,512]{1,0:T(8,128)(2,1)S(1)}, u32[]{:S(2)}, u32[]{:S(2)}) collective-permute-start(bf16[80,512]{1,0:T(8,128)(2,1)S(1)} %shard_map.129.a), channel_id=1, source_target_pairs={{0,224},{1,225},{2,226},{3,227},{4,228},{5,229},{6,230},{7,231},{8... | collective-permute-start | bytes 245768 | tf_op jit(solution)/shard_map/ppermute | solution.py:61
  81.2 4.6 %collective-permute-start.10 = (bf16[80,512]{1,0:T(8,128)(2,1)S(1)}, bf16[80,512]{1,0:T(8,128)(2,1)S(1)}, u32[]{:S(2)}, u32[]{:S(2)}) collective-permute-start(bf16[80,512]{1,0:T(8,128)(2,1)S(1)} %shard_map.130.own), channel_id=1, source_target_pairs={{0,8},{1,9},{2,10},{3,11},{4,5},{5,6},{6,7},{7,4},{8,16},{9,17},{1... | collective-permute-start | bytes 245768 | tf_op jit(solution)/shard_map/ppermute | solution.py:61
  82.0 4.8 %collective-permute-start.11 = (bf16[80,512]{1,0:T(8,128)(2,1)S(1)}, bf16[80,512]{1,0:T(8,128)(2,1)S(1)}, u32[]{:S(2)}, u32[]{:S(2)}) collective-permute-start(bf16[80,512]{1,0:T(8,128)(2,1)S(1)} %shard_map.130.own), channel_id=1, source_target_pairs={{0,16},{1,17},{2,18},{3,19},{4,6},{5,7},{6,4},{7,5},{8,24},{9,25},... | collective-permute-start | bytes 245768 | tf_op jit(solution)/shard_map/ppermute | solution.py:61
  84.0 3.3 %collective-permute-start.12 = (bf16[80,512]{1,0:T(8,128)(2,1)S(1)}, bf16[80,512]{1,0:T(8,128)(2,1)S(1)}, u32[]{:S(2)}, u32[]{:S(2)}) collective-permute-start(bf16[80,512]{1,0:T(8,128)(2,1)S(1)} %shard_map.130.own), channel_id=1, source_target_pairs={{0,24},{1,25},{2,26},{3,27},{4,7},{5,4},{6,5},{7,6},{8,0},{9,1},{1... | collective-permute-start | bytes 245768 | tf_op jit(solution)/shard_map/ppermute | solution.py:61
  87.4 7.1 %collective-permute-start.13 = (bf16[224,512]{1,0:T(8,128)(2,1)S(1)}, bf16[224,512]{1,0:T(8,128)(2,1)S(1)}, u32[]{:S(2)}, u32[]{:S(2)}) collective-permute-start(bf16[224,512]{1,0:T(8,128)(2,1)S(1)} %shard_map.131.own), channel_id=1, source_target_pairs={{0,1},{1,2},{2,3},{3,0},{4,12},{5,13},{6,14},{7,15},{8,9},{9,10},{... | collective-permute-start | bytes 688136 | tf_op jit(solution)/shard_map/ppermute | solution.py:61
  88.4 9.2 %collective-permute-start.14 = (bf16[224,512]{1,0:T(8,128)(2,1)S(1)}, bf16[224,512]{1,0:T(8,128)(2,1)S(1)}, u32[]{:S(2)}, u32[]{:S(2)}) collective-permute-start(bf16[224,512]{1,0:T(8,128)(2,1)S(1)} %shard_map.131.own), channel_id=1, source_target_pairs={{0,2},{1,3},{2,0},{3,1},{4,20},{5,21},{6,22},{7,23},{8,10},{9,11},... | collective-permute-start | bytes 688136 | tf_op jit(solution)/shard_map/ppermute | solution.py:61
  90.7 7.0 %collective-permute-start.15 = (bf16[224,512]{1,0:T(8,128)(2,1)S(1)}, bf16[224,512]{1,0:T(8,128)(2,1)S(1)}, u32[]{:S(2)}, u32[]{:S(2)}) collective-permute-start(bf16[224,512]{1,0:T(8,128)(2,1)S(1)} %shard_map.131.own), channel_id=1, source_target_pairs={{0,3},{1,0},{2,1},{3,2},{4,28},{5,29},{6,30},{7,31},{8,11},{9,8},{... | collective-permute-start | bytes 688136 | tf_op jit(solution)/shard_map/ppermute | solution.py:61
  97.8 12.4 %collective-permute-start.16 = (bf16[800,512]{1,0:T(8,128)(2,1)S(1)}, bf16[800,512]{1,0:T(8,128)(2,1)S(1)}, u32[]{:S(2)}, u32[]{:S(2)}) collective-permute-start(bf16[800,512]{1,0:T(8,128)(2,1)S(1)} %shard_map.132.own), channel_id=1, source_target_pairs={{0,4},{1,5},{2,6},{3,7},{4,0},{5,1},{6,2},{7,3},{8,12},{9,13},{10,... | collective-permute-start | bytes 2457608 | tf_op jit(solution)/shard_map/ppermute | solution.py:61

commit v4 on v3

--- a/solution.py
+++ b/solution.py
@@ -101,7 +101,8 @@
     put(out, 48, small[...])
 
 
-def k_pair(a, b, out):
+def k_pair(a, b, *rest):
+    out = rest[-1]
     head = pl.ds(0, 48)
     out[head, :] = (a[head, :].astype(F32) + b[head, :].astype(F32)).astype(BF)
     put(out, 48, lift(a, 48) + lift(b, 48))
@@ -159,7 +160,7 @@
     return jnp.stack([first, second, core]).astype(jnp.int32)
 
 
-def reduce_all(pos, other, mine, backward, feats):
+def reduce_all(pos, other, mine, backward, features):
     core, one, two, steps = perms()
     row = 512
     third = ((48, row), BF)
@@ -167,21 +168,22 @@
     own = mine(other)
     m1, m2, m3, keep = call(k_scatter_one, [((192, row), BF)] * 3 + [((192, row), F32)], [own, got], pos)
     r = [send(m, p) for m, p in zip((m1, m2, m3), one)]
-    small = backward(0, 4, jnp.zeros((16, row), F32), keep)
+    small = backward(0, 2, jnp.zeros((16, row), F32), keep)
     m1, m2, m3, keep2 = call(
         k_scatter_two, [third] * 3 + [((48, row), F32)], [keep, *r], pos, after=[small]
     )
     r = [send(m, p) for m, p in zip((m1, m2, m3), two)]
-    small = backward(4, 2, small, keep2)
+    small = backward(2, 1, small, keep2)
     (a,) = call(k_sum_two, [((80, row), BF)], [keep2, *r, small])
-    for step in steps:
+    feats = None
+    for n, step in enumerate(steps):
         b = send(a, step)
-        (a,) = call(k_pair, [((80, row), BF)], [a, b])
+        if n == 1:
+            feats, token = features(a)
+        (a,) = call(k_pair, [((80, row), BF)], [a, b], after=[token] if n == 1 else [])
     r = [send(a, p) for p in two]
     (a,) = call(k_join_two, [((224, row), BF)], [a, *r])
-    feats = jnp.transpose(feats, (1, 0, 2))
     r = [send(a, p) for p in one]
-    a, feats, *r = lax.optimization_barrier((a, feats, *r))
     (a,) = call(k_join_one, [((800, row), BF)], [a, *r])
     got = send(a, core)
     room = [pltpu.VMEM((768, row), F32), pltpu.SemaphoreType.DMA((4,))]
@@ -227,7 +229,7 @@
     same = (column(device) == device) & (up < across)
     rank = jnp.sum(jnp.where(same, 1.0, 0.0), axis=0, keepdims=True)
     bucket = (device * 2.0 + rank).astype(jnp.int32)
-    places = out.shape[0]
+    places = out.shape[0] * out.shape[1]
     pick = lax.broadcasted_iota(jnp.int32, (places, spans), 0) == bucket
     pick = jnp.where(pick, 1.0, 0.0).astype(BF)
     rows[...] = jnp.zeros(rows.shape, F32)
@@ -237,7 +239,8 @@
     tail = jnp.where(lane == SAMPLES - 256, column(slot) + 1.0, tail)
     tail = jnp.where(lane == SAMPLES - 255, column(length[...].astype(F32)) - 214.0, tail)
     rows[:, pl.ds(256, 128)] = tail
-    out[...] = jnp.dot(pick, rows[...].astype(BF), preferred_element_type=F32).astype(BF)
+    packed = jnp.dot(pick, rows[...].astype(BF), preferred_element_type=F32)
+    out[...] = packed.reshape(out.shape).astype(BF)
 
 
 def gelu_parts(value):
@@ -247,6 +250,7 @@
 
 
 BLOCK = 8
+BACK = 16
 ROWS = 32 * BLOCK
 
 
@@ -258,17 +262,18 @@
 
 
 def tables(fold, window):
-    sample = lax.broadcasted_iota(jnp.int32, (WIDE, 128), 0).astype(F32)
-    lane = lax.broadcasted_iota(jnp.int32, (WIDE, 128), 1).astype(F32)
+    sample = lax.broadcasted_iota(jnp.int32, (256, 128), 0).astype(F32)
+    lane = lax.broadcasted_iota(jnp.int32, (256, 128), 1).astype(F32)
     tens = jnp.floor((sample + 0.5) * 0.1) * 10.0
-    fold[pl.ds(0, WIDE), :] = jnp.where((sample < SAMPLES) & (sample - tens == lane), 1.0, 0.0).astype(BF)
+    fold[pl.ds(0, 256), :] = jnp.where(sample - tens == lane, 1.0, 0.0).astype(BF)
     tens = jnp.floor((sample - 4.5) * 0.1) * 10.0
-    odd = (sample < SAMPLES) & (sample >= 5.0) & (sample - 5.0 - tens + 16.0 == lane)
-    fold[pl.ds(WIDE, WIDE), :] = jnp.where(odd, 1.0, 0.0).astype(BF)
-    step = lax.broadcasted_iota(jnp.int32, (32, WIDE), 0) * 10
-    at = lax.broadcasted_iota(jnp.int32, (32, WIDE), 1)
-    window[:, pl.ds(0, WIDE)] = jnp.where((at >= step) & (at < step + 10), 1.0, 0.0)
-    window[:, pl.ds(WIDE, WIDE)] = jnp.where((at >= step + 5) & (at < step + 15), 1.0, 0.0)
+    odd = (sample >= 5.0) & (sample - 5.0 - tens + 16.0 == lane)
+    fold[pl.ds(256, 256), :] = jnp.where(odd, 1.0, 0.0).astype(BF)
+    step = lax.broadcasted_iota(jnp.int32, (32, 256), 0)
+    step = jnp.where(step < 16, step, step - 16) * 10
+    at = lax.broadcasted_iota(jnp.int32, (32, 256), 1)
+    window[:, pl.ds(0, 256)] = jnp.where((at >= step) & (at < step + 10), 1.0, 0.0)
+    window[:, pl.ds(256, 256)] = jnp.where((at >= step + 5) & (at < step + 15), 1.0, 0.0)
 
 
 def tall(rows):
@@ -285,8 +290,8 @@
 
 def k_forward(
     scale, pos, arrived, weo, gain, bias, weight, fgrad,
-    feats, g, gs, se, so, ne, no, istd, valid, x, he, ho, other,
-    fold, window, panels, am, pre, hs, pre1,
+    pre1, second_count, g, gs, se, so, ne, no, istd, valid, x, he, ho, other,
+    fold, window, panels, am, pre, hs,
 ):
     spans = panels.shape[0]
     tables(fold, window)
@@ -296,10 +301,13 @@
     slot = meta[:, SAMPLES - 256 : SAMPLES - 255]
     place = jnp.where(slot - 1.0 == lane, 1.0, 0.0).astype(BF)
     moved = dot_t(place, arr)[0:spans]
-    panels[...] = jnp.broadcast_to(moved[:, None, :], panels.shape)
+    late = pltpu.roll(moved, WIDE - 160, 1)
+    both = jnp.concatenate([moved[:, 0:256], late[:, 0:256]], axis=1)
+    panels[...] = jnp.broadcast_to(both[:, None, :], panels.shape)
     length = moved[:, SAMPLES + 1 : SAMPLES + 2] + 214.0
     count = jnp.broadcast_to(jnp.floor((length - 9.5) * 0.2) + 1.0, (spans, 128))
     valid[...] = jnp.broadcast_to(count[:, None, :], valid.shape)
+    second_count[...] = jnp.floor((count - 2.5) * 0.5) + 1.0
     frame = lax.broadcasted_iota(jnp.int32, (32, 128), 0).astype(F32)
 
     def block(b, carry):
@@ -310,9 +318,11 @@
             count = tall(valid[p])
             keep_e, keep_o = 2.0 * frame < count, 2.0 * frame + 1.0 < count
             rows = pl.ds(pl.multiple_of(q * 32, 32), 32)
-            for t in range(6):
-                part = tall(panels[p, :, pl.ds((t % 3) * 128, 128)])
-                part = jnp.where(keep_e if t < 3 else keep_o, part * window[:, pl.ds(t * 128, 128)], 0.0)
+            for t in range(4):
+                early = panels[p, :, pl.ds((t % 2) * 128, 128)]
+                late = panels[p, :, pl.ds(256 + (t % 2) * 128, 128)]
+                part = jnp.concatenate([early, early, late, late], axis=0)
+                part = jnp.where(keep_e if t < 2 else keep_o, part * window[:, pl.ds(t * 128, 128)], 0.0)
                 am[rows, pl.ds(t * 128, 128)] = part.astype(BF)
             return carry
 
@@ -354,24 +364,23 @@
             return carry
 
         lax.fori_loop(0, BLOCK, norm, 0, unroll=2)
-        pre1[...] = (
+        total = (
             jnp.dot(he[every, :], weight[0], preferred_element_type=F32)
             + jnp.dot(ho[every, :], weight[1], preferred_element_type=F32)
             + jnp.dot(hs[...], weight[2], preferred_element_type=F32)
         )
+        for t in range(4):
+            pre1[t, every, :] = total[:, t * 128 : t * 128 + 128]
 
         def second(q, carry):
             p = base + q
             count = tall(jnp.floor((valid[p] - 2.5) * 0.5) + 1.0)
             keep = frame < count
-            rows = pl.ds(pl.multiple_of(q * 32, 32), 32)
             at = pl.ds(pl.multiple_of(p * 32, 32), 32)
             for t in range(4):
                 cols = pl.ds(t * 128, 128)
-                value = pre1[rows, cols]
+                value = pre1[t, at, :]
                 cumul, density = gelu_parts(value)
-                act = jnp.where(keep, value * cumul, 0.0)
-                feats[p, :, cols] = act[0:31].astype(BF)
                 up = fgrad[p, :, cols].astype(F32) * scale
                 up = jnp.concatenate([up, jnp.zeros((1, 128), F32)], axis=0)
                 grad = jnp.where(keep, up * (cumul + value * density), 0.0)
@@ -402,16 +411,32 @@
     half_of(pos[2], he, ho, g, gs, out)
 
 
+def k_features(pre1, count, before, feats, token):
+    token[...] = jnp.zeros(token.shape, F32)
+    spans = count.shape[0]
+
+    def frame(t, carry):
+        keep = count[...] > lax.convert_element_type(t, F32)
+        for c in range(4):
+            cols = pl.ds(c * 128, 128)
+            value = pre1[c, pl.ds(t, spans, stride=32), :]
+            cumul, _ = gelu_parts(value)
+            feats[t, :, cols] = jnp.where(keep, value * cumul, 0.0).astype(BF)
+        return carry
+
+    lax.fori_loop(0, feats.shape[0], frame, 0)
+
+
 def k_backward(
     first, g, gs, se, so, ne, no, istd, valid, x, gain, weight, start, before, small,
     de, do, dxe, dxo, sums,
 ):
-    blocks = dxe.shape[0] // ROWS
+    blocks = dxe.shape[0] // (32 * BACK)
     sums[...] = jnp.zeros(sums.shape, F32)
 
     def block(b, carry):
-        base = (first + b) * BLOCK
-        every = pl.ds(pl.multiple_of((first + b) * ROWS, ROWS), ROWS)
+        base = (first + b) * BACK
+        every = pl.ds(pl.multiple_of((first + b) * (32 * BACK), (32 * BACK)), (32 * BACK))
         de[...] = dot_nt(g[every, :], weight[0]) + dot_nt(gs[every, :], weight[2])
         do[...] = dot_nt(g[every, :], weight[1])
 
@@ -420,7 +445,7 @@
             inverse = 1.0 / valid[p, pl.ds(0, 1), :]
             rows = pl.ds(pl.multiple_of(q * 32, 32), 32)
             at = pl.ds(pl.multiple_of(p * 32, 32), 32)
-            here = pl.ds(pl.multiple_of((b * BLOCK + q) * 32, 32), 32)
+            here = pl.ds(pl.multiple_of((b * BACK + q) * 32, 32), 32)
             for t in range(4):
                 cols = pl.ds(t * 128, 128)
                 pe = de[rows, cols] * se[at, cols].astype(F32)
@@ -436,11 +461,11 @@
                 dxo[here, cols] = ((po - plain - o * mixed) * lead).astype(BF)
             return carry
 
-        lax.fori_loop(0, BLOCK, back, 0, unroll=2)
+        lax.fori_loop(0, BACK, back, 0, unroll=2)
         return carry
 
     lax.fori_loop(0, blocks, block, 0)
-    part = x[pl.ds(first * ROWS, blocks * ROWS), :]
+    part = x[pl.ds(first * (32 * BACK), blocks * (32 * BACK)), :]
     small[...] = start[...] + dot_t(part, dxe[...])[0:16] + dot_t(part, dxo[...])[16:32]
     small[pl.ds(10, 2), :] += sums[pl.ds(0, 2), :]
 
@@ -451,34 +476,40 @@
     (weo,) = call(k_taps, [((128, 1024), BF)], [conv0_weight])
     gain, bias = norm_gain[None], norm_bias[None]
     wide = ((rows, 512), BF)
-    feats, g, gs, se, so, ne, no, istd, valid, x, he, ho, other = call(
+    pre1, count, g, gs, se, so, ne, no, istd, valid, x, he, ho, other = call(
         functools.partial(k_forward, scale),
         [
-            (feature_grad.shape, BF), wide, wide, wide, wide, wide, wide,
+            ((4, rows, 128), F32), ((spans, 128), F32), wide, wide, wide, wide, wide, wide,
             ((spans, 8, 512), F32), ((spans, 8, 128), F32), ((rows, 128), BF), wide, wide, ((768, 512), BF),
         ],
         [arrived, weo, gain, bias, conv1_weight, feature_grad],
         pos,
         scratch=[
-            ((2 * WIDE, 128), BF), ((32, 2 * WIDE), F32), ((spans, 8, WIDE), F32), ((ROWS, 2 * WIDE), BF), ((ROWS, 1024), F32),
-            ((ROWS, 512), BF), ((ROWS, 512), F32),
+            ((512, 128), BF), ((32, 512), F32), ((spans, 8, 512), F32), ((ROWS, 512), BF), ((ROWS, 1024), F32),
+            ((ROWS, 512), BF),
         ],
     )
 
+    def features(before):
+        frames = feature_grad.shape[1]
+        return call(
+            k_features, [((frames, spans, 512), BF), ((8, 128), F32)], [pre1, count], after=[before]
+        )
+
     def mine(before):
         return call(k_half, [((768, 512), F32)], [he, ho, g, gs], pos, after=[before])[0]
 
     def backward(first, blocks, small, before):
-        part = (ROWS * blocks, 512)
+        part, step = (32 * BACK * blocks, 512), (32 * BACK, 512)
         return call(
             functools.partial(k_backward, first),
             [((16, 512), F32)],
             [g, gs, se, so, ne, no, istd, valid, x, gain, conv1_weight, small],
-            scratch=[((ROWS, 512), F32), ((ROWS, 512), F32), (part, BF), (part, BF), ((8, 512), F32)],
+            scratch=[(step, F32), (step, F32), (part, BF), (part, BF), ((8, 512), F32)],
             after=[before],
         )[0]
 
-    return feats, other, mine, backward
+    return features, other, mine, backward
 
 
 def body(waveform, lengths, target, conv0_weight, norm_gain, norm_bias, conv1_weight, feature_grad):
@@ -488,7 +519,7 @@
     pos = where_am_i()
     (packed,) = call(
         k_pack,
-        [((2 * devices, WIDE), BF)],
+        [((devices, 2, WIDE), BF)],
         [],
         scratch=[
             ((spans, WIDE), F32), (waveform.shape[1:], BF), (lengths.shape, jnp.int32), (target.shape, jnp.int32),
@@ -498,13 +529,13 @@
         late=HBM,
         limit=60,
     )
-    arrived = lax.all_to_all(packed.reshape(devices, 2, WIDE), "dp", split_axis=0, concat_axis=0, tiled=True)
+    arrived = lax.all_to_all(packed, "dp", split_axis=0, concat_axis=0, tiled=True)
     arrived = arrived.reshape(2 * devices, WIDE)
     scale = 1.0 / float(lax.axis_size("rep") * devices * spans * frames) ** 0.5
-    feats, other, mine, backward = encode(
+    features, other, mine, backward = encode(
         pos, arrived, conv0_weight, norm_gain, norm_bias, conv1_weight, feature_grad[0], scale
     )
-    full, conv0, gain, bias, feats = reduce_all(pos, other, mine, backward, feats)
+    full, conv0, gain, bias, feats = reduce_all(pos, other, mine, backward, features)
     return (feats[None], conv0, gain, bias, full.reshape(conv1_weight.shape))
 
 

time: 114 us -> 110 us (0.965)
  local copies, waits for them, and re-layouts: 6.87 us -> 3.31 us
  Pallas kernels: 35.6 us -> 39.1 us
  waiting for transfers between devices: 29.6 us -> 27.5 us
  starting transfers between devices: 39.5 us -> 38.2 us
    pallas_call x14 -> x15, Pallas kernels: 31.5 us -> 35 us  [call(): pl.pallas_call(kernel, out_shape=shapes, in_specs=specs, out_specs=[VM] *...]
    ppermute x17, waiting for transfers between devices: 21.6 us -> 19.6 us  [send(): return lax.ppermute(value, BOTH, perm)]
    unnamed x10 -> x9, local copies, waits for them, and re-layouts: 4.36 us -> 2.37 us
    reshape x1 -> x0, local copies, waits for them, and re-layouts: 1.57 us -> none  [body(): packed.reshape(devices, 2, WIDE)]
    ppermute x17, starting transfers between devices: 26.2 us -> 24.8 us  [send(): return lax.ppermute(value, BOTH, perm)]
  transfers between devices with their start and end apart: 18 -> 18, of which waited for: 11 -> 12; matrix products, arithmetic and copies ran while one was open for 4% -> 2% of each run, Pallas kernels for 10% -> 14%
where the time goes in v4:
time: 110 us; the launch traced here: 109 us
  Pallas kernels  39.1 us (36%)
  starting transfers between devices  38.2 us (35%)
  waiting for transfers between devices  27.5 us (25%)
  local copies, waits for them, and re-layouts  3.31 us (3%)
    pallas_call x15, Pallas kernels, call(): pl.pallas_call(kernel, out_shape=shapes, in_specs=specs, out_specs=[VM] *...  35 us
    ppermute x17, starting transfers between devices, send(): return lax.ppermute(value, BOTH, perm)  24.8 us
    ppermute x17, waiting for transfers between devices, send(): return lax.ppermute(value, BOTH, perm)  19.6 us
    all_to_all x1, starting transfers between devices, body(): lax.all_to_all(packed, 'dp', split_axis=0, concat_axis=0, tiled=True)  13.3 us
    all_to_all x1, waiting for transfers between devices, body(): lax.all_to_all(packed, 'dp', split_axis=0, concat_axis=0, tiled=True)  7.96 us
    unnamed x9, local copies, waits for them, and re-layouts  2.37 us
    pallas_call x1, Pallas kernels, reduce_all(): pl.pallas_call(k_final, out_shape=[whole] + [jax.ShapeDtypeStruct((n, row...  2.36 us
  transfers between devices with their start and end apart: 18, of which 12 were waited for; matrix products, arithmetic and copies ran while one was open for 2% of the time, Pallas kernels for 14%

profile of v4, /device:TPU:1, one launch (start us, length us, event | category | flops | bytes accessed | tf_op | source)
XLA Modules:
  0.0 109.2 jit_solution(9218442085278917112)
XLA Ops:
  0.6 1.8 %shard_map.119 = bf16[64,2,384]{2,1,0:T(2,128)(2,1)} custom-call(bf16[48,320]{1,0:T(8,128)(2,1)} %bitcast.21, s32[1,48]{1,0:T(1,128)} %length_in.1, s32[1,48]{1,0:T(1,128)} %target_in.1), custom_call_target="tpu_custom_call" | custom-call | tf_op jit(solution)/shard_map/pallas_call | solution.py:26
  2.4 13.3 %all-to-all-start = ((bf16[64,2,384]{2,1,0:T(2,128)(2,1)}), bf16[64,2,384]{2,1,0:T(2,128)(2,1)}, u32[]{:S(2)}, u32[]{:S(2)}) async-start(bf16[64,2,384]{2,1,0:T(2,128)(2,1)} %shard_map.119), calls=%async_computation | async-start | bytes 196608 | tf_op jit(solution)/shard_map/all_to_all | solution.py:532
  15.8 2.3 %copy.16 = bf16[1,48,31,512]{3,2,1,0:T(8,128)(2,1)S(1)} copy(bf16[1,48,31,512]{3,1,2,0:T(8,128)(2,1)} %param.15) | data formatting | bytes 3047424 | tf_op args[7]
  18.3 8.0 %all-to-all-done = bf16[64,2,384]{2,1,0:T(2,128)(2,1)} async-done(((bf16[64,2,384]{2,1,0:T(2,128)(2,1)}), bf16[64,2,384]{2,1,0:T(2,128)(2,1)}, u32[]{:S(2)}, u32[]{:S(2)}) %all-to-all-start) | async-done | bytes 98336 | tf_op jit(solution)/shard_map/all_to_all | solution.py:532
  26.3 0.9 reshape.16.arrived
  27.2 17.8 %shard_map.121 = (f32[4,1536,128]{2,1,0:T(8,128)S(1)}, f32[48,128]{1,0:T(8,128)S(1)}, bf16[1536,512]{1,0:T(8,128)(2,1)S(1)}, bf16[1536,512]{1,0:T(8,128)(2,1)S(1...) custom-call(s32[3]{0:T(128)S(1)} %pad_add_fusion.pos, ...), custom_call_target="tpu_custom_call" | custom-call | tf_op jit(solution)/shard_map/pallas_call | solution.py:26
  45.0 0.5 collective-permute-start
  45.5 2.0 %shard_map.122.own = f32[768,512]{1,0:T(8,128)S(1)} custom-call(s32[3]{0:T(128)S(1)} %pad_add_fusion.pos, bf16[1536,512]{1,0:T(8,128)(2,1)S(1)} %get-tuple-element.35.he, bf16[1536,512]{1,0:T(8,128)(2,1)S(1)} %get-tuple-element.36.ho, bf16[1536,512]{1,0:T(8,128)(2,1)S(1)} %get-tuple-element.37.g, bf16[1536,512]{1,0:T(8,128)(2,1)S(1)} %get-tuple-element.38.gs, ...), custom_call_target="tpu_custom_call" | custom-call | tf_op jit(solution)/shard_map/pallas_call | solution.py:26
  47.5 0.7 shard_map.123
  48.4 1.4 %collective-permute-start.2 = (bf16[192,512]{1,0:T(8,128)(2,1)S(1)}, bf16[192,512]{1,0:T(8,128)(2,1)S(1)}, u32[]{:S(2)}, u32[]{:S(2)}) collective-permute-start(bf16[192,512]{1,0:T(8,128)(2,1)S(1)} %get-tuple-element.42), channel_id=1, source_target_pairs={{0,2},{1,3},{2,0},{3,1},{4,20},{5,21},{6,22},{7,23},{8,10},{9,11},... | collective-permute-start | bytes 589832 | tf_op jit(solution)/shard_map/ppermute | solution.py:61
  49.8 1.6 %collective-permute-start.3 = (bf16[192,512]{1,0:T(8,128)(2,1)S(1)}, bf16[192,512]{1,0:T(8,128)(2,1)S(1)}, u32[]{:S(2)}, u32[]{:S(2)}) collective-permute-start(bf16[192,512]{1,0:T(8,128)(2,1)S(1)} %get-tuple-element.43), channel_id=1, source_target_pairs={{0,3},{1,0},{2,1},{3,2},{4,28},{5,29},{6,30},{7,31},{8,11},{9,8},{... | collective-permute-start | bytes 589832 | tf_op jit(solution)/shard_map/ppermute | solution.py:61
  51.4 4.7 %shard_map.124.before.start = f32[16,512]{1,0:T(8,128)S(1)} custom-call(bf16[1536,512]{1,0:T(8,128)(2,1)S(1)} %get-tuple-element.37.g, bf16[1536,512]{1,0:T(8,128)(2,1)S(1)} %get-tuple-element.38.gs, bf16[1536,512]{1,0:T(8,128)(2,1)S(1)} %get-tuple-element.44.se, bf16[1536,512]{1,0:T(8,128)(2,1)S(1)} %get-tuple-element.45.so, ...), custom_call_target="tpu_custom_call" | custom-call | tf_op jit(solution)/shard_map/pallas_call | solution.py:26
  56.4 0.6 collective-permute-done.3.r3
  57.0 0.6 shard_map.125
  57.6 1.5 %collective-permute-start.4 = (bf16[48,512]{1,0:T(8,128)(2,1)S(1)}, bf16[48,512]{1,0:T(8,128)(2,1)S(1)}, u32[]{:S(2)}, u32[]{:S(2)}) collective-permute-start(bf16[48,512]{1,0:T(8,128)(2,1)S(1)} %get-tuple-element.52), channel_id=1, source_target_pairs={{0,8},{1,9},{2,10},{3,11},{4,5},{5,6},{6,7},{7,4},{8,16},{9,17},{1... | collective-permute-start | bytes 147464 | tf_op jit(solution)/shard_map/ppermute | solution.py:61
  59.1 2.5 %collective-permute-start.5 = (bf16[48,512]{1,0:T(8,128)(2,1)S(1)}, bf16[48,512]{1,0:T(8,128)(2,1)S(1)}, u32[]{:S(2)}, u32[]{:S(2)}) collective-permute-start(bf16[48,512]{1,0:T(8,128)(2,1)S(1)} %get-tuple-element.53), channel_id=1, source_target_pairs={{0,16},{1,17},{2,18},{3,19},{4,6},{5,7},{6,4},{7,5},{8,24},{9,25},... | collective-permute-start | bytes 147464 | tf_op jit(solution)/shard_map/ppermute | solution.py:61
  61.5 1.1 %collective-permute-start.6 = (bf16[48,512]{1,0:T(8,128)(2,1)S(1)}, bf16[48,512]{1,0:T(8,128)(2,1)S(1)}, u32[]{:S(2)}, u32[]{:S(2)}) collective-permute-start(bf16[48,512]{1,0:T(8,128)(2,1)S(1)} %get-tuple-element.54), channel_id=1, source_target_pairs={{0,24},{1,25},{2,26},{3,27},{4,7},{5,4},{6,5},{7,6},{8,0},{9,1},{1... | collective-permute-start | bytes 147464 | tf_op jit(solution)/shard_map/ppermute | solution.py:61
  62.7 2.4 %shard_map.126.small = f32[16,512]{1,0:T(8,128)S(1)} custom-call(bf16[1536,512]{1,0:T(8,128)(2,1)S(1)} %get-tuple-element.37.g, bf16[1536,512]{1,0:T(8,128)(2,1)S(1)} %get-tuple-element.38.gs, bf16[1536,512]{1,0:T(8,128)(2,1)S(1)} %get-tuple-element.44.se, bf16[1536,512]{1,0:T(8,128)(2,1)S(1)} %get-tuple-element.45.so, ...), custom_call_target="tpu_custom_call" | custom-call | tf_op jit(solution)/shard_map/pallas_call | solution.py:26
  65.6 2.9 %collective-permute-done.7.b = bf16[80,512]{1,0:T(8,128)(2,1)S(1)} collective-permute-done((bf16[80,512]{1,0:T(8,128)(2,1)S(1)}, bf16[80,512]{1,0:T(8,128)(2,1)S(1)}, u32[]{:S(2)}, u32[]{:S(2)}) %collective-permute-start.7) | collective-permute-done | bytes 81952 | tf_op jit(solution)/shard_map/ppermute | solution.py:61
  68.6 0.8 collective-permute-start.8
  69.5 4.8 %shard_map.129 = (bf16[31,48,512]{2,1,0:T(8,128)(2,1)}, f32[8,128]{1,0:T(8,128)S(1)}) custom-call(f32[4,1536,128]{2,1,0:T(8,128)S(1)} %get-tuple-element.33.pre1, f32[48,128]{1,0:T(8,128)S(1)} %get-tuple-element.34.count, bf16[80,512]{1,0:T(8,128)(2,1)S(1)} %shard_map.128.before.a), custom_call_target="tpu_custom_call" | custom-call | tf_op jit(solution)/shard_map/pallas_call | solution.py:26
  74.6 5.1 %collective-permute-done.9.b = bf16[80,512]{1,0:T(8,128)(2,1)S(1)} collective-permute-done((bf16[80,512]{1,0:T(8,128)(2,1)S(1)}, bf16[80,512]{1,0:T(8,128)(2,1)S(1)}, u32[]{:S(2)}, u32[]{:S(2)}) %collective-permute-start.9) | collective-permute-done | bytes 81952 | tf_op jit(solution)/shard_map/ppermute | solution.py:61
  80.2 2.8 %collective-permute-start.11 = (bf16[80,512]{1,0:T(8,128)(2,1)S(1)}, bf16[80,512]{1,0:T(8,128)(2,1)S(1)}, u32[]{:S(2)}, u32[]{:S(2)}) collective-permute-start(bf16[80,512]{1,0:T(8,128)(2,1)S(1)} %shard_map.131.own), channel_id=1, source_target_pairs={{0,16},{1,17},{2,18},{3,19},{4,6},{5,7},{6,4},{7,5},{8,24},{9,25},... | collective-permute-start | bytes 245768 | tf_op jit(solution)/shard_map/ppermute | solution.py:61
  83.0 1.4 %collective-permute-done.10.r1 = bf16[80,512]{1,0:T(8,128)(2,1)S(1)} collective-permute-done((bf16[80,512]{1,0:T(8,128)(2,1)S(1)}, bf16[80,512]{1,0:T(8,128)(2,1)S(1)}, u32[]{:S(2)}, u32[]{:S(2)}) %collective-permute-start.10) | collective-permute-done | bytes 81952 | tf_op jit(solution)/shard_map/ppermute | solution.py:61
  84.3 1.3 %collective-permute-done.11.r2 = bf16[80,512]{1,0:T(8,128)(2,1)S(1)} collective-permute-done((bf16[80,512]{1,0:T(8,128)(2,1)S(1)}, bf16[80,512]{1,0:T(8,128)(2,1)S(1)}, u32[]{:S(2)}, u32[]{:S(2)}) %collective-permute-start.11) | collective-permute-done | bytes 81952 | tf_op jit(solution)/shard_map/ppermute | solution.py:61
  85.7 0.6 collective-permute-done.12.r3
  86.4 2.7 %collective-permute-start.14 = (bf16[224,512]{1,0:T(8,128)(2,1)S(1)}, bf16[224,512]{1,0:T(8,128)(2,1)S(1)}, u32[]{:S(2)}, u32[]{:S(2)}) collective-permute-start(bf16[224,512]{1,0:T(8,128)(2,1)S(1)} %shard_map.132.own), channel_id=1, source_target_pairs={{0,2},{1,3},{2,0},{3,1},{4,20},{5,21},{6,22},{7,23},{8,10},{9,11},... | collective-permute-start | bytes 688136 | tf_op jit(solution)/shard_map/ppermute | solution.py:61
  89.2 4.1 %collective-permute-done.13.r1 = bf16[224,512]{1,0:T(8,128)(2,1)S(1)} collective-permute-done((bf16[224,512]{1,0:T(8,128)(2,1)S(1)}, bf16[224,512]{1,0:T(8,128)(2,1)S(1)}, u32[]{:S(2)}, u32[]{:S(2)}) %collective-permute-start.13) | collective-permute-done | bytes 229408 | tf_op jit(solution)/shard_map/ppermute | solution.py:61
  93.4 2.6 %collective-permute-done.14.r2 = bf16[224,512]{1,0:T(8,128)(2,1)S(1)} collective-permute-done((bf16[224,512]{1,0:T(8,128)(2,1)S(1)}, bf16[224,512]{1,0:T(8,128)(2,1)S(1)}, u32[]{:S(2)}, u32[]{:S(2)}) %collective-permute-start.14) | collective-permute-done | bytes 229408 | tf_op jit(solution)/shard_map/ppermute | solution.py:61
  96.5 8.2 %collective-permute-start.16 = (bf16[800,512]{1,0:T(8,128)(2,1)S(1)}, bf16[800,512]{1,0:T(8,128)(2,1)S(1)}, u32[]{:S(2)}, u32[]{:S(2)}) collective-permute-start(bf16[800,512]{1,0:T(8,128)(2,1)S(1)} %shard_map.133.own), channel_id=1, source_target_pairs={{0,4},{1,5},{2,6},{3,7},{4,0},{5,1},{6,2},{7,3},{8,12},{9,13},{10,... | collective-permute-start | bytes 2457608 | tf_op jit(solution)/shard_map/ppermute | solution.py:61
  104.7 1.7 %shard_map.134.half = f32[1536,512]{1,0:T(8,128)} custom-call(s32[3]{0:T(128)S(1)} %pad_add_fusion.pos, bf16[800,512]{1,0:T(8,128)(2,1)S(1)} %shard_map.133.own), custom_call_target="tpu_custom_call" | custom-call | tf_op jit(solution)/shard_map/pallas_call | solution.py:192
  106.7 2.4 %shard_map.135 = (f32[1536,512]{1,0:T(8,128)}, f32[10,512]{1,0:T(8,128)}, f32[1,512]{1,0:T(1,128)}, f32[1,512]{1,0:T(1,128)}) custom-call(s32[3]{0:T(128)S(1)} %pad_add_fusion.pos, bf16[800,512]{1,0:T(8,128)(2,1)S(1)} %shard_map.133.own, bf16[800,512]{1,0:T(8,128)(2,1)S(1)} %collective-permute-done.16.got, ...), custom_call_target="tpu_custom_call", output_to_operand_aliasing={{0}: (3, {})} | custom-call | tf_op jit(solution)/shard_map/pallas_call | solution.py:195
  (33 shorter events, 2.9 us)
Async XLA Ops:
  2.4 23.8 %all-to-all-start = ((bf16[64,2,384]{2,1,0:T(2,128)(2,1)}), bf16[64,2,384]{2,1,0:T(2,128)(2,1)}, u32[]{:S(2)}, u32[]{:S(2)}) async-start(bf16[64,2,384]{2,1,0:T(2,128)(2,1)} %shard_map.119), calls=%async_computation | async-start | bytes 196608 | tf_op jit(solution)/shard_map/all_to_all | solution.py:532
  15.8 2.4 %copy-start.2 = (bf16[10,512]{1,0:T(8,128)(2,1)S(1)}, bf16[10,512]{1,0:T(8,128)(2,1)}, u32[]{:S(2)}) copy-start(bf16[10,512]{1,0:T(8,128)(2,1)} %conv0.1) | copy-start | bytes 30724
  15.8 11.4 %copy-start = (bf16[3,512,512]{2,1,0:T(8,128)(2,1)S(1)}, bf16[3,512,512]{2,1,0:T(8,128)(2,1)}, u32[]{:S(2)}) copy-start(bf16[3,512,512]{2,1,0:T(8,128)(2,1)} %weight.5) | copy-start | bytes 4718596
  15.8 11.4 %copy-start.1 = (f32[512]{0:T(512)S(1)}, f32[512]{0:T(512)}, u32[]{:S(2)}) copy-start(f32[512]{0:T(512)} %param.12) | copy-start | bytes 6148
  15.8 11.4 %copy-start.3 = (f32[512]{0:T(512)S(1)}, f32[512]{0:T(512)}, u32[]{:S(2)}) copy-start(f32[512]{0:T(512)} %param.13) | copy-start | bytes 6148
  45.0 2.4 %collective-permute-start = (bf16[768,512]{1,0:T(8,128)(2,1)S(1)}, bf16[768,512]{1,0:T(8,128)(2,1)S(1)}, u32[]{:S(2)}, u32[]{:S(2)}) collective-permute-start(bf16[768,512]{1,0:T(8,128)(2,1)S(1)} %get-tuple-element.39.before), channel_id=1, source_target_pairs={{0,4},{1,5},{2,6},{3,7},{4,0},{5,1},{6,2},{7,3},{8,12},{9,13},{10,... | collective-permute-start | bytes 2359304 | tf_op jit(solution)/shard_map/ppermute | solution.py:61
  48.1 8.2 %collective-permute-start.1 = (bf16[192,512]{1,0:T(8,128)(2,1)S(1)}, bf16[192,512]{1,0:T(8,128)(2,1)S(1)}, u32[]{:S(2)}, u32[]{:S(2)}) collective-permute-start(bf16[192,512]{1,0:T(8,128)(2,1)S(1)} %get-tuple-element.41), channel_id=1, source_target_pairs={{0,1},{1,2},{2,3},{3,0},{4,12},{5,13},{6,14},{7,15},{8,9},{9,10},{... | collective-permute-start | bytes 589832 | tf_op jit(solution)/shard_map/ppermute | solution.py:61
  48.4 7.9 %collective-permute-start.2 = (bf16[192,512]{1,0:T(8,128)(2,1)S(1)}, bf16[192,512]{1,0:T(8,128)(2,1)S(1)}, u32[]{:S(2)}, u32[]{:S(2)}) collective-permute-start(bf16[192,512]{1,0:T(8,128)(2,1)S(1)} %get-tuple-element.42), channel_id=1, source_target_pairs={{0,2},{1,3},{2,0},{3,1},{4,20},{5,21},{6,22},{7,23},{8,10},{9,11},... | collective-permute-start | bytes 589832 | tf_op jit(solution)/shard_map/ppermute | solution.py:61
  49.8 7.1 %collective-permute-start.3 = (bf16[192,512]{1,0:T(8,128)(2,1)S(1)}, bf16[192,512]{1,0:T(8,128)(2,1)S(1)}, u32[]{:S(2)}, u32[]{:S(2)}) collective-permute-start(bf16[192,512]{1,0:T(8,128)(2,1)S(1)} %get-tuple-element.43), channel_id=1, source_target_pairs={{0,3},{1,0},{2,1},{3,2},{4,28},{5,29},{6,30},{7,31},{8,11},{9,8},{... | collective-permute-start | bytes 589832 | tf_op jit(solution)/shard_map/ppermute | solution.py:61
  57.6 7.5 %collective-permute-start.4 = (bf16[48,512]{1,0:T(8,128)(2,1)S(1)}, bf16[48,512]{1,0:T(8,128)(2,1)S(1)}, u32[]{:S(2)}, u32[]{:S(2)}) collective-permute-start(bf16[48,512]{1,0:T(8,128)(2,1)S(1)} %get-tuple-element.52), channel_id=1, source_target_pairs={{0,8},{1,9},{2,10},{3,11},{4,5},{5,6},{6,7},{7,4},{8,16},{9,17},{1... | collective-permute-start | bytes 147464 | tf_op jit(solution)/shard_map/ppermute | solution.py:61
  59.1 6.1 %collective-permute-start.5 = (bf16[48,512]{1,0:T(8,128)(2,1)S(1)}, bf16[48,512]{1,0:T(8,128)(2,1)S(1)}, u32[]{:S(2)}, u32[]{:S(2)}) collective-permute-start(bf16[48,512]{1,0:T(8,128)(2,1)S(1)} %get-tuple-element.53), channel_id=1, source_target_pairs={{0,16},{1,17},{2,18},{3,19},{4,6},{5,7},{6,4},{7,5},{8,24},{9,25},... | collective-permute-start | bytes 147464 | tf_op jit(solution)/shard_map/ppermute | solution.py:61
  61.5 3.6 %collective-permute-start.6 = (bf16[48,512]{1,0:T(8,128)(2,1)S(1)}, bf16[48,512]{1,0:T(8,128)(2,1)S(1)}, u32[]{:S(2)}, u32[]{:S(2)}) collective-permute-start(bf16[48,512]{1,0:T(8,128)(2,1)S(1)} %get-tuple-element.54), channel_id=1, source_target_pairs={{0,24},{1,25},{2,26},{3,27},{4,7},{5,4},{6,5},{7,6},{8,0},{9,1},{1... | collective-permute-start | bytes 147464 | tf_op jit(solution)/shard_map/ppermute | solution.py:61
  65.2 3.4 %collective-permute-start.7 = (bf16[80,512]{1,0:T(8,128)(2,1)S(1)}, bf16[80,512]{1,0:T(8,128)(2,1)S(1)}, u32[]{:S(2)}, u32[]{:S(2)}) collective-permute-start(bf16[80,512]{1,0:T(8,128)(2,1)S(1)} %shard_map.127.a), channel_id=1, source_target_pairs={{0,32},{1,33},{2,34},{3,35},{4,36},{5,37},{6,38},{7,39},{8,40},{9,... | collective-permute-start | bytes 245768 | tf_op jit(solution)/shard_map/ppermute | solution.py:61
  68.6 5.6 %collective-permute-start.8 = (bf16[80,512]{1,0:T(8,128)(2,1)S(1)}, bf16[80,512]{1,0:T(8,128)(2,1)S(1)}, u32[]{:S(2)}, u32[]{:S(2)}) collective-permute-start(bf16[80,512]{1,0:T(8,128)(2,1)S(1)} %shard_map.128.before.a), channel_id=1, source_target_pairs={{0,96},{1,97},{2,98},{3,99},{4,100},{5,101},{6,102},{7,103},{8,104... | collective-permute-start | bytes 245768 | tf_op jit(solution)/shard_map/ppermute | solution.py:61
  74.3 5.5 %collective-permute-start.9 = (bf16[80,512]{1,0:T(8,128)(2,1)S(1)}, bf16[80,512]{1,0:T(8,128)(2,1)S(1)}, u32[]{:S(2)}, u32[]{:S(2)}) collective-permute-start(bf16[80,512]{1,0:T(8,128)(2,1)S(1)} %shard_map.130.a), channel_id=1, source_target_pairs={{0,224},{1,225},{2,226},{3,227},{4,228},{5,229},{6,230},{7,231},{8... | collective-permute-start | bytes 245768 | tf_op jit(solution)/shard_map/ppermute | solution.py:61
  79.8 4.6 %collective-permute-start.10 = (bf16[80,512]{1,0:T(8,128)(2,1)S(1)}, bf16[80,512]{1,0:T(8,128)(2,1)S(1)}, u32[]{:S(2)}, u32[]{:S(2)}) collective-permute-start(bf16[80,512]{1,0:T(8,128)(2,1)S(1)} %shard_map.131.own), channel_id=1, source_target_pairs={{0,8},{1,9},{2,10},{3,11},{4,5},{5,6},{6,7},{7,4},{8,16},{9,17},{1... | collective-permute-start | bytes 245768 | tf_op jit(solution)/shard_map/ppermute | solution.py:61
  80.2 5.5 %collective-permute-start.11 = (bf16[80,512]{1,0:T(8,128)(2,1)S(1)}, bf16[80,512]{1,0:T(8,128)(2,1)S(1)}, u32[]{:S(2)}, u32[]{:S(2)}) collective-permute-start(bf16[80,512]{1,0:T(8,128)(2,1)S(1)} %shard_map.131.own), channel_id=1, source_target_pairs={{0,16},{1,17},{2,18},{3,19},{4,6},{5,7},{6,4},{7,5},{8,24},{9,25},... | collective-permute-start | bytes 245768 | tf_op jit(solution)/shard_map/ppermute | solution.py:61
  83.0 3.3 %collective-permute-start.12 = (bf16[80,512]{1,0:T(8,128)(2,1)S(1)}, bf16[80,512]{1,0:T(8,128)(2,1)S(1)}, u32[]{:S(2)}, u32[]{:S(2)}) collective-permute-start(bf16[80,512]{1,0:T(8,128)(2,1)S(1)} %shard_map.131.own), channel_id=1, source_target_pairs={{0,24},{1,25},{2,26},{3,27},{4,7},{5,4},{6,5},{7,6},{8,0},{9,1},{1... | collective-permute-start | bytes 245768 | tf_op jit(solution)/shard_map/ppermute | solution.py:61
  86.3 7.0 %collective-permute-start.13 = (bf16[224,512]{1,0:T(8,128)(2,1)S(1)}, bf16[224,512]{1,0:T(8,128)(2,1)S(1)}, u32[]{:S(2)}, u32[]{:S(2)}) collective-permute-start(bf16[224,512]{1,0:T(8,128)(2,1)S(1)} %shard_map.132.own), channel_id=1, source_target_pairs={{0,1},{1,2},{2,3},{3,0},{4,12},{5,13},{6,14},{7,15},{8,9},{9,10},{... | collective-permute-start | bytes 688136 | tf_op jit(solution)/shard_map/ppermute | solution.py:61
  86.4 9.5 %collective-permute-start.14 = (bf16[224,512]{1,0:T(8,128)(2,1)S(1)}, bf16[224,512]{1,0:T(8,128)(2,1)S(1)}, u32[]{:S(2)}, u32[]{:S(2)}) collective-permute-start(bf16[224,512]{1,0:T(8,128)(2,1)S(1)} %shard_map.132.own), channel_id=1, source_target_pairs={{0,2},{1,3},{2,0},{3,1},{4,20},{5,21},{6,22},{7,23},{8,10},{9,11},... | collective-permute-start | bytes 688136 | tf_op jit(solution)/shard_map/ppermute | solution.py:61
  89.2 7.2 %collective-permute-start.15 = (bf16[224,512]{1,0:T(8,128)(2,1)S(1)}, bf16[224,512]{1,0:T(8,128)(2,1)S(1)}, u32[]{:S(2)}, u32[]{:S(2)}) collective-permute-start(bf16[224,512]{1,0:T(8,128)(2,1)S(1)} %shard_map.132.own), channel_id=1, source_target_pairs={{0,3},{1,0},{2,1},{3,2},{4,28},{5,29},{6,30},{7,31},{8,11},{9,8},{... | collective-permute-start | bytes 688136 | tf_op jit(solution)/shard_map/ppermute | solution.py:61
  96.5 10.2 %collective-permute-start.16 = (bf16[800,512]{1,0:T(8,128)(2,1)S(1)}, bf16[800,512]{1,0:T(8,128)(2,1)S(1)}, u32[]{:S(2)}, u32[]{:S(2)}) collective-permute-start(bf16[800,512]{1,0:T(8,128)(2,1)S(1)} %shard_map.133.own), channel_id=1, source_target_pairs={{0,4},{1,5},{2,6},{3,7},{4,0},{5,1},{6,2},{7,3},{8,12},{9,13},{10,... | collective-permute-start | bytes 2457608 | tf_op jit(solution)/shard_map/ppermute | solution.py:61

commit v5 on v4

--- a/solution.py
+++ b/solution.py
@@ -44,7 +44,7 @@
 
     def along(first, k):
         def move(z, y, c, x):
-            if (c == 0) == first:
+            if (c == 1) == first:
                 return (z, y, c, (x + k) % 4)
             return (z, (y + k) % 4, c, x)
 
@@ -142,12 +142,18 @@
         copy.wait()
 
 
-def k_final(pos, own, got, half, full, conv0, gain, bias, rest, sems):
-    copies = flush(1 - pos[2], full, rest, sems, got, pos[1], pos[0])
+def k_final(pos, own, got, half, full, conv0, gain, bias, rest, sems, conv0_row, gain_row, bias_row, small_sems):
     total = lift(own, 768) + lift(got, 768)
-    conv0[...] = total[0:10]
-    gain[...] = total[10:11]
-    bias[...] = total[11:12]
+    conv0_row[...] = total[0:10]
+    gain_row[...] = total[10:11]
+    bias_row[...] = total[11:12]
+    copies = [
+        pltpu.make_async_copy(source, out, small_sems.at[n])
+        for n, (source, out) in enumerate(((conv0_row, conv0), (gain_row, gain), (bias_row, bias)))
+    ]
+    for copy in copies:
+        copy.start()
+    copies += flush(1 - pos[2], full, rest, sems, got, pos[1], pos[0])
     for copy in copies:
         copy.wait()
 
@@ -155,8 +161,8 @@
 def where_am_i():
     dp, x = lax.axis_index("dp"), lax.axis_index("rep")
     core, y = lax.rem(dp, 2), lax.rem(lax.div(dp, 2), 4)
-    first = jnp.where(core == 0, x, y)
-    second = jnp.where(core == 0, y, x)
+    first = jnp.where(core == 0, y, x)
+    second = jnp.where(core == 0, x, y)
     return jnp.stack([first, second, core]).astype(jnp.int32)
 
 
@@ -196,8 +202,8 @@
         k_final,
         out_shape=[whole] + [jax.ShapeDtypeStruct((n, row), F32) for n in (10, 1, 1)],
         in_specs=[SM, VM, VM, ANY],
-        out_specs=[ANY, VM, VM, VM],
-        scratch_shapes=room,
+        out_specs=[ANY] * 4,
+        scratch_shapes=[*room, *(pltpu.VMEM((n, row), F32) for n in (10, 1, 1)), pltpu.SemaphoreType.DMA((3,))],
         input_output_aliases={3: 0},
         compiler_params=grant,
     )(pos, a, got, half)
@@ -295,7 +301,7 @@
 ):
     spans = panels.shape[0]
     tables(fold, window)
-    arr = arrived[...]
+    arr = arrived[...].astype(F32).reshape(128, WIDE).astype(BF)
     lane = lax.broadcasted_iota(jnp.int32, (128, 128), 1).astype(F32)
     meta = arr[:, 256:384].astype(F32)
     slot = meta[:, SAMPLES - 256 : SAMPLES - 255]
@@ -530,7 +536,6 @@
         limit=60,
     )
     arrived = lax.all_to_all(packed, "dp", split_axis=0, concat_axis=0, tiled=True)
-    arrived = arrived.reshape(2 * devices, WIDE)
     scale = 1.0 / float(lax.axis_size("rep") * devices * spans * frames) ** 0.5
     features, other, mine, backward = encode(
         pos, arrived, conv0_weight, norm_gain, norm_bias, conv1_weight, feature_grad[0], scale

time: 110 us -> 109 us (level)
  starting transfers between devices: 38.2 us -> 42.2 us
  waiting for transfers between devices: 27.5 us -> 24.8 us
    ppermute x17, starting transfers between devices: 24.8 us -> 29.1 us  [send(): return lax.ppermute(value, BOTH, perm)]
    ppermute x17, waiting for transfers between devices: 19.6 us -> 16.7 us  [send(): return lax.ppermute(value, BOTH, perm)]
  transfers between devices with their start and end apart: 18 -> 18, of which waited for: 12 -> 9; matrix products, arithmetic and copies ran while one was open for 2% -> 2% of each run, Pallas kernels for 14% -> 14%
where the time goes in v5:
time: 109 us
  starting transfers between devices  42.2 us (39%)
  Pallas kernels  38.6 us (35%)
  waiting for transfers between devices  24.8 us (23%)
  local copies, waits for them, and re-layouts  2.37 us (2%)
    pallas_call x15, Pallas kernels, call(): pl.pallas_call(kernel, out_shape=shapes, in_specs=specs, out_specs=[VM] *...  35.1 us
    ppermute x17, starting transfers between devices, send(): return lax.ppermute(value, BOTH, perm)  29.1 us
    ppermute x17, waiting for transfers between devices, send(): return lax.ppermute(value, BOTH, perm)  16.7 us
    all_to_all x1, starting transfers between devices, body(): lax.all_to_all(packed, 'dp', split_axis=0, concat_axis=0, tiled=True)  13.2 us
    all_to_all x1, waiting for transfers between devices, body(): lax.all_to_all(packed, 'dp', split_axis=0, concat_axis=0, tiled=True)  8.02 us
    unnamed x9, local copies, waits for them, and re-layouts  2.37 us
  transfers between devices with their start and end apart: 18, of which 9 were waited for; matrix products, arithmetic and copies ran while one was open for 2% of the time, Pallas kernels for 14%

profile of v5, /device:TPU:1, one launch (start us, length us, event | category | flops | bytes accessed | tf_op | source)
XLA Modules:
  0.0 109.1 jit_solution(10921838562767872855)
XLA Ops:
  0.6 1.8 %shard_map.119 = bf16[64,2,384]{2,1,0:T(2,128)(2,1)} custom-call(bf16[48,320]{1,0:T(8,128)(2,1)} %bitcast.21, s32[1,48]{1,0:T(1,128)} %length_in.1, s32[1,48]{1,0:T(1,128)} %target_in.1), custom_call_target="tpu_custom_call" | custom-call | tf_op jit(solution)/shard_map/pallas_call | solution.py:26
  2.4 13.2 %all-to-all-start = ((bf16[64,2,384]{2,1,0:T(2,128)(2,1)}), bf16[64,2,384]{2,1,0:T(2,128)(2,1)S(1)}, u32[]{:S(2)}, u32[]{:S(2)}) async-start(bf16[64,2,384]{2,1,0:T(2,128)(2,1)} %shard_map.119), calls=%async_computation | async-start | bytes 196608 | tf_op jit(solution)/shard_map/all_to_all | solution.py:538
  15.7 2.3 %copy.16 = bf16[1,48,31,512]{3,2,1,0:T(8,128)(2,1)S(1)} copy(bf16[1,48,31,512]{3,1,2,0:T(8,128)(2,1)} %param.15) | data formatting | bytes 3047424 | tf_op args[7]
  18.1 8.0 %all-to-all-done.arrived = bf16[64,2,384]{2,1,0:T(2,128)(2,1)S(1)} async-done(((bf16[64,2,384]{2,1,0:T(2,128)(2,1)}), bf16[64,2,384]{2,1,0:T(2,128)(2,1)S(1)}, u32[]{:S(2)}, u32[]{:S(2)}) %all-to-all-start) | async-done | bytes 98336 | tf_op jit(solution)/shard_map/all_to_all | solution.py:538
  26.2 17.9 %shard_map.121 = (f32[4,1536,128]{2,1,0:T(8,128)S(1)}, f32[48,128]{1,0:T(8,128)S(1)}, bf16[1536,512]{1,0:T(8,128)(2,1)S(1)}, bf16[1536,512]{1,0:T(8,128)(2,1)S(1...) custom-call(s32[3]{0:T(128)S(1)} %pad_add_fusion.pos, ...), custom_call_target="tpu_custom_call" | custom-call | tf_op jit(solution)/shard_map/pallas_call | solution.py:26
  44.6 1.9 %shard_map.122.own = f32[768,512]{1,0:T(8,128)S(1)} custom-call(s32[3]{0:T(128)S(1)} %pad_add_fusion.pos, bf16[1536,512]{1,0:T(8,128)(2,1)S(1)} %get-tuple-element.35.he, bf16[1536,512]{1,0:T(8,128)(2,1)S(1)} %get-tuple-element.36.ho, bf16[1536,512]{1,0:T(8,128)(2,1)S(1)} %get-tuple-element.37.g, bf16[1536,512]{1,0:T(8,128)(2,1)S(1)} %get-tuple-element.38.gs, ...), custom_call_target="tpu_custom_call" | custom-call | tf_op jit(solution)/shard_map/pallas_call | solution.py:26
  46.5 0.7 shard_map.123
  47.2 1.3 %collective-permute-start.1 = (bf16[192,512]{1,0:T(8,128)(2,1)S(1)}, bf16[192,512]{1,0:T(8,128)(2,1)S(1)}, u32[]{:S(2)}, u32[]{:S(2)}) collective-permute-start(bf16[192,512]{1,0:T(8,128)(2,1)S(1)} %get-tuple-element.41), channel_id=1, source_target_pairs={{0,8},{1,9},{2,10},{3,11},{4,5},{5,6},{6,7},{7,4},{8,16},{9,17},{1... | collective-permute-start | bytes 589832 | tf_op jit(solution)/shard_map/ppermute | solution.py:61
  48.5 2.5 %collective-permute-start.2 = (bf16[192,512]{1,0:T(8,128)(2,1)S(1)}, bf16[192,512]{1,0:T(8,128)(2,1)S(1)}, u32[]{:S(2)}, u32[]{:S(2)}) collective-permute-start(bf16[192,512]{1,0:T(8,128)(2,1)S(1)} %get-tuple-element.42), channel_id=1, source_target_pairs={{0,16},{1,17},{2,18},{3,19},{4,6},{5,7},{6,4},{7,5},{8,24},{9,25},... | collective-permute-start | bytes 589832 | tf_op jit(solution)/shard_map/ppermute | solution.py:61
  50.9 1.1 %collective-permute-start.3 = (bf16[192,512]{1,0:T(8,128)(2,1)S(1)}, bf16[192,512]{1,0:T(8,128)(2,1)S(1)}, u32[]{:S(2)}, u32[]{:S(2)}) collective-permute-start(bf16[192,512]{1,0:T(8,128)(2,1)S(1)} %get-tuple-element.43), channel_id=1, source_target_pairs={{0,24},{1,25},{2,26},{3,27},{4,7},{5,4},{6,5},{7,6},{8,0},{9,1},{1... | collective-permute-start | bytes 589832 | tf_op jit(solution)/shard_map/ppermute | solution.py:61
  52.1 4.7 %shard_map.124.before.start = f32[16,512]{1,0:T(8,128)S(1)} custom-call(bf16[1536,512]{1,0:T(8,128)(2,1)S(1)} %get-tuple-element.37.g, bf16[1536,512]{1,0:T(8,128)(2,1)S(1)} %get-tuple-element.38.gs, bf16[1536,512]{1,0:T(8,128)(2,1)S(1)} %get-tuple-element.44.se, bf16[1536,512]{1,0:T(8,128)(2,1)S(1)} %get-tuple-element.45.so, ...), custom_call_target="tpu_custom_call" | custom-call | tf_op jit(solution)/shard_map/pallas_call | solution.py:26
  56.9 0.6 shard_map.125
  58.0 1.4 %collective-permute-start.5 = (bf16[48,512]{1,0:T(8,128)(2,1)S(1)}, bf16[48,512]{1,0:T(8,128)(2,1)S(1)}, u32[]{:S(2)}, u32[]{:S(2)}) collective-permute-start(bf16[48,512]{1,0:T(8,128)(2,1)S(1)} %get-tuple-element.53), channel_id=1, source_target_pairs={{0,2},{1,3},{2,0},{3,1},{4,20},{5,21},{6,22},{7,23},{8,10},{9,11},... | collective-permute-start | bytes 147464 | tf_op jit(solution)/shard_map/ppermute | solution.py:61
  59.4 1.6 %collective-permute-start.6 = (bf16[48,512]{1,0:T(8,128)(2,1)S(1)}, bf16[48,512]{1,0:T(8,128)(2,1)S(1)}, u32[]{:S(2)}, u32[]{:S(2)}) collective-permute-start(bf16[48,512]{1,0:T(8,128)(2,1)S(1)} %get-tuple-element.54), channel_id=1, source_target_pairs={{0,3},{1,0},{2,1},{3,2},{4,28},{5,29},{6,30},{7,31},{8,11},{9,8},{... | collective-permute-start | bytes 147464 | tf_op jit(solution)/shard_map/ppermute | solution.py:61
  60.9 2.4 %shard_map.126.small = f32[16,512]{1,0:T(8,128)S(1)} custom-call(bf16[1536,512]{1,0:T(8,128)(2,1)S(1)} %get-tuple-element.37.g, bf16[1536,512]{1,0:T(8,128)(2,1)S(1)} %get-tuple-element.38.gs, bf16[1536,512]{1,0:T(8,128)(2,1)S(1)} %get-tuple-element.44.se, bf16[1536,512]{1,0:T(8,128)(2,1)S(1)} %get-tuple-element.45.so, ...), custom_call_target="tpu_custom_call" | custom-call | tf_op jit(solution)/shard_map/pallas_call | solution.py:26
  63.5 0.5 collective-permute-start.7
  64.0 2.8 %collective-permute-done.7.b = bf16[80,512]{1,0:T(8,128)(2,1)S(1)} collective-permute-done((bf16[80,512]{1,0:T(8,128)(2,1)S(1)}, bf16[80,512]{1,0:T(8,128)(2,1)S(1)}, u32[]{:S(2)}, u32[]{:S(2)}) %collective-permute-start.7) | collective-permute-done | bytes 81952 | tf_op jit(solution)/shard_map/ppermute | solution.py:61
  66.9 0.7 collective-permute-start.8
  67.6 4.8 %shard_map.129 = (bf16[31,48,512]{2,1,0:T(8,128)(2,1)}, f32[8,128]{1,0:T(8,128)S(1)}) custom-call(f32[4,1536,128]{2,1,0:T(8,128)S(1)} %get-tuple-element.33.pre1, f32[48,128]{1,0:T(8,128)S(1)} %get-tuple-element.34.count, bf16[80,512]{1,0:T(8,128)(2,1)S(1)} %shard_map.128.before.a), custom_call_target="tpu_custom_call" | custom-call | tf_op jit(solution)/shard_map/pallas_call | solution.py:26
  72.7 4.4 %collective-permute-done.9.b = bf16[80,512]{1,0:T(8,128)(2,1)S(1)} collective-permute-done((bf16[80,512]{1,0:T(8,128)(2,1)S(1)}, bf16[80,512]{1,0:T(8,128)(2,1)S(1)}, u32[]{:S(2)}, u32[]{:S(2)}) %collective-permute-start.9) | collective-permute-done | bytes 81952 | tf_op jit(solution)/shard_map/ppermute | solution.py:61
  77.2 1.7 %collective-permute-start.10 = (bf16[80,512]{1,0:T(8,128)(2,1)S(1)}, bf16[80,512]{1,0:T(8,128)(2,1)S(1)}, u32[]{:S(2)}, u32[]{:S(2)}) collective-permute-start(bf16[80,512]{1,0:T(8,128)(2,1)S(1)} %shard_map.131.own), channel_id=1, source_target_pairs={{0,1},{1,2},{2,3},{3,0},{4,12},{5,13},{6,14},{7,15},{8,9},{9,10},{... | collective-permute-start | bytes 245768 | tf_op jit(solution)/shard_map/ppermute | solution.py:61
  78.9 1.9 %collective-permute-start.11 = (bf16[80,512]{1,0:T(8,128)(2,1)S(1)}, bf16[80,512]{1,0:T(8,128)(2,1)S(1)}, u32[]{:S(2)}, u32[]{:S(2)}) collective-permute-start(bf16[80,512]{1,0:T(8,128)(2,1)S(1)} %shard_map.131.own), channel_id=1, source_target_pairs={{0,2},{1,3},{2,0},{3,1},{4,20},{5,21},{6,22},{7,23},{8,10},{9,11},... | collective-permute-start | bytes 245768 | tf_op jit(solution)/shard_map/ppermute | solution.py:61
  80.8 1.2 %collective-permute-start.12 = (bf16[80,512]{1,0:T(8,128)(2,1)S(1)}, bf16[80,512]{1,0:T(8,128)(2,1)S(1)}, u32[]{:S(2)}, u32[]{:S(2)}) collective-permute-start(bf16[80,512]{1,0:T(8,128)(2,1)S(1)} %shard_map.131.own), channel_id=1, source_target_pairs={{0,3},{1,0},{2,1},{3,2},{4,28},{5,29},{6,30},{7,31},{8,11},{9,8},{... | collective-permute-start | bytes 245768 | tf_op jit(solution)/shard_map/ppermute | solution.py:61
  82.1 1.6 %collective-permute-done.11.r2 = bf16[80,512]{1,0:T(8,128)(2,1)S(1)} collective-permute-done((bf16[80,512]{1,0:T(8,128)(2,1)S(1)}, bf16[80,512]{1,0:T(8,128)(2,1)S(1)}, u32[]{:S(2)}, u32[]{:S(2)}) %collective-permute-start.11) | collective-permute-done | bytes 81952 | tf_op jit(solution)/shard_map/ppermute | solution.py:61
  84.2 0.9 collective-permute-start.13
  85.1 2.9 %collective-permute-start.14 = (bf16[224,512]{1,0:T(8,128)(2,1)S(1)}, bf16[224,512]{1,0:T(8,128)(2,1)S(1)}, u32[]{:S(2)}, u32[]{:S(2)}) collective-permute-start(bf16[224,512]{1,0:T(8,128)(2,1)S(1)} %shard_map.132.own), channel_id=1, source_target_pairs={{0,16},{1,17},{2,18},{3,19},{4,6},{5,7},{6,4},{7,5},{8,24},{9,25},... | collective-permute-start | bytes 688136 | tf_op jit(solution)/shard_map/ppermute | solution.py:61
  88.0 0.5 collective-permute-start.15
  88.5 2.7 %collective-permute-done.13.r1 = bf16[224,512]{1,0:T(8,128)(2,1)S(1)} collective-permute-done((bf16[224,512]{1,0:T(8,128)(2,1)S(1)}, bf16[224,512]{1,0:T(8,128)(2,1)S(1)}, u32[]{:S(2)}, u32[]{:S(2)}) %collective-permute-start.13) | collective-permute-done | bytes 229408 | tf_op jit(solution)/shard_map/ppermute | solution.py:61
  91.2 4.4 %collective-permute-done.14.r2 = bf16[224,512]{1,0:T(8,128)(2,1)S(1)} collective-permute-done((bf16[224,512]{1,0:T(8,128)(2,1)S(1)}, bf16[224,512]{1,0:T(8,128)(2,1)S(1)}, u32[]{:S(2)}, u32[]{:S(2)}) %collective-permute-start.14) | collective-permute-done | bytes 229408 | tf_op jit(solution)/shard_map/ppermute | solution.py:61
  95.7 9.5 %collective-permute-start.16 = (bf16[800,512]{1,0:T(8,128)(2,1)S(1)}, bf16[800,512]{1,0:T(8,128)(2,1)S(1)}, u32[]{:S(2)}, u32[]{:S(2)}) collective-permute-start(bf16[800,512]{1,0:T(8,128)(2,1)S(1)} %shard_map.133.own), channel_id=1, source_target_pairs={{0,4},{1,5},{2,6},{3,7},{4,0},{5,1},{6,2},{7,3},{8,12},{9,13},{10,... | collective-permute-start | bytes 2457608 | tf_op jit(solution)/shard_map/ppermute | solution.py:61
  105.2 1.7 %shard_map.134.half = f32[1536,512]{1,0:T(8,128)} custom-call(s32[3]{0:T(128)S(1)} %pad_add_fusion.pos, bf16[800,512]{1,0:T(8,128)(2,1)S(1)} %shard_map.133.own), custom_call_target="tpu_custom_call" | custom-call | tf_op jit(solution)/shard_map/pallas_call | solution.py:198
  107.2 1.8 %shard_map.135 = (f32[1536,512]{1,0:T(8,128)}, f32[10,512]{1,0:T(8,128)}, f32[1,512]{1,0:T(1,128)}, f32[1,512]{1,0:T(1,128)}) custom-call(s32[3]{0:T(128)S(1)} %pad_add_fusion.pos, bf16[800,512]{1,0:T(8,128)(2,1)S(1)} %shard_map.133.own, bf16[800,512]{1,0:T(8,128)(2,1)S(1)} %collective-permute-done.16.got, ...), custom_call_target="tpu_custom_call", output_to_operand_aliasing={{0}: (3, {})} | custom-call | tf_op jit(solution)/shard_map/pallas_call | solution.py:201
  (32 shorter events, 2.4 us)
Async XLA Ops:
  2.4 23.7 %all-to-all-start = ((bf16[64,2,384]{2,1,0:T(2,128)(2,1)}), bf16[64,2,384]{2,1,0:T(2,128)(2,1)S(1)}, u32[]{:S(2)}, u32[]{:S(2)}) async-start(bf16[64,2,384]{2,1,0:T(2,128)(2,1)} %shard_map.119), calls=%async_computation | async-start | bytes 196608 | tf_op jit(solution)/shard_map/all_to_all | solution.py:538
  15.6 2.4 %copy-start.2 = (bf16[10,512]{1,0:T(8,128)(2,1)S(1)}, bf16[10,512]{1,0:T(8,128)(2,1)}, u32[]{:S(2)}) copy-start(bf16[10,512]{1,0:T(8,128)(2,1)} %conv0.1) | copy-start | bytes 30724
  15.6 10.5 %copy-start = (bf16[3,512,512]{2,1,0:T(8,128)(2,1)S(1)}, bf16[3,512,512]{2,1,0:T(8,128)(2,1)}, u32[]{:S(2)}) copy-start(bf16[3,512,512]{2,1,0:T(8,128)(2,1)} %weight.5) | copy-start | bytes 4718596
  15.6 10.5 %copy-start.1 = (f32[512]{0:T(512)S(1)}, f32[512]{0:T(512)}, u32[]{:S(2)}) copy-start(f32[512]{0:T(512)} %param.12) | copy-start | bytes 6148
  15.6 10.5 %copy-start.3 = (f32[512]{0:T(512)S(1)}, f32[512]{0:T(512)}, u32[]{:S(2)}) copy-start(f32[512]{0:T(512)} %param.13) | copy-start | bytes 6148
  44.1 2.4 %collective-permute-start = (bf16[768,512]{1,0:T(8,128)(2,1)S(1)}, bf16[768,512]{1,0:T(8,128)(2,1)S(1)}, u32[]{:S(2)}, u32[]{:S(2)}) collective-permute-start(bf16[768,512]{1,0:T(8,128)(2,1)S(1)} %get-tuple-element.39.before), channel_id=1, source_target_pairs={{0,4},{1,5},{2,6},{3,7},{4,0},{5,1},{6,2},{7,3},{8,12},{9,13},{10,... | collective-permute-start | bytes 2359304 | tf_op jit(solution)/shard_map/ppermute | solution.py:61
  47.2 9.6 %collective-permute-start.1 = (bf16[192,512]{1,0:T(8,128)(2,1)S(1)}, bf16[192,512]{1,0:T(8,128)(2,1)S(1)}, u32[]{:S(2)}, u32[]{:S(2)}) collective-permute-start(bf16[192,512]{1,0:T(8,128)(2,1)S(1)} %get-tuple-element.41), channel_id=1, source_target_pairs={{0,8},{1,9},{2,10},{3,11},{4,5},{5,6},{6,7},{7,4},{8,16},{9,17},{1... | collective-permute-start | bytes 589832 | tf_op jit(solution)/shard_map/ppermute | solution.py:61
  48.5 8.3 %collective-permute-start.2 = (bf16[192,512]{1,0:T(8,128)(2,1)S(1)}, bf16[192,512]{1,0:T(8,128)(2,1)S(1)}, u32[]{:S(2)}, u32[]{:S(2)}) collective-permute-start(bf16[192,512]{1,0:T(8,128)(2,1)S(1)} %get-tuple-element.42), channel_id=1, source_target_pairs={{0,16},{1,17},{2,18},{3,19},{4,6},{5,7},{6,4},{7,5},{8,24},{9,25},... | collective-permute-start | bytes 589832 | tf_op jit(solution)/shard_map/ppermute | solution.py:61
  50.9 5.9 %collective-permute-start.3 = (bf16[192,512]{1,0:T(8,128)(2,1)S(1)}, bf16[192,512]{1,0:T(8,128)(2,1)S(1)}, u32[]{:S(2)}, u32[]{:S(2)}) collective-permute-start(bf16[192,512]{1,0:T(8,128)(2,1)S(1)} %get-tuple-element.43), channel_id=1, source_target_pairs={{0,24},{1,25},{2,26},{3,27},{4,7},{5,4},{6,5},{7,6},{8,0},{9,1},{1... | collective-permute-start | bytes 589832 | tf_op jit(solution)/shard_map/ppermute | solution.py:61
  57.5 5.9 %collective-permute-start.4 = (bf16[48,512]{1,0:T(8,128)(2,1)S(1)}, bf16[48,512]{1,0:T(8,128)(2,1)S(1)}, u32[]{:S(2)}, u32[]{:S(2)}) collective-permute-start(bf16[48,512]{1,0:T(8,128)(2,1)S(1)} %get-tuple-element.52), channel_id=1, source_target_pairs={{0,1},{1,2},{2,3},{3,0},{4,12},{5,13},{6,14},{7,15},{8,9},{9,10},{... | collective-permute-start | bytes 147464 | tf_op jit(solution)/shard_map/ppermute | solution.py:61
  58.0 5.4 %collective-permute-start.5 = (bf16[48,512]{1,0:T(8,128)(2,1)S(1)}, bf16[48,512]{1,0:T(8,128)(2,1)S(1)}, u32[]{:S(2)}, u32[]{:S(2)}) collective-permute-start(bf16[48,512]{1,0:T(8,128)(2,1)S(1)} %get-tuple-element.53), channel_id=1, source_target_pairs={{0,2},{1,3},{2,0},{3,1},{4,20},{5,21},{6,22},{7,23},{8,10},{9,11},... | collective-permute-start | bytes 147464 | tf_op jit(solution)/shard_map/ppermute | solution.py:61
  59.4 4.0 %collective-permute-start.6 = (bf16[48,512]{1,0:T(8,128)(2,1)S(1)}, bf16[48,512]{1,0:T(8,128)(2,1)S(1)}, u32[]{:S(2)}, u32[]{:S(2)}) collective-permute-start(bf16[48,512]{1,0:T(8,128)(2,1)S(1)} %get-tuple-element.54), channel_id=1, source_target_pairs={{0,3},{1,0},{2,1},{3,2},{4,28},{5,29},{6,30},{7,31},{8,11},{9,8},{... | collective-permute-start | bytes 147464 | tf_op jit(solution)/shard_map/ppermute | solution.py:61
  63.5 3.4 %collective-permute-start.7 = (bf16[80,512]{1,0:T(8,128)(2,1)S(1)}, bf16[80,512]{1,0:T(8,128)(2,1)S(1)}, u32[]{:S(2)}, u32[]{:S(2)}) collective-permute-start(bf16[80,512]{1,0:T(8,128)(2,1)S(1)} %shard_map.127.a), channel_id=1, source_target_pairs={{0,32},{1,33},{2,34},{3,35},{4,36},{5,37},{6,38},{7,39},{8,40},{9,... | collective-permute-start | bytes 245768 | tf_op jit(solution)/shard_map/ppermute | solution.py:61
  66.9 5.5 %collective-permute-start.8 = (bf16[80,512]{1,0:T(8,128)(2,1)S(1)}, bf16[80,512]{1,0:T(8,128)(2,1)S(1)}, u32[]{:S(2)}, u32[]{:S(2)}) collective-permute-start(bf16[80,512]{1,0:T(8,128)(2,1)S(1)} %shard_map.128.before.a), channel_id=1, source_target_pairs={{0,96},{1,97},{2,98},{3,99},{4,100},{5,101},{6,102},{7,103},{8,104... | collective-permute-start | bytes 245768 | tf_op jit(solution)/shard_map/ppermute | solution.py:61
  72.4 4.8 %collective-permute-start.9 = (bf16[80,512]{1,0:T(8,128)(2,1)S(1)}, bf16[80,512]{1,0:T(8,128)(2,1)S(1)}, u32[]{:S(2)}, u32[]{:S(2)}) collective-permute-start(bf16[80,512]{1,0:T(8,128)(2,1)S(1)} %shard_map.130.a), channel_id=1, source_target_pairs={{0,224},{1,225},{2,226},{3,227},{4,228},{5,229},{6,230},{7,231},{8... | collective-permute-start | bytes 245768 | tf_op jit(solution)/shard_map/ppermute | solution.py:61
  77.2 4.9 %collective-permute-start.10 = (bf16[80,512]{1,0:T(8,128)(2,1)S(1)}, bf16[80,512]{1,0:T(8,128)(2,1)S(1)}, u32[]{:S(2)}, u32[]{:S(2)}) collective-permute-start(bf16[80,512]{1,0:T(8,128)(2,1)S(1)} %shard_map.131.own), channel_id=1, source_target_pairs={{0,1},{1,2},{2,3},{3,0},{4,12},{5,13},{6,14},{7,15},{8,9},{9,10},{... | collective-permute-start | bytes 245768 | tf_op jit(solution)/shard_map/ppermute | solution.py:61
  78.9 4.8 %collective-permute-start.11 = (bf16[80,512]{1,0:T(8,128)(2,1)S(1)}, bf16[80,512]{1,0:T(8,128)(2,1)S(1)}, u32[]{:S(2)}, u32[]{:S(2)}) collective-permute-start(bf16[80,512]{1,0:T(8,128)(2,1)S(1)} %shard_map.131.own), channel_id=1, source_target_pairs={{0,2},{1,3},{2,0},{3,1},{4,20},{5,21},{6,22},{7,23},{8,10},{9,11},... | collective-permute-start | bytes 245768 | tf_op jit(solution)/shard_map/ppermute | solution.py:61
  80.8 3.3 %collective-permute-start.12 = (bf16[80,512]{1,0:T(8,128)(2,1)S(1)}, bf16[80,512]{1,0:T(8,128)(2,1)S(1)}, u32[]{:S(2)}, u32[]{:S(2)}) collective-permute-start(bf16[80,512]{1,0:T(8,128)(2,1)S(1)} %shard_map.131.own), channel_id=1, source_target_pairs={{0,3},{1,0},{2,1},{3,2},{4,28},{5,29},{6,30},{7,31},{8,11},{9,8},{... | collective-permute-start | bytes 245768 | tf_op jit(solution)/shard_map/ppermute | solution.py:61
  84.2 7.1 %collective-permute-start.13 = (bf16[224,512]{1,0:T(8,128)(2,1)S(1)}, bf16[224,512]{1,0:T(8,128)(2,1)S(1)}, u32[]{:S(2)}, u32[]{:S(2)}) collective-permute-start(bf16[224,512]{1,0:T(8,128)(2,1)S(1)} %shard_map.132.own), channel_id=1, source_target_pairs={{0,8},{1,9},{2,10},{3,11},{4,5},{5,6},{6,7},{7,4},{8,16},{9,17},{1... | collective-permute-start | bytes 688136 | tf_op jit(solution)/shard_map/ppermute | solution.py:61
  85.1 10.5 %collective-permute-start.14 = (bf16[224,512]{1,0:T(8,128)(2,1)S(1)}, bf16[224,512]{1,0:T(8,128)(2,1)S(1)}, u32[]{:S(2)}, u32[]{:S(2)}) collective-permute-start(bf16[224,512]{1,0:T(8,128)(2,1)S(1)} %shard_map.132.own), channel_id=1, source_target_pairs={{0,16},{1,17},{2,18},{3,19},{4,6},{5,7},{6,4},{7,5},{8,24},{9,25},... | collective-permute-start | bytes 688136 | tf_op jit(solution)/shard_map/ppermute | solution.py:61
  88.0 7.6 %collective-permute-start.15 = (bf16[224,512]{1,0:T(8,128)(2,1)S(1)}, bf16[224,512]{1,0:T(8,128)(2,1)S(1)}, u32[]{:S(2)}, u32[]{:S(2)}) collective-permute-start(bf16[224,512]{1,0:T(8,128)(2,1)S(1)} %shard_map.132.own), channel_id=1, source_target_pairs={{0,24},{1,25},{2,26},{3,27},{4,7},{5,4},{6,5},{7,6},{8,0},{9,1},{1... | collective-permute-start | bytes 688136 | tf_op jit(solution)/shard_map/ppermute | solution.py:61
  95.7 11.5 %collective-permute-start.16 = (bf16[800,512]{1,0:T(8,128)(2,1)S(1)}, bf16[800,512]{1,0:T(8,128)(2,1)S(1)}, u32[]{:S(2)}, u32[]{:S(2)}) collective-permute-start(bf16[800,512]{1,0:T(8,128)(2,1)S(1)} %shard_map.133.own), channel_id=1, source_target_pairs={{0,4},{1,5},{2,6},{3,7},{4,0},{5,1},{6,2},{7,3},{8,12},{9,13},{10,... | collective-permute-start | bytes 2457608 | tf_op jit(solution)/shard_map/ppermute | solution.py:61

commit v6 on v5

--- a/solution.py
+++ b/solution.py
@@ -255,7 +255,7 @@
     return cumul, density
 
 
-BLOCK = 8
+BLOCK = 16
 BACK = 16
 ROWS = 32 * BLOCK
 
@@ -332,7 +332,7 @@
                 am[rows, pl.ds(t * 128, 128)] = part.astype(BF)
             return carry
 
-        lax.fori_loop(0, BLOCK, patch, 0, unroll=2)
+        lax.fori_loop(0, BLOCK, patch, 0, unroll=BLOCK)
         every = pl.ds(pl.multiple_of(b * ROWS, ROWS), ROWS)
         xs = jnp.dot(am[...], fold[...], preferred_element_type=F32).astype(BF)
         x[every, :] = xs
@@ -394,7 +394,7 @@
                 gs[at, cols] = pltpu.roll(grad, 1, 0).astype(BF)
             return carry
 
-        lax.fori_loop(0, BLOCK, second, 0, unroll=2)
+        lax.fori_loop(0, BLOCK, second, 0, unroll=BLOCK)
         return carry
 
     lax.fori_loop(0, spans // BLOCK, block, 0)
@@ -430,7 +430,7 @@
             feats[t, :, cols] = jnp.where(keep, value * cumul, 0.0).astype(BF)
         return carry
 
-    lax.fori_loop(0, feats.shape[0], frame, 0)
+    lax.fori_loop(0, feats.shape[0], frame, 0, unroll=True)
 
 
 def k_backward(
@@ -467,7 +467,7 @@
                 dxo[here, cols] = ((po - plain - o * mixed) * lead).astype(BF)
             return carry
 
-        lax.fori_loop(0, BACK, back, 0, unroll=2)
+        lax.fori_loop(0, BACK, back, 0, unroll=BACK)
         return carry
 
     lax.fori_loop(0, blocks, block, 0)

time: 109 us -> 107 us (0.982)
  Pallas kernels: 38.6 us -> 35.2 us
  waiting for transfers between devices: 24.8 us -> 27.5 us
  starting transfers between devices: 42.2 us -> 40.7 us
    pallas_call x15, Pallas kernels: 35.1 us -> 31.7 us  [call(): pl.pallas_call(kernel, out_shape=shapes, in_specs=specs, out_specs=[VM] *...]
    ppermute x17, waiting for transfers between devices: 16.7 us -> 19.5 us  [send(): return lax.ppermute(value, BOTH, perm)]
    ppermute x17, starting transfers between devices: 29.1 us -> 27.5 us  [send(): return lax.ppermute(value, BOTH, perm)]
  transfers between devices with their start and end apart: 18 -> 18, of which waited for: 9 -> 11; matrix products, arithmetic and copies ran while one was open for 2% -> 2% of each run, Pallas kernels for 14% -> 13%
where the time goes in v6:
time: 107 us
  starting transfers between devices  40.7 us (38%)
  Pallas kernels  35.2 us (33%)
  waiting for transfers between devices  27.5 us (26%)
  local copies, waits for them, and re-layouts  2.37 us (2%)
    pallas_call x15, Pallas kernels, call(): pl.pallas_call(kernel, out_shape=shapes, in_specs=specs, out_specs=[VM] *...  31.7 us
    ppermute x17, starting transfers between devices, send(): return lax.ppermute(value, BOTH, perm)  27.5 us
    ppermute x17, waiting for transfers between devices, send(): return lax.ppermute(value, BOTH, perm)  19.5 us
    all_to_all x1, starting transfers between devices, body(): lax.all_to_all(packed, 'dp', split_axis=0, concat_axis=0, tiled=True)  13.2 us
    all_to_all x1, waiting for transfers between devices, body(): lax.all_to_all(packed, 'dp', split_axis=0, concat_axis=0, tiled=True)  8.02 us
    unnamed x9, local copies, waits for them, and re-layouts  2.37 us
  transfers between devices with their start and end apart: 18, of which 11 were waited for; matrix products, arithmetic and copies ran while one was open for 2% of the time, Pallas kernels for 13%

profile of v6, /device:TPU:1, one launch (start us, length us, event | category | flops | bytes accessed | tf_op | source)
XLA Modules:
  0.0 106.9 jit_solution(8292976562254784254)
XLA Ops:
  0.6 1.8 %shard_map.119 = bf16[64,2,384]{2,1,0:T(2,128)(2,1)} custom-call(bf16[48,320]{1,0:T(8,128)(2,1)} %bitcast.21, s32[1,48]{1,0:T(1,128)} %length_in.1, s32[1,48]{1,0:T(1,128)} %target_in.1), custom_call_target="tpu_custom_call" | custom-call | tf_op jit(solution)/shard_map/pallas_call | solution.py:26
  2.4 13.2 %all-to-all-start = ((bf16[64,2,384]{2,1,0:T(2,128)(2,1)}), bf16[64,2,384]{2,1,0:T(2,128)(2,1)S(1)}, u32[]{:S(2)}, u32[]{:S(2)}) async-start(bf16[64,2,384]{2,1,0:T(2,128)(2,1)} %shard_map.119), calls=%async_computation | async-start | bytes 196608 | tf_op jit(solution)/shard_map/all_to_all | solution.py:538
  15.7 2.3 %copy.16 = bf16[1,48,31,512]{3,2,1,0:T(8,128)(2,1)S(1)} copy(bf16[1,48,31,512]{3,1,2,0:T(8,128)(2,1)} %param.15) | data formatting | bytes 3047424 | tf_op args[7]
  18.1 8.0 %all-to-all-done.arrived = bf16[64,2,384]{2,1,0:T(2,128)(2,1)S(1)} async-done(((bf16[64,2,384]{2,1,0:T(2,128)(2,1)}), bf16[64,2,384]{2,1,0:T(2,128)(2,1)S(1)}, u32[]{:S(2)}, u32[]{:S(2)}) %all-to-all-start) | async-done | bytes 98336 | tf_op jit(solution)/shard_map/all_to_all | solution.py:538
  26.2 16.1 %shard_map.121 = (f32[4,1536,128]{2,1,0:T(8,128)S(1)}, f32[48,128]{1,0:T(8,128)S(1)}, bf16[1536,512]{1,0:T(8,128)(2,1)S(1)}, bf16[1536,512]{1,0:T(8,128)(2,1)S(1...) custom-call(s32[3]{0:T(128)S(1)} %pad_add_fusion.pos, ...), custom_call_target="tpu_custom_call" | custom-call | tf_op jit(solution)/shard_map/pallas_call | solution.py:26
  42.2 0.5 collective-permute-start
  42.7 2.0 %shard_map.122.own = f32[768,512]{1,0:T(8,128)S(1)} custom-call(s32[3]{0:T(128)S(1)} %pad_add_fusion.pos, bf16[1536,512]{1,0:T(8,128)(2,1)S(1)} %get-tuple-element.35.he, bf16[1536,512]{1,0:T(8,128)(2,1)S(1)} %get-tuple-element.36.ho, bf16[1536,512]{1,0:T(8,128)(2,1)S(1)} %get-tuple-element.37.g, bf16[1536,512]{1,0:T(8,128)(2,1)S(1)} %get-tuple-element.38.gs, ...), custom_call_target="tpu_custom_call" | custom-call | tf_op jit(solution)/shard_map/pallas_call | solution.py:26
  44.7 0.7 shard_map.123
  45.4 1.3 %collective-permute-start.1 = (bf16[192,512]{1,0:T(8,128)(2,1)S(1)}, bf16[192,512]{1,0:T(8,128)(2,1)S(1)}, u32[]{:S(2)}, u32[]{:S(2)}) collective-permute-start(bf16[192,512]{1,0:T(8,128)(2,1)S(1)} %get-tuple-element.41), channel_id=1, source_target_pairs={{0,8},{1,9},{2,10},{3,11},{4,5},{5,6},{6,7},{7,4},{8,16},{9,17},{1... | collective-permute-start | bytes 589832 | tf_op jit(solution)/shard_map/ppermute | solution.py:61
  46.6 2.5 %collective-permute-start.2 = (bf16[192,512]{1,0:T(8,128)(2,1)S(1)}, bf16[192,512]{1,0:T(8,128)(2,1)S(1)}, u32[]{:S(2)}, u32[]{:S(2)}) collective-permute-start(bf16[192,512]{1,0:T(8,128)(2,1)S(1)} %get-tuple-element.42), channel_id=1, source_target_pairs={{0,16},{1,17},{2,18},{3,19},{4,6},{5,7},{6,4},{7,5},{8,24},{9,25},... | collective-permute-start | bytes 589832 | tf_op jit(solution)/shard_map/ppermute | solution.py:61
  49.1 1.1 %collective-permute-start.3 = (bf16[192,512]{1,0:T(8,128)(2,1)S(1)}, bf16[192,512]{1,0:T(8,128)(2,1)S(1)}, u32[]{:S(2)}, u32[]{:S(2)}) collective-permute-start(bf16[192,512]{1,0:T(8,128)(2,1)S(1)} %get-tuple-element.43), channel_id=1, source_target_pairs={{0,24},{1,25},{2,26},{3,27},{4,7},{5,4},{6,5},{7,6},{8,0},{9,1},{1... | collective-permute-start | bytes 589832 | tf_op jit(solution)/shard_map/ppermute | solution.py:61
  50.2 4.2 %shard_map.124.before.start = f32[16,512]{1,0:T(8,128)S(1)} custom-call(bf16[1536,512]{1,0:T(8,128)(2,1)S(1)} %get-tuple-element.37.g, bf16[1536,512]{1,0:T(8,128)(2,1)S(1)} %get-tuple-element.38.gs, bf16[1536,512]{1,0:T(8,128)(2,1)S(1)} %get-tuple-element.44.se, bf16[1536,512]{1,0:T(8,128)(2,1)S(1)} %get-tuple-element.45.so, ...), custom_call_target="tpu_custom_call" | custom-call | tf_op jit(solution)/shard_map/pallas_call | solution.py:26
  54.4 0.6 shard_map.125
  55.4 1.5 %collective-permute-start.5 = (bf16[48,512]{1,0:T(8,128)(2,1)S(1)}, bf16[48,512]{1,0:T(8,128)(2,1)S(1)}, u32[]{:S(2)}, u32[]{:S(2)}) collective-permute-start(bf16[48,512]{1,0:T(8,128)(2,1)S(1)} %get-tuple-element.53), channel_id=1, source_target_pairs={{0,2},{1,3},{2,0},{3,1},{4,20},{5,21},{6,22},{7,23},{8,10},{9,11},... | collective-permute-start | bytes 147464 | tf_op jit(solution)/shard_map/ppermute | solution.py:61
  56.9 1.5 %collective-permute-start.6 = (bf16[48,512]{1,0:T(8,128)(2,1)S(1)}, bf16[48,512]{1,0:T(8,128)(2,1)S(1)}, u32[]{:S(2)}, u32[]{:S(2)}) collective-permute-start(bf16[48,512]{1,0:T(8,128)(2,1)S(1)} %get-tuple-element.54), channel_id=1, source_target_pairs={{0,3},{1,0},{2,1},{3,2},{4,28},{5,29},{6,30},{7,31},{8,11},{9,8},{... | collective-permute-start | bytes 147464 | tf_op jit(solution)/shard_map/ppermute | solution.py:61
  58.4 2.2 %shard_map.126.small = f32[16,512]{1,0:T(8,128)S(1)} custom-call(bf16[1536,512]{1,0:T(8,128)(2,1)S(1)} %get-tuple-element.37.g, bf16[1536,512]{1,0:T(8,128)(2,1)S(1)} %get-tuple-element.38.gs, bf16[1536,512]{1,0:T(8,128)(2,1)S(1)} %get-tuple-element.44.se, bf16[1536,512]{1,0:T(8,128)(2,1)S(1)} %get-tuple-element.45.so, ...), custom_call_target="tpu_custom_call" | custom-call | tf_op jit(solution)/shard_map/pallas_call | solution.py:26
  61.2 3.1 %collective-permute-done.7.b = bf16[80,512]{1,0:T(8,128)(2,1)S(1)} collective-permute-done((bf16[80,512]{1,0:T(8,128)(2,1)S(1)}, bf16[80,512]{1,0:T(8,128)(2,1)S(1)}, u32[]{:S(2)}, u32[]{:S(2)}) %collective-permute-start.7) | collective-permute-done | bytes 81952 | tf_op jit(solution)/shard_map/ppermute | solution.py:61
  64.3 0.9 collective-permute-start.8
  65.1 4.0 %shard_map.129 = (bf16[31,48,512]{2,1,0:T(8,128)(2,1)}, f32[8,128]{1,0:T(8,128)S(1)}) custom-call(f32[4,1536,128]{2,1,0:T(8,128)S(1)} %get-tuple-element.33.pre1, f32[48,128]{1,0:T(8,128)S(1)} %get-tuple-element.34.count, bf16[80,512]{1,0:T(8,128)(2,1)S(1)} %shard_map.128.before.a), custom_call_target="tpu_custom_call" | custom-call | tf_op jit(solution)/shard_map/pallas_call | solution.py:26
  69.2 0.5 collective-permute-done.8.b
  70.0 5.2 %collective-permute-done.9.b = bf16[80,512]{1,0:T(8,128)(2,1)S(1)} collective-permute-done((bf16[80,512]{1,0:T(8,128)(2,1)S(1)}, bf16[80,512]{1,0:T(8,128)(2,1)S(1)}, u32[]{:S(2)}, u32[]{:S(2)}) %collective-permute-start.9) | collective-permute-done | bytes 81952 | tf_op jit(solution)/shard_map/ppermute | solution.py:61
  75.4 3.4 %collective-permute-start.11 = (bf16[80,512]{1,0:T(8,128)(2,1)S(1)}, bf16[80,512]{1,0:T(8,128)(2,1)S(1)}, u32[]{:S(2)}, u32[]{:S(2)}) collective-permute-start(bf16[80,512]{1,0:T(8,128)(2,1)S(1)} %shard_map.131.own), channel_id=1, source_target_pairs={{0,2},{1,3},{2,0},{3,1},{4,20},{5,21},{6,22},{7,23},{8,10},{9,11},... | collective-permute-start | bytes 245768 | tf_op jit(solution)/shard_map/ppermute | solution.py:61
  78.8 0.9 collective-permute-done.10.r1
  79.8 1.7 %collective-permute-done.11.r2 = bf16[80,512]{1,0:T(8,128)(2,1)S(1)} collective-permute-done((bf16[80,512]{1,0:T(8,128)(2,1)S(1)}, bf16[80,512]{1,0:T(8,128)(2,1)S(1)}, u32[]{:S(2)}, u32[]{:S(2)}) %collective-permute-start.11) | collective-permute-done | bytes 81952 | tf_op jit(solution)/shard_map/ppermute | solution.py:61
  81.5 0.6 collective-permute-done.12.r3
  82.3 3.4 %collective-permute-start.14 = (bf16[224,512]{1,0:T(8,128)(2,1)S(1)}, bf16[224,512]{1,0:T(8,128)(2,1)S(1)}, u32[]{:S(2)}, u32[]{:S(2)}) collective-permute-start(bf16[224,512]{1,0:T(8,128)(2,1)S(1)} %shard_map.132.own), channel_id=1, source_target_pairs={{0,16},{1,17},{2,18},{3,19},{4,6},{5,7},{6,4},{7,5},{8,24},{9,25},... | collective-permute-start | bytes 688136 | tf_op jit(solution)/shard_map/ppermute | solution.py:61
  85.6 0.5 collective-permute-start.15
  86.2 3.3 %collective-permute-done.13.r1 = bf16[224,512]{1,0:T(8,128)(2,1)S(1)} collective-permute-done((bf16[224,512]{1,0:T(8,128)(2,1)S(1)}, bf16[224,512]{1,0:T(8,128)(2,1)S(1)}, u32[]{:S(2)}, u32[]{:S(2)}) %collective-permute-start.13) | collective-permute-done | bytes 229408 | tf_op jit(solution)/shard_map/ppermute | solution.py:61
  89.5 3.8 %collective-permute-done.14.r2 = bf16[224,512]{1,0:T(8,128)(2,1)S(1)} collective-permute-done((bf16[224,512]{1,0:T(8,128)(2,1)S(1)}, bf16[224,512]{1,0:T(8,128)(2,1)S(1)}, u32[]{:S(2)}, u32[]{:S(2)}) %collective-permute-start.14) | collective-permute-done | bytes 229408 | tf_op jit(solution)/shard_map/ppermute | solution.py:61
  93.3 9.6 %collective-permute-start.16 = (bf16[800,512]{1,0:T(8,128)(2,1)S(1)}, bf16[800,512]{1,0:T(8,128)(2,1)S(1)}, u32[]{:S(2)}, u32[]{:S(2)}) collective-permute-start(bf16[800,512]{1,0:T(8,128)(2,1)S(1)} %shard_map.133.own), channel_id=1, source_target_pairs={{0,4},{1,5},{2,6},{3,7},{4,0},{5,1},{6,2},{7,3},{8,12},{9,13},{10,... | collective-permute-start | bytes 2457608 | tf_op jit(solution)/shard_map/ppermute | solution.py:61
  103.0 1.7 %shard_map.134.half = f32[1536,512]{1,0:T(8,128)} custom-call(s32[3]{0:T(128)S(1)} %pad_add_fusion.pos, bf16[800,512]{1,0:T(8,128)(2,1)S(1)} %shard_map.133.own), custom_call_target="tpu_custom_call" | custom-call | tf_op jit(solution)/shard_map/pallas_call | solution.py:198
  104.9 1.8 %shard_map.135 = (f32[1536,512]{1,0:T(8,128)}, f32[10,512]{1,0:T(8,128)}, f32[1,512]{1,0:T(1,128)}, f32[1,512]{1,0:T(1,128)}) custom-call(s32[3]{0:T(128)S(1)} %pad_add_fusion.pos, bf16[800,512]{1,0:T(8,128)(2,1)S(1)} %shard_map.133.own, bf16[800,512]{1,0:T(8,128)(2,1)S(1)} %collective-permute-done.16.got, ...), custom_call_target="tpu_custom_call", output_to_operand_aliasing={{0}: (3, {})} | custom-call | tf_op jit(solution)/shard_map/pallas_call | solution.py:201
  (32 shorter events, 2.0 us)
Async XLA Ops:
  2.4 23.7 %all-to-all-start = ((bf16[64,2,384]{2,1,0:T(2,128)(2,1)}), bf16[64,2,384]{2,1,0:T(2,128)(2,1)S(1)}, u32[]{:S(2)}, u32[]{:S(2)}) async-start(bf16[64,2,384]{2,1,0:T(2,128)(2,1)} %shard_map.119), calls=%async_computation | async-start | bytes 196608 | tf_op jit(solution)/shard_map/all_to_all | solution.py:538
  15.6 2.4 %copy-start.2 = (bf16[10,512]{1,0:T(8,128)(2,1)S(1)}, bf16[10,512]{1,0:T(8,128)(2,1)}, u32[]{:S(2)}) copy-start(bf16[10,512]{1,0:T(8,128)(2,1)} %conv0.1) | copy-start | bytes 30724
  15.6 10.5 %copy-start = (bf16[3,512,512]{2,1,0:T(8,128)(2,1)S(1)}, bf16[3,512,512]{2,1,0:T(8,128)(2,1)}, u32[]{:S(2)}) copy-start(bf16[3,512,512]{2,1,0:T(8,128)(2,1)} %weight.5) | copy-start | bytes 4718596
  15.6 10.5 %copy-start.1 = (f32[512]{0:T(512)S(1)}, f32[512]{0:T(512)}, u32[]{:S(2)}) copy-start(f32[512]{0:T(512)} %param.12) | copy-start | bytes 6148
  15.6 10.5 %copy-start.3 = (f32[512]{0:T(512)S(1)}, f32[512]{0:T(512)}, u32[]{:S(2)}) copy-start(f32[512]{0:T(512)} %param.13) | copy-start | bytes 6148
  42.2 2.4 %collective-permute-start = (bf16[768,512]{1,0:T(8,128)(2,1)S(1)}, bf16[768,512]{1,0:T(8,128)(2,1)S(1)}, u32[]{:S(2)}, u32[]{:S(2)}) collective-permute-start(bf16[768,512]{1,0:T(8,128)(2,1)S(1)} %get-tuple-element.39.before), channel_id=1, source_target_pairs={{0,4},{1,5},{2,6},{3,7},{4,0},{5,1},{6,2},{7,3},{8,12},{9,13},{10,... | collective-permute-start | bytes 2359304 | tf_op jit(solution)/shard_map/ppermute | solution.py:61
  45.4 9.1 %collective-permute-start.1 = (bf16[192,512]{1,0:T(8,128)(2,1)S(1)}, bf16[192,512]{1,0:T(8,128)(2,1)S(1)}, u32[]{:S(2)}, u32[]{:S(2)}) collective-permute-start(bf16[192,512]{1,0:T(8,128)(2,1)S(1)} %get-tuple-element.41), channel_id=1, source_target_pairs={{0,8},{1,9},{2,10},{3,11},{4,5},{5,6},{6,7},{7,4},{8,16},{9,17},{1... | collective-permute-start | bytes 589832 | tf_op jit(solution)/shard_map/ppermute | solution.py:61
  46.6 7.8 %collective-permute-start.2 = (bf16[192,512]{1,0:T(8,128)(2,1)S(1)}, bf16[192,512]{1,0:T(8,128)(2,1)S(1)}, u32[]{:S(2)}, u32[]{:S(2)}) collective-permute-start(bf16[192,512]{1,0:T(8,128)(2,1)S(1)} %get-tuple-element.42), channel_id=1, source_target_pairs={{0,16},{1,17},{2,18},{3,19},{4,6},{5,7},{6,4},{7,5},{8,24},{9,25},... | collective-permute-start | bytes 589832 | tf_op jit(solution)/shard_map/ppermute | solution.py:61
  49.1 5.3 %collective-permute-start.3 = (bf16[192,512]{1,0:T(8,128)(2,1)S(1)}, bf16[192,512]{1,0:T(8,128)(2,1)S(1)}, u32[]{:S(2)}, u32[]{:S(2)}) collective-permute-start(bf16[192,512]{1,0:T(8,128)(2,1)S(1)} %get-tuple-element.43), channel_id=1, source_target_pairs={{0,24},{1,25},{2,26},{3,27},{4,7},{5,4},{6,5},{7,6},{8,0},{9,1},{1... | collective-permute-start | bytes 589832 | tf_op jit(solution)/shard_map/ppermute | solution.py:61
  55.1 5.5 %collective-permute-start.4 = (bf16[48,512]{1,0:T(8,128)(2,1)S(1)}, bf16[48,512]{1,0:T(8,128)(2,1)S(1)}, u32[]{:S(2)}, u32[]{:S(2)}) collective-permute-start(bf16[48,512]{1,0:T(8,128)(2,1)S(1)} %get-tuple-element.52), channel_id=1, source_target_pairs={{0,1},{1,2},{2,3},{3,0},{4,12},{5,13},{6,14},{7,15},{8,9},{9,10},{... | collective-permute-start | bytes 147464 | tf_op jit(solution)/shard_map/ppermute | solution.py:61
  55.4 5.2 %collective-permute-start.5 = (bf16[48,512]{1,0:T(8,128)(2,1)S(1)}, bf16[48,512]{1,0:T(8,128)(2,1)S(1)}, u32[]{:S(2)}, u32[]{:S(2)}) collective-permute-start(bf16[48,512]{1,0:T(8,128)(2,1)S(1)} %get-tuple-element.53), channel_id=1, source_target_pairs={{0,2},{1,3},{2,0},{3,1},{4,20},{5,21},{6,22},{7,23},{8,10},{9,11},... | collective-permute-start | bytes 147464 | tf_op jit(solution)/shard_map/ppermute | solution.py:61
  56.9 3.8 %collective-permute-start.6 = (bf16[48,512]{1,0:T(8,128)(2,1)S(1)}, bf16[48,512]{1,0:T(8,128)(2,1)S(1)}, u32[]{:S(2)}, u32[]{:S(2)}) collective-permute-start(bf16[48,512]{1,0:T(8,128)(2,1)S(1)} %get-tuple-element.54), channel_id=1, source_target_pairs={{0,3},{1,0},{2,1},{3,2},{4,28},{5,29},{6,30},{7,31},{8,11},{9,8},{... | collective-permute-start | bytes 147464 | tf_op jit(solution)/shard_map/ppermute | solution.py:61
  60.7 3.5 %collective-permute-start.7 = (bf16[80,512]{1,0:T(8,128)(2,1)S(1)}, bf16[80,512]{1,0:T(8,128)(2,1)S(1)}, u32[]{:S(2)}, u32[]{:S(2)}) collective-permute-start(bf16[80,512]{1,0:T(8,128)(2,1)S(1)} %shard_map.127.a), channel_id=1, source_target_pairs={{0,32},{1,33},{2,34},{3,35},{4,36},{5,37},{6,38},{7,39},{8,40},{9,... | collective-permute-start | bytes 245768 | tf_op jit(solution)/shard_map/ppermute | solution.py:61
  64.3 5.4 %collective-permute-start.8 = (bf16[80,512]{1,0:T(8,128)(2,1)S(1)}, bf16[80,512]{1,0:T(8,128)(2,1)S(1)}, u32[]{:S(2)}, u32[]{:S(2)}) collective-permute-start(bf16[80,512]{1,0:T(8,128)(2,1)S(1)} %shard_map.128.before.a), channel_id=1, source_target_pairs={{0,96},{1,97},{2,98},{3,99},{4,100},{5,101},{6,102},{7,103},{8,104... | collective-permute-start | bytes 245768 | tf_op jit(solution)/shard_map/ppermute | solution.py:61
  69.7 5.4 %collective-permute-start.9 = (bf16[80,512]{1,0:T(8,128)(2,1)S(1)}, bf16[80,512]{1,0:T(8,128)(2,1)S(1)}, u32[]{:S(2)}, u32[]{:S(2)}) collective-permute-start(bf16[80,512]{1,0:T(8,128)(2,1)S(1)} %shard_map.130.a), channel_id=1, source_target_pairs={{0,224},{1,225},{2,226},{3,227},{4,228},{5,229},{6,230},{7,231},{8... | collective-permute-start | bytes 245768 | tf_op jit(solution)/shard_map/ppermute | solution.py:61
  75.2 4.6 %collective-permute-start.10 = (bf16[80,512]{1,0:T(8,128)(2,1)S(1)}, bf16[80,512]{1,0:T(8,128)(2,1)S(1)}, u32[]{:S(2)}, u32[]{:S(2)}) collective-permute-start(bf16[80,512]{1,0:T(8,128)(2,1)S(1)} %shard_map.131.own), channel_id=1, source_target_pairs={{0,1},{1,2},{2,3},{3,0},{4,12},{5,13},{6,14},{7,15},{8,9},{9,10},{... | collective-permute-start | bytes 245768 | tf_op jit(solution)/shard_map/ppermute | solution.py:61
  75.4 6.1 %collective-permute-start.11 = (bf16[80,512]{1,0:T(8,128)(2,1)S(1)}, bf16[80,512]{1,0:T(8,128)(2,1)S(1)}, u32[]{:S(2)}, u32[]{:S(2)}) collective-permute-start(bf16[80,512]{1,0:T(8,128)(2,1)S(1)} %shard_map.131.own), channel_id=1, source_target_pairs={{0,2},{1,3},{2,0},{3,1},{4,20},{5,21},{6,22},{7,23},{8,10},{9,11},... | collective-permute-start | bytes 245768 | tf_op jit(solution)/shard_map/ppermute | solution.py:61
  78.8 3.3 %collective-permute-start.12 = (bf16[80,512]{1,0:T(8,128)(2,1)S(1)}, bf16[80,512]{1,0:T(8,128)(2,1)S(1)}, u32[]{:S(2)}, u32[]{:S(2)}) collective-permute-start(bf16[80,512]{1,0:T(8,128)(2,1)S(1)} %shard_map.131.own), channel_id=1, source_target_pairs={{0,3},{1,0},{2,1},{3,2},{4,28},{5,29},{6,30},{7,31},{8,11},{9,8},{... | collective-permute-start | bytes 245768 | tf_op jit(solution)/shard_map/ppermute | solution.py:61
  82.1 7.3 %collective-permute-start.13 = (bf16[224,512]{1,0:T(8,128)(2,1)S(1)}, bf16[224,512]{1,0:T(8,128)(2,1)S(1)}, u32[]{:S(2)}, u32[]{:S(2)}) collective-permute-start(bf16[224,512]{1,0:T(8,128)(2,1)S(1)} %shard_map.132.own), channel_id=1, source_target_pairs={{0,8},{1,9},{2,10},{3,11},{4,5},{5,6},{6,7},{7,4},{8,16},{9,17},{1... | collective-permute-start | bytes 688136 | tf_op jit(solution)/shard_map/ppermute | solution.py:61
  82.3 11.0 %collective-permute-start.14 = (bf16[224,512]{1,0:T(8,128)(2,1)S(1)}, bf16[224,512]{1,0:T(8,128)(2,1)S(1)}, u32[]{:S(2)}, u32[]{:S(2)}) collective-permute-start(bf16[224,512]{1,0:T(8,128)(2,1)S(1)} %shard_map.132.own), channel_id=1, source_target_pairs={{0,16},{1,17},{2,18},{3,19},{4,6},{5,7},{6,4},{7,5},{8,24},{9,25},... | collective-permute-start | bytes 688136 | tf_op jit(solution)/shard_map/ppermute | solution.py:61
  85.6 7.6 %collective-permute-start.15 = (bf16[224,512]{1,0:T(8,128)(2,1)S(1)}, bf16[224,512]{1,0:T(8,128)(2,1)S(1)}, u32[]{:S(2)}, u32[]{:S(2)}) collective-permute-start(bf16[224,512]{1,0:T(8,128)(2,1)S(1)} %shard_map.132.own), channel_id=1, source_target_pairs={{0,24},{1,25},{2,26},{3,27},{4,7},{5,4},{6,5},{7,6},{8,0},{9,1},{1... | collective-permute-start | bytes 688136 | tf_op jit(solution)/shard_map/ppermute | solution.py:61
  93.3 11.6 %collective-permute-start.16 = (bf16[800,512]{1,0:T(8,128)(2,1)S(1)}, bf16[800,512]{1,0:T(8,128)(2,1)S(1)}, u32[]{:S(2)}, u32[]{:S(2)}) collective-permute-start(bf16[800,512]{1,0:T(8,128)(2,1)S(1)} %shard_map.133.own), channel_id=1, source_target_pairs={{0,4},{1,5},{2,6},{3,7},{4,0},{5,1},{6,2},{7,3},{8,12},{9,13},{10,... | collective-permute-start | bytes 2457608 | tf_op jit(solution)/shard_map/ppermute | solution.py:61

commit v7 on v6

--- a/solution.py
+++ b/solution.py
@@ -397,7 +397,7 @@
         lax.fori_loop(0, BLOCK, second, 0, unroll=BLOCK)
         return carry
 
-    lax.fori_loop(0, spans // BLOCK, block, 0)
+    lax.fori_loop(0, spans // BLOCK, block, 0, unroll=True)
     half_of(1 - pos[2], he, ho, g, gs, other)
 
 
@@ -470,7 +470,7 @@
         lax.fori_loop(0, BACK, back, 0, unroll=BACK)
         return carry
 
-    lax.fori_loop(0, blocks, block, 0)
+    lax.fori_loop(0, blocks, block, 0, unroll=True)
     part = x[pl.ds(first * (32 * BACK), blocks * (32 * BACK)), :]
     small[...] = start[...] + dot_t(part, dxe[...])[0:16] + dot_t(part, dxo[...])[16:32]
     small[pl.ds(10, 2), :] += sums[pl.ds(0, 2), :]

time: 107 us -> 107 us (level)
  transfers between devices with their start and end apart: 18 -> 18, of which waited for: 11 -> 12; matrix products, arithmetic and copies ran while one was open for 2% -> 2% of each run, Pallas kernels for 13% -> 13%
where the time goes in v7:
time: 107 us; the launch traced here: 106 us
  starting transfers between devices  41.1 us (38%)
  Pallas kernels  34.8 us (33%)
  waiting for transfers between devices  27.1 us (25%)
  local copies, waits for them, and re-layouts  2.37 us (2%)
    pallas_call x15, Pallas kernels, call(): pl.pallas_call(kernel, out_shape=shapes, in_specs=specs, out_specs=[VM] *...  31.2 us
    ppermute x17, starting transfers between devices, send(): return lax.ppermute(value, BOTH, perm)  27.9 us
    ppermute x17, waiting for transfers between devices, send(): return lax.ppermute(value, BOTH, perm)  19 us
    all_to_all x1, starting transfers between devices, body(): lax.all_to_all(packed, 'dp', split_axis=0, concat_axis=0, tiled=True)  13.2 us
    all_to_all x1, waiting for transfers between devices, body(): lax.all_to_all(packed, 'dp', split_axis=0, concat_axis=0, tiled=True)  8.02 us
    unnamed x9, local copies, waits for them, and re-layouts  2.37 us
  transfers between devices with their start and end apart: 18, of which 12 were waited for; matrix products, arithmetic and copies ran while one was open for 2% of the time, Pallas kernels for 13%

profile of v7, /device:TPU:1, one launch (start us, length us, event | category | flops | bytes accessed | tf_op | source)
XLA Modules:
  0.0 106.4 jit_solution(3578736411110846214)
XLA Ops:
  0.6 1.8 %shard_map.119 = bf16[64,2,384]{2,1,0:T(2,128)(2,1)} custom-call(bf16[48,320]{1,0:T(8,128)(2,1)} %bitcast.21, s32[1,48]{1,0:T(1,128)} %length_in.1, s32[1,48]{1,0:T(1,128)} %target_in.1), custom_call_target="tpu_custom_call" | custom-call | tf_op jit(solution)/shard_map/pallas_call | solution.py:26
  2.4 13.2 %all-to-all-start = ((bf16[64,2,384]{2,1,0:T(2,128)(2,1)}), bf16[64,2,384]{2,1,0:T(2,128)(2,1)S(1)}, u32[]{:S(2)}, u32[]{:S(2)}) async-start(bf16[64,2,384]{2,1,0:T(2,128)(2,1)} %shard_map.119), calls=%async_computation | async-start | bytes 196608 | tf_op jit(solution)/shard_map/all_to_all | solution.py:538
  15.7 2.3 %copy.16 = bf16[1,48,31,512]{3,2,1,0:T(8,128)(2,1)S(1)} copy(bf16[1,48,31,512]{3,1,2,0:T(8,128)(2,1)} %param.15) | data formatting | bytes 3047424 | tf_op args[7]
  18.1 8.0 %all-to-all-done.arrived = bf16[64,2,384]{2,1,0:T(2,128)(2,1)S(1)} async-done(((bf16[64,2,384]{2,1,0:T(2,128)(2,1)}), bf16[64,2,384]{2,1,0:T(2,128)(2,1)S(1)}, u32[]{:S(2)}, u32[]{:S(2)}) %all-to-all-start) | async-done | bytes 98336 | tf_op jit(solution)/shard_map/all_to_all | solution.py:538
  26.2 15.8 %shard_map.121 = (f32[4,1536,128]{2,1,0:T(8,128)S(1)}, f32[48,128]{1,0:T(8,128)S(1)}, bf16[1536,512]{1,0:T(8,128)(2,1)S(1)}, bf16[1536,512]{1,0:T(8,128)(2,1)S(1...) custom-call(s32[3]{0:T(128)S(1)} %pad_add_fusion.pos, ...), custom_call_target="tpu_custom_call" | custom-call | tf_op jit(solution)/shard_map/pallas_call | solution.py:26
  42.0 0.5 collective-permute-start
  42.5 2.1 %shard_map.122.own = f32[768,512]{1,0:T(8,128)S(1)} custom-call(s32[3]{0:T(128)S(1)} %pad_add_fusion.pos, bf16[1536,512]{1,0:T(8,128)(2,1)S(1)} %get-tuple-element.35.he, bf16[1536,512]{1,0:T(8,128)(2,1)S(1)} %get-tuple-element.36.ho, bf16[1536,512]{1,0:T(8,128)(2,1)S(1)} %get-tuple-element.37.g, bf16[1536,512]{1,0:T(8,128)(2,1)S(1)} %get-tuple-element.38.gs, ...), custom_call_target="tpu_custom_call" | custom-call | tf_op jit(solution)/shard_map/pallas_call | solution.py:26
  44.6 0.7 shard_map.123
  45.3 1.3 %collective-permute-start.1 = (bf16[192,512]{1,0:T(8,128)(2,1)S(1)}, bf16[192,512]{1,0:T(8,128)(2,1)S(1)}, u32[]{:S(2)}, u32[]{:S(2)}) collective-permute-start(bf16[192,512]{1,0:T(8,128)(2,1)S(1)} %get-tuple-element.41), channel_id=1, source_target_pairs={{0,8},{1,9},{2,10},{3,11},{4,5},{5,6},{6,7},{7,4},{8,16},{9,17},{1... | collective-permute-start | bytes 589832 | tf_op jit(solution)/shard_map/ppermute | solution.py:61
  46.6 2.4 %collective-permute-start.2 = (bf16[192,512]{1,0:T(8,128)(2,1)S(1)}, bf16[192,512]{1,0:T(8,128)(2,1)S(1)}, u32[]{:S(2)}, u32[]{:S(2)}) collective-permute-start(bf16[192,512]{1,0:T(8,128)(2,1)S(1)} %get-tuple-element.42), channel_id=1, source_target_pairs={{0,16},{1,17},{2,18},{3,19},{4,6},{5,7},{6,4},{7,5},{8,24},{9,25},... | collective-permute-start | bytes 589832 | tf_op jit(solution)/shard_map/ppermute | solution.py:61
  49.1 1.1 %collective-permute-start.3 = (bf16[192,512]{1,0:T(8,128)(2,1)S(1)}, bf16[192,512]{1,0:T(8,128)(2,1)S(1)}, u32[]{:S(2)}, u32[]{:S(2)}) collective-permute-start(bf16[192,512]{1,0:T(8,128)(2,1)S(1)} %get-tuple-element.43), channel_id=1, source_target_pairs={{0,24},{1,25},{2,26},{3,27},{4,7},{5,4},{6,5},{7,6},{8,0},{9,1},{1... | collective-permute-start | bytes 589832 | tf_op jit(solution)/shard_map/ppermute | solution.py:61
  50.2 3.7 %shard_map.124.before.start = f32[16,512]{1,0:T(8,128)S(1)} custom-call(bf16[1536,512]{1,0:T(8,128)(2,1)S(1)} %get-tuple-element.37.g, bf16[1536,512]{1,0:T(8,128)(2,1)S(1)} %get-tuple-element.38.gs, bf16[1536,512]{1,0:T(8,128)(2,1)S(1)} %get-tuple-element.44.se, bf16[1536,512]{1,0:T(8,128)(2,1)S(1)} %get-tuple-element.45.so, ...), custom_call_target="tpu_custom_call" | custom-call | tf_op jit(solution)/shard_map/pallas_call | solution.py:26
  54.2 0.6 shard_map.125
  55.2 1.7 %collective-permute-start.5 = (bf16[48,512]{1,0:T(8,128)(2,1)S(1)}, bf16[48,512]{1,0:T(8,128)(2,1)S(1)}, u32[]{:S(2)}, u32[]{:S(2)}) collective-permute-start(bf16[48,512]{1,0:T(8,128)(2,1)S(1)} %get-tuple-element.53), channel_id=1, source_target_pairs={{0,2},{1,3},{2,0},{3,1},{4,20},{5,21},{6,22},{7,23},{8,10},{9,11},... | collective-permute-start | bytes 147464 | tf_op jit(solution)/shard_map/ppermute | solution.py:61
  56.9 1.3 %collective-permute-start.6 = (bf16[48,512]{1,0:T(8,128)(2,1)S(1)}, bf16[48,512]{1,0:T(8,128)(2,1)S(1)}, u32[]{:S(2)}, u32[]{:S(2)}) collective-permute-start(bf16[48,512]{1,0:T(8,128)(2,1)S(1)} %get-tuple-element.54), channel_id=1, source_target_pairs={{0,3},{1,0},{2,1},{3,2},{4,28},{5,29},{6,30},{7,31},{8,11},{9,8},{... | collective-permute-start | bytes 147464 | tf_op jit(solution)/shard_map/ppermute | solution.py:61
  58.1 2.2 %shard_map.126.small = f32[16,512]{1,0:T(8,128)S(1)} custom-call(bf16[1536,512]{1,0:T(8,128)(2,1)S(1)} %get-tuple-element.37.g, bf16[1536,512]{1,0:T(8,128)(2,1)S(1)} %get-tuple-element.38.gs, bf16[1536,512]{1,0:T(8,128)(2,1)S(1)} %get-tuple-element.44.se, bf16[1536,512]{1,0:T(8,128)(2,1)S(1)} %get-tuple-element.45.so, ...), custom_call_target="tpu_custom_call" | custom-call | tf_op jit(solution)/shard_map/pallas_call | solution.py:26
  60.9 3.1 %collective-permute-done.7.b = bf16[80,512]{1,0:T(8,128)(2,1)S(1)} collective-permute-done((bf16[80,512]{1,0:T(8,128)(2,1)S(1)}, bf16[80,512]{1,0:T(8,128)(2,1)S(1)}, u32[]{:S(2)}, u32[]{:S(2)}) %collective-permute-start.7) | collective-permute-done | bytes 81952 | tf_op jit(solution)/shard_map/ppermute | solution.py:61
  64.0 1.1 %collective-permute-start.8 = (bf16[80,512]{1,0:T(8,128)(2,1)S(1)}, bf16[80,512]{1,0:T(8,128)(2,1)S(1)}, u32[]{:S(2)}, u32[]{:S(2)}) collective-permute-start(bf16[80,512]{1,0:T(8,128)(2,1)S(1)} %shard_map.128.before.a), channel_id=1, source_target_pairs={{0,96},{1,97},{2,98},{3,99},{4,100},{5,101},{6,102},{7,103},{8,104... | collective-permute-start | bytes 245768 | tf_op jit(solution)/shard_map/ppermute | solution.py:61
  65.2 4.0 %shard_map.129 = (bf16[31,48,512]{2,1,0:T(8,128)(2,1)}, f32[8,128]{1,0:T(8,128)S(1)}) custom-call(f32[4,1536,128]{2,1,0:T(8,128)S(1)} %get-tuple-element.33.pre1, f32[48,128]{1,0:T(8,128)S(1)} %get-tuple-element.34.count, bf16[80,512]{1,0:T(8,128)(2,1)S(1)} %shard_map.128.before.a), custom_call_target="tpu_custom_call" | custom-call | tf_op jit(solution)/shard_map/pallas_call | solution.py:26
  70.0 5.0 %collective-permute-done.9.b = bf16[80,512]{1,0:T(8,128)(2,1)S(1)} collective-permute-done((bf16[80,512]{1,0:T(8,128)(2,1)S(1)}, bf16[80,512]{1,0:T(8,128)(2,1)S(1)}, u32[]{:S(2)}, u32[]{:S(2)}) %collective-permute-start.9) | collective-permute-done | bytes 81952 | tf_op jit(solution)/shard_map/ppermute | solution.py:61
  75.4 3.2 %collective-permute-start.11 = (bf16[80,512]{1,0:T(8,128)(2,1)S(1)}, bf16[80,512]{1,0:T(8,128)(2,1)S(1)}, u32[]{:S(2)}, u32[]{:S(2)}) collective-permute-start(bf16[80,512]{1,0:T(8,128)(2,1)S(1)} %shard_map.131.own), channel_id=1, source_target_pairs={{0,2},{1,3},{2,0},{3,1},{4,20},{5,21},{6,22},{7,23},{8,10},{9,11},... | collective-permute-start | bytes 245768 | tf_op jit(solution)/shard_map/ppermute | solution.py:61
  78.7 0.8 collective-permute-done.10.r1
  79.6 1.7 %collective-permute-done.11.r2 = bf16[80,512]{1,0:T(8,128)(2,1)S(1)} collective-permute-done((bf16[80,512]{1,0:T(8,128)(2,1)S(1)}, bf16[80,512]{1,0:T(8,128)(2,1)S(1)}, u32[]{:S(2)}, u32[]{:S(2)}) %collective-permute-start.11) | collective-permute-done | bytes 81952 | tf_op jit(solution)/shard_map/ppermute | solution.py:61
  81.2 0.6 collective-permute-done.12.r3
  81.9 1.1 %collective-permute-start.13 = (bf16[224,512]{1,0:T(8,128)(2,1)S(1)}, bf16[224,512]{1,0:T(8,128)(2,1)S(1)}, u32[]{:S(2)}, u32[]{:S(2)}) collective-permute-start(bf16[224,512]{1,0:T(8,128)(2,1)S(1)} %shard_map.132.own), channel_id=1, source_target_pairs={{0,8},{1,9},{2,10},{3,11},{4,5},{5,6},{6,7},{7,4},{8,16},{9,17},{1... | collective-permute-start | bytes 688136 | tf_op jit(solution)/shard_map/ppermute | solution.py:61
  83.0 2.7 %collective-permute-start.14 = (bf16[224,512]{1,0:T(8,128)(2,1)S(1)}, bf16[224,512]{1,0:T(8,128)(2,1)S(1)}, u32[]{:S(2)}, u32[]{:S(2)}) collective-permute-start(bf16[224,512]{1,0:T(8,128)(2,1)S(1)} %shard_map.132.own), channel_id=1, source_target_pairs={{0,16},{1,17},{2,18},{3,19},{4,6},{5,7},{6,4},{7,5},{8,24},{9,25},... | collective-permute-start | bytes 688136 | tf_op jit(solution)/shard_map/ppermute | solution.py:61
  85.7 0.7 collective-permute-start.15
  86.4 3.0 %collective-permute-done.13.r1 = bf16[224,512]{1,0:T(8,128)(2,1)S(1)} collective-permute-done((bf16[224,512]{1,0:T(8,128)(2,1)S(1)}, bf16[224,512]{1,0:T(8,128)(2,1)S(1)}, u32[]{:S(2)}, u32[]{:S(2)}) %collective-permute-start.13) | collective-permute-done | bytes 229408 | tf_op jit(solution)/shard_map/ppermute | solution.py:61
  89.3 4.0 %collective-permute-done.14.r2 = bf16[224,512]{1,0:T(8,128)(2,1)S(1)} collective-permute-done((bf16[224,512]{1,0:T(8,128)(2,1)S(1)}, bf16[224,512]{1,0:T(8,128)(2,1)S(1)}, u32[]{:S(2)}, u32[]{:S(2)}) %collective-permute-start.14) | collective-permute-done | bytes 229408 | tf_op jit(solution)/shard_map/ppermute | solution.py:61
  93.4 9.1 %collective-permute-start.16 = (bf16[800,512]{1,0:T(8,128)(2,1)S(1)}, bf16[800,512]{1,0:T(8,128)(2,1)S(1)}, u32[]{:S(2)}, u32[]{:S(2)}) collective-permute-start(bf16[800,512]{1,0:T(8,128)(2,1)S(1)} %shard_map.133.own), channel_id=1, source_target_pairs={{0,4},{1,5},{2,6},{3,7},{4,0},{5,1},{6,2},{7,3},{8,12},{9,13},{10,... | collective-permute-start | bytes 2457608 | tf_op jit(solution)/shard_map/ppermute | solution.py:61
  102.5 1.7 %shard_map.134.half = f32[1536,512]{1,0:T(8,128)} custom-call(s32[3]{0:T(128)S(1)} %pad_add_fusion.pos, bf16[800,512]{1,0:T(8,128)(2,1)S(1)} %shard_map.133.own), custom_call_target="tpu_custom_call" | custom-call | tf_op jit(solution)/shard_map/pallas_call | solution.py:198
  104.4 1.8 %shard_map.135 = (f32[1536,512]{1,0:T(8,128)}, f32[10,512]{1,0:T(8,128)}, f32[1,512]{1,0:T(1,128)}, f32[1,512]{1,0:T(1,128)}) custom-call(s32[3]{0:T(128)S(1)} %pad_add_fusion.pos, bf16[800,512]{1,0:T(8,128)(2,1)S(1)} %shard_map.133.own, bf16[800,512]{1,0:T(8,128)(2,1)S(1)} %collective-permute-done.16.got, ...), custom_call_target="tpu_custom_call", output_to_operand_aliasing={{0}: (3, {})} | custom-call | tf_op jit(solution)/shard_map/pallas_call | solution.py:201
  (32 shorter events, 3.0 us)
Async XLA Ops:
  2.4 23.7 %all-to-all-start = ((bf16[64,2,384]{2,1,0:T(2,128)(2,1)}), bf16[64,2,384]{2,1,0:T(2,128)(2,1)S(1)}, u32[]{:S(2)}, u32[]{:S(2)}) async-start(bf16[64,2,384]{2,1,0:T(2,128)(2,1)} %shard_map.119), calls=%async_computation | async-start | bytes 196608 | tf_op jit(solution)/shard_map/all_to_all | solution.py:538
  15.6 2.4 %copy-start.2 = (bf16[10,512]{1,0:T(8,128)(2,1)S(1)}, bf16[10,512]{1,0:T(8,128)(2,1)}, u32[]{:S(2)}) copy-start(bf16[10,512]{1,0:T(8,128)(2,1)} %conv0.1) | copy-start | bytes 30724
  15.6 10.5 %copy-start = (bf16[3,512,512]{2,1,0:T(8,128)(2,1)S(1)}, bf16[3,512,512]{2,1,0:T(8,128)(2,1)}, u32[]{:S(2)}) copy-start(bf16[3,512,512]{2,1,0:T(8,128)(2,1)} %weight.5) | copy-start | bytes 4718596
  15.6 10.5 %copy-start.1 = (f32[512]{0:T(512)S(1)}, f32[512]{0:T(512)}, u32[]{:S(2)}) copy-start(f32[512]{0:T(512)} %param.12) | copy-start | bytes 6148
  15.6 10.5 %copy-start.3 = (f32[512]{0:T(512)S(1)}, f32[512]{0:T(512)}, u32[]{:S(2)}) copy-start(f32[512]{0:T(512)} %param.13) | copy-start | bytes 6148
  42.0 2.6 %collective-permute-start = (bf16[768,512]{1,0:T(8,128)(2,1)S(1)}, bf16[768,512]{1,0:T(8,128)(2,1)S(1)}, u32[]{:S(2)}, u32[]{:S(2)}) collective-permute-start(bf16[768,512]{1,0:T(8,128)(2,1)S(1)} %get-tuple-element.39.before), channel_id=1, source_target_pairs={{0,4},{1,5},{2,6},{3,7},{4,0},{5,1},{6,2},{7,3},{8,12},{9,13},{10,... | collective-permute-start | bytes 2359304 | tf_op jit(solution)/shard_map/ppermute | solution.py:61
  45.3 8.6 %collective-permute-start.1 = (bf16[192,512]{1,0:T(8,128)(2,1)S(1)}, bf16[192,512]{1,0:T(8,128)(2,1)S(1)}, u32[]{:S(2)}, u32[]{:S(2)}) collective-permute-start(bf16[192,512]{1,0:T(8,128)(2,1)S(1)} %get-tuple-element.41), channel_id=1, source_target_pairs={{0,8},{1,9},{2,10},{3,11},{4,5},{5,6},{6,7},{7,4},{8,16},{9,17},{1... | collective-permute-start | bytes 589832 | tf_op jit(solution)/shard_map/ppermute | solution.py:61
  46.6 7.6 %collective-permute-start.2 = (bf16[192,512]{1,0:T(8,128)(2,1)S(1)}, bf16[192,512]{1,0:T(8,128)(2,1)S(1)}, u32[]{:S(2)}, u32[]{:S(2)}) collective-permute-start(bf16[192,512]{1,0:T(8,128)(2,1)S(1)} %get-tuple-element.42), channel_id=1, source_target_pairs={{0,16},{1,17},{2,18},{3,19},{4,6},{5,7},{6,4},{7,5},{8,24},{9,25},... | collective-permute-start | bytes 589832 | tf_op jit(solution)/shard_map/ppermute | solution.py:61
  49.1 5.2 %collective-permute-start.3 = (bf16[192,512]{1,0:T(8,128)(2,1)S(1)}, bf16[192,512]{1,0:T(8,128)(2,1)S(1)}, u32[]{:S(2)}, u32[]{:S(2)}) collective-permute-start(bf16[192,512]{1,0:T(8,128)(2,1)S(1)} %get-tuple-element.43), channel_id=1, source_target_pairs={{0,24},{1,25},{2,26},{3,27},{4,7},{5,4},{6,5},{7,6},{8,0},{9,1},{1... | collective-permute-start | bytes 589832 | tf_op jit(solution)/shard_map/ppermute | solution.py:61
  54.9 5.5 %collective-permute-start.4 = (bf16[48,512]{1,0:T(8,128)(2,1)S(1)}, bf16[48,512]{1,0:T(8,128)(2,1)S(1)}, u32[]{:S(2)}, u32[]{:S(2)}) collective-permute-start(bf16[48,512]{1,0:T(8,128)(2,1)S(1)} %get-tuple-element.52), channel_id=1, source_target_pairs={{0,1},{1,2},{2,3},{3,0},{4,12},{5,13},{6,14},{7,15},{8,9},{9,10},{... | collective-permute-start | bytes 147464 | tf_op jit(solution)/shard_map/ppermute | solution.py:61
  55.2 5.2 %collective-permute-start.5 = (bf16[48,512]{1,0:T(8,128)(2,1)S(1)}, bf16[48,512]{1,0:T(8,128)(2,1)S(1)}, u32[]{:S(2)}, u32[]{:S(2)}) collective-permute-start(bf16[48,512]{1,0:T(8,128)(2,1)S(1)} %get-tuple-element.53), channel_id=1, source_target_pairs={{0,2},{1,3},{2,0},{3,1},{4,20},{5,21},{6,22},{7,23},{8,10},{9,11},... | collective-permute-start | bytes 147464 | tf_op jit(solution)/shard_map/ppermute | solution.py:61
  56.9 3.6 %collective-permute-start.6 = (bf16[48,512]{1,0:T(8,128)(2,1)S(1)}, bf16[48,512]{1,0:T(8,128)(2,1)S(1)}, u32[]{:S(2)}, u32[]{:S(2)}) collective-permute-start(bf16[48,512]{1,0:T(8,128)(2,1)S(1)} %get-tuple-element.54), channel_id=1, source_target_pairs={{0,3},{1,0},{2,1},{3,2},{4,28},{5,29},{6,30},{7,31},{8,11},{9,8},{... | collective-permute-start | bytes 147464 | tf_op jit(solution)/shard_map/ppermute | solution.py:61
  60.5 3.5 %collective-permute-start.7 = (bf16[80,512]{1,0:T(8,128)(2,1)S(1)}, bf16[80,512]{1,0:T(8,128)(2,1)S(1)}, u32[]{:S(2)}, u32[]{:S(2)}) collective-permute-start(bf16[80,512]{1,0:T(8,128)(2,1)S(1)} %shard_map.127.a), channel_id=1, source_target_pairs={{0,32},{1,33},{2,34},{3,35},{4,36},{5,37},{6,38},{7,39},{8,40},{9,... | collective-permute-start | bytes 245768 | tf_op jit(solution)/shard_map/ppermute | solution.py:61
  64.0 5.4 %collective-permute-start.8 = (bf16[80,512]{1,0:T(8,128)(2,1)S(1)}, bf16[80,512]{1,0:T(8,128)(2,1)S(1)}, u32[]{:S(2)}, u32[]{:S(2)}) collective-permute-start(bf16[80,512]{1,0:T(8,128)(2,1)S(1)} %shard_map.128.before.a), channel_id=1, source_target_pairs={{0,96},{1,97},{2,98},{3,99},{4,100},{5,101},{6,102},{7,103},{8,104... | collective-permute-start | bytes 245768 | tf_op jit(solution)/shard_map/ppermute | solution.py:61
  69.5 5.5 %collective-permute-start.9 = (bf16[80,512]{1,0:T(8,128)(2,1)S(1)}, bf16[80,512]{1,0:T(8,128)(2,1)S(1)}, u32[]{:S(2)}, u32[]{:S(2)}) collective-permute-start(bf16[80,512]{1,0:T(8,128)(2,1)S(1)} %shard_map.130.a), channel_id=1, source_target_pairs={{0,224},{1,225},{2,226},{3,227},{4,228},{5,229},{6,230},{7,231},{8... | collective-permute-start | bytes 245768 | tf_op jit(solution)/shard_map/ppermute | solution.py:61
  75.0 4.6 %collective-permute-start.10 = (bf16[80,512]{1,0:T(8,128)(2,1)S(1)}, bf16[80,512]{1,0:T(8,128)(2,1)S(1)}, u32[]{:S(2)}, u32[]{:S(2)}) collective-permute-start(bf16[80,512]{1,0:T(8,128)(2,1)S(1)} %shard_map.131.own), channel_id=1, source_target_pairs={{0,1},{1,2},{2,3},{3,0},{4,12},{5,13},{6,14},{7,15},{8,9},{9,10},{... | collective-permute-start | bytes 245768 | tf_op jit(solution)/shard_map/ppermute | solution.py:61
  75.4 5.9 %collective-permute-start.11 = (bf16[80,512]{1,0:T(8,128)(2,1)S(1)}, bf16[80,512]{1,0:T(8,128)(2,1)S(1)}, u32[]{:S(2)}, u32[]{:S(2)}) collective-permute-start(bf16[80,512]{1,0:T(8,128)(2,1)S(1)} %shard_map.131.own), channel_id=1, source_target_pairs={{0,2},{1,3},{2,0},{3,1},{4,20},{5,21},{6,22},{7,23},{8,10},{9,11},... | collective-permute-start | bytes 245768 | tf_op jit(solution)/shard_map/ppermute | solution.py:61
  78.5 3.3 %collective-permute-start.12 = (bf16[80,512]{1,0:T(8,128)(2,1)S(1)}, bf16[80,512]{1,0:T(8,128)(2,1)S(1)}, u32[]{:S(2)}, u32[]{:S(2)}) collective-permute-start(bf16[80,512]{1,0:T(8,128)(2,1)S(1)} %shard_map.131.own), channel_id=1, source_target_pairs={{0,3},{1,0},{2,1},{3,2},{4,28},{5,29},{6,30},{7,31},{8,11},{9,8},{... | collective-permute-start | bytes 245768 | tf_op jit(solution)/shard_map/ppermute | solution.py:61
  81.9 7.5 %collective-permute-start.13 = (bf16[224,512]{1,0:T(8,128)(2,1)S(1)}, bf16[224,512]{1,0:T(8,128)(2,1)S(1)}, u32[]{:S(2)}, u32[]{:S(2)}) collective-permute-start(bf16[224,512]{1,0:T(8,128)(2,1)S(1)} %shard_map.132.own), channel_id=1, source_target_pairs={{0,8},{1,9},{2,10},{3,11},{4,5},{5,6},{6,7},{7,4},{8,16},{9,17},{1... | collective-permute-start | bytes 688136 | tf_op jit(solution)/shard_map/ppermute | solution.py:61
  83.0 10.3 %collective-permute-start.14 = (bf16[224,512]{1,0:T(8,128)(2,1)S(1)}, bf16[224,512]{1,0:T(8,128)(2,1)S(1)}, u32[]{:S(2)}, u32[]{:S(2)}) collective-permute-start(bf16[224,512]{1,0:T(8,128)(2,1)S(1)} %shard_map.132.own), channel_id=1, source_target_pairs={{0,16},{1,17},{2,18},{3,19},{4,6},{5,7},{6,4},{7,5},{8,24},{9,25},... | collective-permute-start | bytes 688136 | tf_op jit(solution)/shard_map/ppermute | solution.py:61
  85.7 7.6 %collective-permute-start.15 = (bf16[224,512]{1,0:T(8,128)(2,1)S(1)}, bf16[224,512]{1,0:T(8,128)(2,1)S(1)}, u32[]{:S(2)}, u32[]{:S(2)}) collective-permute-start(bf16[224,512]{1,0:T(8,128)(2,1)S(1)} %shard_map.132.own), channel_id=1, source_target_pairs={{0,24},{1,25},{2,26},{3,27},{4,7},{5,4},{6,5},{7,6},{8,0},{9,1},{1... | collective-permute-start | bytes 688136 | tf_op jit(solution)/shard_map/ppermute | solution.py:61
  93.4 11.0 %collective-permute-start.16 = (bf16[800,512]{1,0:T(8,128)(2,1)S(1)}, bf16[800,512]{1,0:T(8,128)(2,1)S(1)}, u32[]{:S(2)}, u32[]{:S(2)}) collective-permute-start(bf16[800,512]{1,0:T(8,128)(2,1)S(1)} %shard_map.133.own), channel_id=1, source_target_pairs={{0,4},{1,5},{2,6},{3,7},{4,0},{5,1},{6,2},{7,3},{8,12},{9,13},{10,... | collective-permute-start | bytes 2457608 | tf_op jit(solution)/shard_map/ppermute | solution.py:61
